TPU v7x, 512 devices: a whole 4x8x8 slice. The times are simulated.
512 devices in a mesh: row: 32 (over x_hi, z, core), col: 16 (over y, x_lo).
Axes of the slice: x: 4 (x_hi: 2, x_lo: 2; x = x_hi * 2 + x_lo), y: 8, z: 8, core: 2. Of those that a mesh axis runs over, the one named last changes fastest.
Arguments:
- ancestor_inverse: float32 [12288, 12288], P('row', 'col'), may hold values from -6 to 6
- panel: float32 [4096, 512], P('col', 'row'), may hold values from -0.09375 to 0.09375
- unit_inverse: float32 [512, 512], P('row'), may hold values from -1 to 1, as said below
- pivot_inverse: float32 [512, 512], P('row', 'col'), may hold values from -6 to 6
- panel_blocks: int32 [32], replicated, may hold values from 0 to 95, as said below
Outputs:
- inverse_row: float32 [512, 12288], P('col', 'row')
- diagonal_block: float32 [512, 512], P('row', 'col')
Inputs may be any that keep to these rules, and one draw needn't show every extreme that they name: `panel_blocks`: Distinct, in no particular order. Among the window blocks c * 6 to c * 6 + 5 of any process column c at most 3 are listed, and exactly 3 for some columns. `unit_inverse`: unit lower triangular: ones on the diagonal, zeros above it.
All inputs are finite; a program needn't handle non-finite values.
Results may differ from a plain program's by a relative error of at most 0.00011.
Values sent between devices are 32-bit elements; how exact they have to be, the bound alone decides.
No kernel may reach another device: no remote copies, remote signals or barrier semaphores. Data moves between devices by JAX's collectives and lax.ppermute only.
A program may use at most 64 MiB of HBM per device.

v0:
```python
import jax
import jax.numpy as jnp
from jax import lax
from jax.sharding import Mesh
from jax.sharding import PartitionSpec as P

BLK = 128
COL = ("col_0", "col_1")


def in_blocks(value, dim, length):
    before, after = (value.shape[:dim], value.shape[dim + 1 :])
    return jnp.moveaxis(value.reshape(*before, length, -1, *after), dim, 0)


def summed_on_arrival(value, axis, dim):
    tiles = in_blocks(value, dim, lax.axis_size(axis))
    arrived = lax.all_to_all(tiles, axis, split_axis=0, concat_axis=0, tiled=True)
    return arrived.sum(axis=0)


def joined_along(tiles, dim):
    tiles = jnp.moveaxis(tiles, 0, dim)
    dims = tiles.shape
    return tiles.reshape(*dims[:dim], dims[dim] * dims[dim + 1], *dims[dim + 2 :])


def copy_for_each(value, axis):
    length = lax.axis_size(axis)
    return lax.all_to_all(
        jnp.broadcast_to(value[None], (length, *value.shape)), axis, 0, 0, tiled=True
    )


def gather_directly(value, axis, dim):
    return joined_along(copy_for_each(value, axis), dim)


def from_root(value, axes, root):
    value = jnp.where(lax.axis_index(axes) == root, value, jnp.zeros_like(value))
    for axis in axes:
        value = lax.psum(value, axis)
    return value


def place_blocks(stacked, block_ids, wanted):
    onehot = (block_ids[None, :] == wanted[:, None]).astype(jnp.float32)
    placed = jnp.einsum("kp,pbw->kbw", onehot, stacked, precision=lax.Precision.HIGHEST)
    return placed.reshape(wanted.shape[0] * stacked.shape[1], stacked.shape[2])


def on_device(ancestor_inverse, panel, unit_inverse, pivot_inverse, panel_blocks):
    highest = lax.Precision.HIGHEST
    row_index = lax.axis_index("row")
    col_index = lax.axis_index(COL)
    rows_here, cols_here = ancestor_inverse.shape
    width = unit_inverse.shape[1]
    block_total = panel_blocks.shape[0]
    range_blocks = cols_here // BLK
    row_blocks = rows_here // BLK
    first_block = col_index * range_blocks
    partial_value = jnp.dot(
        panel, unit_inverse, precision=highest, preferred_element_type=jnp.float32
    )
    normal = summed_on_arrival(partial_value, "row", 1)
    all_rows = gather_directly(normal, COL, 0)
    stacked = all_rows.reshape(block_total, BLK, all_rows.shape[1])
    slot_count = range_blocks // 2
    in_range = ((panel_blocks >= first_block) & (panel_blocks < first_block + range_blocks)).astype(
        jnp.int32
    )
    rank_of = jnp.cumsum(in_range) - 1
    slot_ids = jnp.arange(slot_count, dtype=jnp.int32)
    selected = (in_range[None, :] == 1) & (rank_of[None, :] == slot_ids[:, None])
    chosen = jnp.einsum("sp,pbw->sbw", selected.astype(jnp.float32), stacked, precision=highest)
    chosen = chosen.reshape(slot_count * BLK, stacked.shape[2])
    chosen_ids = jnp.sum(jnp.where(selected, panel_blocks[None, :], 0), axis=1)
    slot_live = jnp.sum(selected.astype(jnp.int32), axis=1) > 0
    window_ids = jnp.where(slot_live, chosen_ids, -1)
    local_ids = jnp.clip(chosen_ids - first_block, 0, range_blocks - 1)
    window = gather_directly(chosen, "row", 1)
    columns = jnp.take(ancestor_inverse.reshape(rows_here, range_blocks, BLK), local_ids, axis=1)
    columns = columns.reshape(rows_here, slot_count * BLK)
    inverse_tile = summed_on_arrival(
        -lax.dot_general(
            window,
            columns,
            (((0,), (1,)), ((), ())),
            precision=highest,
            preferred_element_type=jnp.float32,
        ),
        COL,
        0,
    )
    row_ids = row_index * row_blocks + jnp.arange(row_blocks, dtype=jnp.int32)
    window_stack = window.reshape(window.shape[0] // BLK, BLK, width)
    candidate = place_blocks(window_stack, window_ids, row_ids)
    owner = row_index * rows_here // cols_here
    own_window = from_root(candidate, COL, owner)
    crossed = -lax.dot_general(
        own_window,
        inverse_tile,
        (((0,), (1,)), ((), ())),
        precision=highest,
        preferred_element_type=jnp.float32,
    )
    diagonal_block = pivot_inverse + summed_on_arrival(crossed, "row", 0)
    return (inverse_tile, diagonal_block)


def solution(mesh):
    finer = Mesh(mesh.devices.reshape(mesh.shape["row"], 8, 2), ("row", "col_0", "col_1"))
    return jax.shard_map(
        on_device,
        mesh=finer,
        in_specs=(P("row", COL), P(COL, "row"), P("row", None), P("row", COL), P()),
        out_specs=(P(COL, "row"), P("row", COL)),
        check_vma=False,
    )
```

profile of v0, /device:TPU:1, one launch (start us, length us, event | category | flops | bytes accessed | tf_op | source)
XLA Modules:
  0.0 258.6 jit_solution(13069033184812062134)
XLA Ops:
  7.2 0.7 copy-done
  7.9 1.3 fusion.9
  9.3 32.3 %all_to_all.25 = f32[32,256,16]{1,2,0:T(8,128)S(1)} all-to-all(f32[32,256,16]{1,2,0:T(8,128)S(1)} %bitcast.47), channel_id=1, replica_groups=mesh['row'=32,'col_0'=8,'col_1'=2] {'row'}, dimensions={0} | all-to-all | bytes 1048576 | tf_op jit(solution)/shard_map/all_to_all | solution.py:18
  41.6 0.7 broadcast_in_dim.48
  42.4 7.0 %all-to-all-start.1 = ((f32[16,256,16]{1,2,0:T(8,128)}), f32[16,256,16]{1,2,0:T(8,128)S(1)}, u32[]{:S(2)}, u32[]{:S(2)}) async-start(f32[16,256,16]{1,2,0:T(8,128)} %broadcast_in_dim.48), calls=%async_computation.1 | async-start | bytes 524288 | tf_op jit(solution)/shard_map/all_to_all | solution.py:30
  49.5 0.1 add_reduce_fusion
  49.6 9.3 %all-to-all-done.1 = f32[16,256,16]{1,2,0:T(8,128)S(1)} async-done(((f32[16,256,16]{1,2,0:T(8,128)}), f32[16,256,16]{1,2,0:T(8,128)S(1)}, u32[]{:S(2)}, u32[]{:S(2)}) %all-to-all-start.1) | async-done | bytes 262176 | tf_op jit(solution)/shard_map/all_to_all | solution.py:30
  58.9 0.2 copy.19
  59.1 0.2 fusion.2
  59.4 0.9 broadcast_in_dim.50
  60.3 8.1 %all-to-all-start.2 = ((f32[32,384,16]{1,2,0:T(8,128)}), f32[32,384,16]{1,2,0:T(8,128)S(1)}, u32[]{:S(2)}, u32[]{:S(2)}) async-start(f32[32,384,16]{1,2,0:T(8,128)} %broadcast_in_dim.50), calls=%async_computation.2 | async-start | bytes 1572864 | tf_op jit(solution)/shard_map/all_to_all | solution.py:30
  68.5 0.4 copy.20
  68.9 0.4 copy.21
  69.2 0.2 convert_reduce_fusion
  69.4 0.6 gather_fusion
  70.1 0.2 copy.22
  70.4 20.8 %all-to-all-done.2 = f32[32,384,16]{1,2,0:T(8,128)S(1)} async-done(((f32[32,384,16]{1,2,0:T(8,128)}), f32[32,384,16]{1,2,0:T(8,128)S(1)}, u32[]{:S(2)}, u32[]{:S(2)}) %all-to-all-start.2) | async-done | bytes 786464 | tf_op jit(solution)/shard_map/all_to_all | solution.py:30
  91.2 0.3 reshape_reshape.7
  91.5 0.6 copy.23
  92.1 1.1 convolution_select_fusion
  93.2 1.1 copy.24
  94.4 2.5 convolution_negate_fusion
  96.9 3.6 %all-to-all-start.3 = ((f32[16,32,384]{2,1,0:T(8,128)}), f32[16,32,384]{2,1,0:T(8,128)S(1)}, u32[]{:S(2)}, u32[]{:S(2)}) async-start(f32[16,32,384]{2,1,0:T(8,128)} %bitcast.11), calls=%async_computation.3 | async-start | bytes 1572864 | tf_op jit(solution)/shard_map/all_to_all | solution.py:18
  100.6 69.3 %all-reduce.3.cloned.1.call-done = f32[384,512]{1,0:T(8,128)} async-done(((f32[384,512]{1,0:T(8,128)}), f32[384,512]{1,0:T(8,128)}) %all-reduce.3.cloned.1.call-update) | async-done | bytes 786448 | tf_op jit(solution)/shard_map/psum | solution.py:42
  170.1 57.9 %all-reduce.5.cloned.1.call-done = f32[384,512]{1,0:T(8,128)} async-done(((f32[384,512]{1,0:T(8,128)}), f32[384,512]{1,0:T(8,128)}) %all-reduce.5.cloned.1.call-update) | async-done | bytes 786448 | tf_op jit(solution)/shard_map/psum | solution.py:42
  227.9 1.7 convolution_negate_fusion.1
  229.6 0.1 copy.25
  229.8 0.2 reshape.144
  230.0 19.7 %all_to_all.26 = f32[32,1,512]{2,1,0:T(1,128)S(1)} all-to-all(f32[32,1,512]{2,1,0:T(1,128)S(1)} %reshape.144), channel_id=1, replica_groups=mesh['row'=32,'col_0'=8,'col_1'=2] {'row'}, dimensions={0} | all-to-all | bytes 131072 | tf_op jit(solution)/shard_map/all_to_all | solution.py:18
  249.7 0.5 broadcast.139
  250.2 0.8 reduce.2
  251.2 0.6 add.52
  (28 shorter events, 0.7 us)
Async XLA Ops:
  7.2 0.8 copy-start
  9.3 40.1 %copy-start.4 = (s32[32]{0:T(128)S(1)}, s32[32]{0:T(128)}, u32[]{:S(2)}) copy-start(s32[32]{0:T(128)} %param.9) | copy-start | bytes 388
  42.4 16.6 %all-to-all-start.1 = ((f32[16,256,16]{1,2,0:T(8,128)}), f32[16,256,16]{1,2,0:T(8,128)S(1)}, u32[]{:S(2)}, u32[]{:S(2)}) async-start(f32[16,256,16]{1,2,0:T(8,128)} %broadcast_in_dim.48), calls=%async_computation.1 | async-start | bytes 524288 | tf_op jit(solution)/shard_map/all_to_all | solution.py:30
  59.3 9.2 %copy-start.1 = (f32[384,768]{1,0:T(8,128)S(1)}, f32[384,768]{1,0:T(8,128)}, u32[]{:S(2)}) copy-start(f32[384,768]{1,0:T(8,128)} %param.5) | copy-start | bytes 3538948
  60.3 30.9 %all-to-all-start.2 = ((f32[32,384,16]{1,2,0:T(8,128)}), f32[32,384,16]{1,2,0:T(8,128)S(1)}, u32[]{:S(2)}, u32[]{:S(2)}) async-start(f32[32,384,16]{1,2,0:T(8,128)} %broadcast_in_dim.50), calls=%async_computation.2 | async-start | bytes 1572864 | tf_op jit(solution)/shard_map/all_to_all | solution.py:30
  68.4 101.5 %all-reduce.3.cloned.1.call-start = ((), (), s32[]{:S(2)}) async-start(), calls=%async_computation.5 | async-start | bytes 1572864 | tf_op jit(solution)/shard_map/psum | solution.py:42
  96.9 73.0 %all-to-all-start.3 = ((f32[16,32,384]{2,1,0:T(8,128)}), f32[16,32,384]{2,1,0:T(8,128)S(1)}, u32[]{:S(2)}, u32[]{:S(2)}) async-start(f32[16,32,384]{2,1,0:T(8,128)} %bitcast.11), calls=%async_computation.3 | async-start | bytes 1572864 | tf_op jit(solution)/shard_map/all_to_all | solution.py:18
  100.5 127.4 %all-reduce.5.cloned.1.call-start = ((), (), s32[]{:S(2)}) async-start(), calls=%async_computation.6 | async-start | bytes 1572864 | tf_op jit(solution)/shard_map/psum | solution.py:42
  170.0 81.1 %copy-start.2 = (f32[32,384]{1,0:T(8,128)}, f32[32,384]{1,0:T(8,128)S(1)}, u32[]{:S(2)}) copy-start(f32[32,384]{1,0:T(8,128)S(1)} %reduce_sum.47) | copy-start | bytes 147460
  170.0 81.1 %copy-start.3 = (f32[16,32]{1,0:T(8,128)S(1)}, f32[16,32]{1,0:T(8,128)}, u32[]{:S(2)}) copy-start(f32[16,32]{1,0:T(8,128)} %param.8) | copy-start | bytes 6148
Sparse Core Ops, SparseCore 0:
  94.5 75.3 all-reduce.2
  173.1 54.8 all-reduce.4
where the time goes:
time: 259 us
  waiting for transfers between devices  157 us (61%)
  blocking collectives  52 us (20%)
  starting transfers between devices  18.8 us (7%)
  between operations  14.4 us (6%)
  local copies, waits for them, and re-layouts  7.21 us (3%)
  matrix products  6.89 us (3%)
    psum x2, waiting for transfers between devices, from_root(): value = lax.psum(value, axis)  127 us
    all_to_all x2, blocking collectives, summed_on_arrival(): lax.all_to_all(tiles, axis, split_axis=0, concat_axis=0, tiled=True)  52 us
    all_to_all x2, waiting for transfers between devices, copy_for_each(): lax.all_to_all(jnp.broadcast_to(value[None], (length, *value.shape)), axi...  30.1 us
    all_to_all x2, starting transfers between devices, copy_for_each(): lax.all_to_all(jnp.broadcast_to(value[None], (length, *value.shape)), axi...  15.1 us
  transfers between devices with their start and end apart: 5, of which 4 were waited for; matrix products, arithmetic and copies ran while one was open for 2% of the time, Pallas kernels for 0%

commit v1 on v0

v1 whole, which is shorter than its diff:
```python
import jax
import jax.numpy as jnp
from jax import lax
from jax.experimental import pallas as pl
from jax.experimental.pallas import tpu as pltpu
from jax.sharding import Mesh
from jax.sharding import PartitionSpec as P

BLK = 128
SLOTS = 3
ROW = ("x_hi", "z", "core")
CHIPS = ("x_hi", "z")
COL = ("y", "x_lo")
PARAMS = pltpu.CompilerParams(vmem_limit_bytes=32 * 1024 * 1024)
VMEM = pl.BlockSpec(memory_space=pltpu.VMEM)
SMEM = pl.BlockSpec(memory_space=pltpu.SMEM)


def split(value):
    high = value.astype(jnp.bfloat16)
    low = (value - high.astype(jnp.float32)).astype(jnp.bfloat16)
    return high, low


def product(left, right, dims):
    left_high, left_low = split(left)
    right_high, right_low = split(right)

    def dot(a, b):
        return lax.dot_general(a, b, (dims, ((), ())), preferred_element_type=jnp.float32)

    return dot(left_high, right_high) + (dot(left_high, right_low) + dot(left_low, right_high))


def pack_kernel(slots, place, stored, unit, out):
    here = place[0]
    chips, rows, _ = out.shape
    span = SLOTS * BLK

    def block(slot):
        index = slots[slot]
        safe = jnp.maximum(index, 0)
        lane = pl.multiple_of(lax.rem(safe, 2) * BLK, BLK)
        value = stored[lax.div(safe, 2), :, pl.ds(lane, BLK)]
        return jnp.where(index >= 0, value, 0.0)

    mine = jnp.concatenate([block(here * SLOTS + s) for s in range(SLOTS)], axis=1)
    unit_rows = unit[...]
    for chip in range(chips):
        out[chip, :, 0:span] = mine
        out[chip, :, 2 * span :] = unit_rows
        for s in range(SLOTS):
            out[chip, :, span + s * BLK : span + (s + 1) * BLK] = block(chip * SLOTS + s)


def normal_kernel(gathered, col_out, row_out):
    span = SLOTS * BLK
    unit = gathered[:, 2 * span :].T
    col_out[...] = product(unit, gathered[:, :span], ((1,), (0,)))
    row_out[...] = product(unit, gathered[:, span : 2 * span], ((1,), (0,)))


def window_kernel(blocks, own, other, inverse, out):
    total = None
    for s in range(SLOTS):
        lane = pl.multiple_of(jnp.maximum(blocks[s], 0) * BLK, BLK)
        at = slice(s * BLK, (s + 1) * BLK)
        value = product(own[:, at] + other[:, at], inverse[:, pl.ds(lane, BLK)], ((1,), (1,)))
        total = value if total is None else total + value
    out[...] = total


def diagonal_kernel(blocks, own, other, arrived, tile_out, out):
    tile = arrived[0]
    for c in range(1, arrived.shape[0]):
        tile = tile + arrived[c]
    tile_out[...] = -tile
    total = None
    for s in range(SLOTS):
        place = blocks[s]
        lane = pl.multiple_of(jnp.maximum(place, 0) * BLK, BLK)
        at = slice(s * BLK, (s + 1) * BLK)
        listed = jnp.where(place >= 0, tile_out[:, pl.ds(lane, BLK)], 0.0)
        value = product(own[:, at] + other[:, at], listed, ((1,), (1,)))
        total = value if total is None else total + value
    rows = out.shape[0]
    width = total.shape[1]
    total = total.reshape(rows, 2, 8, width)
    pad = jnp.zeros((rows, 8, 128 - 2 * width), jnp.float32)
    out[...] = jnp.concatenate([total[:, 0], total[:, 1], pad], axis=2)


def final_kernel(arrived, pivot, out):
    total = arrived[0]
    for r in range(1, arrived.shape[0]):
        total = total + arrived[r]
    width = out.shape[1]
    out[0:8, :] = pivot[0:8, :] - total[:, 0:width]
    out[8:16, :] = pivot[8:16, :] - total[:, width : 2 * width]


def call(kernel, shapes, specs, flops=0, moved=0):
    return pl.pallas_call(
        kernel,
        out_shape=shapes,
        in_specs=specs,
        out_specs=jax.tree.map(lambda _: VMEM, shapes),
        compiler_params=PARAMS,
        cost_estimate=pl.CostEstimate(flops=flops, bytes_accessed=moved, transcendentals=0),
    )


def f32(*shape):
    return jax.ShapeDtypeStruct(shape, jnp.float32)


def on_device(ancestor_inverse, panel, unit_inverse, pivot_inverse, panel_blocks):
    chip = lax.axis_index(CHIPS)
    core = lax.axis_index("core")
    col = lax.axis_index(COL)
    cols = lax.axis_size(COL)
    chips = lax.axis_size(CHIPS)
    rows_here, cols_here = ancestor_inverse.shape
    unit_rows, width = unit_inverse.shape
    range_blocks = cols_here // BLK
    row_blocks = rows_here // BLK
    span = SLOTS * BLK
    total_blocks = panel_blocks.shape[0]

    owner = panel_blocks // range_blocks
    order = jnp.arange(total_blocks, dtype=jnp.int32)
    same = (owner[:, None] == owner[None, :]) & (order[None, :] < order[:, None])
    slot_of = owner * SLOTS + jnp.sum(same.astype(jnp.int32), axis=1)
    all_slots = jnp.arange(cols * SLOTS, dtype=jnp.int32)
    hit = (slot_of[None, :] == all_slots[:, None]).astype(jnp.int32)
    slots = jnp.sum(hit * (order + 1)[None, :], axis=1) - 1
    window = jnp.sum(hit * (panel_blocks + 1)[None, :], axis=1) - 1
    col_blocks = lax.dynamic_slice(window, (col * SLOTS,), (SLOTS,)) - col * range_blocks
    own_blocks = lax.dynamic_slice(window, (chip * SLOTS,), (SLOTS,))
    own_blocks = own_blocks - chip * range_blocks - core * row_blocks
    own_blocks = jnp.where(own_blocks < row_blocks, own_blocks, -1)
    place = col.reshape(1).astype(jnp.int32)

    stored = jnp.broadcast_to(panel.T[None], (cols, panel.shape[1], panel.shape[0]))
    stored = lax.all_to_all(stored, COL, 0, 0, tiled=True)
    payload = call(
        pack_kernel,
        f32(chips, unit_rows, 2 * span + width),
        [SMEM, SMEM, VMEM, VMEM],
        moved=2 * 1024 * 1024,
    )(slots, place, stored, unit_inverse)
    gathered = lax.all_to_all(payload, CHIPS, 0, 0, tiled=True)
    gathered = gathered.reshape(chips * unit_rows, 2 * span + width)
    col_own, row_own = call(
        normal_kernel,
        (f32(width, span), f32(width, span)),
        [VMEM],
        flops=2 * 3 * chips * unit_rows * width * 2 * span,
        moved=3 * 1024 * 1024,
    )(gathered)
    swap = [(0, 1), (1, 0)]
    col_other = lax.ppermute(col_own, "core", swap)
    row_other = lax.ppermute(row_own, "core", swap)
    partial_tile = call(
        window_kernel,
        f32(width, rows_here),
        [SMEM, VMEM, VMEM, VMEM],
        flops=2 * 3 * width * span * rows_here,
        moved=3 * 1024 * 1024,
    )(col_blocks, col_own, col_other, ancestor_inverse)
    partial_tile = partial_tile.reshape(cols, width // cols, rows_here)
    arrived = lax.all_to_all(partial_tile, COL, 0, 0, tiled=True)
    row_count = lax.axis_size(ROW)
    inverse_tile, share = call(
        diagonal_kernel,
        (f32(width // cols, rows_here), f32(row_count, 8, 128)),
        [SMEM, VMEM, VMEM, VMEM],
        flops=2 * 3 * width * span * (width // cols),
        moved=3 * 1024 * 1024,
    )(own_blocks, row_own, row_other, arrived)
    shares = lax.all_to_all(share, ROW, 0, 0, tiled=True)
    diagonal_block = call(
        final_kernel, f32(*pivot_inverse.shape), [VMEM, VMEM], moved=1024 * 128
    )(shares, pivot_inverse)
    return (inverse_tile, diagonal_block)


def solution(mesh):
    finer = Mesh(
        mesh.devices.reshape(2, mesh.shape["row"] // 4, 2, mesh.shape["col"] // 2, 2),
        (*ROW, *COL),
    )
    return jax.shard_map(
        on_device,
        mesh=finer,
        in_specs=(P(ROW, COL), P(COL, ROW), P(ROW, None), P(ROW, COL), P()),
        out_specs=(P(COL, ROW), P(ROW, COL)),
        check_vma=False,
    )
```

time: 259 us -> 123 us (0.47)
  waiting for transfers between devices: 157 us -> 29.1 us
  between operations: 14.4 us -> 0.72 us
  blocking collectives: 52 us -> 60.9 us
  matrix products: 6.89 us -> 0 us
  Pallas kernels: 0 us -> 6.45 us
  local copies, waits for them, and re-layouts: 7.21 us -> 2.21 us
  starting transfers between devices: 18.8 us -> 21.8 us
    psum x2 -> x0, waiting for transfers between devices: 127 us -> none  [from_root(): value = lax.psum(value, axis)]
    ppermute x0 -> x2, starting transfers between devices: none -> 9.55 us  [the longest x1 7.27 us: on_device(): col_other = lax.ppermute(col_own, 'core', swap)]
    all_to_all x2, blocking collectives: 52 us -> 60.9 us  [the longest x1 42.6 us: on_device(): gathered = lax.all_to_all(payload, CHIPS, 0, 0, tiled=True)]
    dot_general x5 -> x0, matrix products: 6.89 us -> none  [the longest x1 2.51 us: on_device(): lax.dot_general(window, columns, (((0,), (1,)), ((), ())), precision=high...]
    pallas_call x0 -> x5, Pallas kernels: none -> 6.45 us  [the longest x1 2.54 us: on_device(): call(window_kernel, f32(width, rows_here), [SMEM, VMEM, VMEM, VMEM], flop...]
    all_to_all x3 -> x2, starting transfers between devices: 18.7 us -> 12.3 us  [the longest x1 8.68 us: on_device(): stored = lax.all_to_all(stored, COL, 0, 0, tiled=True)]
    all_to_all x3 -> x2, waiting for transfers between devices: 30.1 us -> 25.4 us  [the longest x1 16.6 us: on_device(): arrived = lax.all_to_all(partial_tile, COL, 0, 0, tiled=True)]
    ppermute x0 -> x2, waiting for transfers between devices: none -> 3.68 us  [the longest x1 1.89 us: on_device(): row_other = lax.ppermute(row_own, 'core', swap)]
  transfers between devices with their start and end apart: 5 -> 4, of which waited for: 4 -> 4; matrix products, arithmetic and copies ran while one was open for 2% -> 1% of each run, Pallas kernels for 0% -> 0%
where the time goes in v1:
time: 123 us; the launch traced here: 122 us
  blocking collectives  60.9 us (50%)
  waiting for transfers between devices  29.1 us (24%)
  starting transfers between devices  21.8 us (18%)
  Pallas kernels  6.45 us (5%)
  local copies, waits for them, and re-layouts  2.21 us (2%)
    all_to_all x1, blocking collectives, on_device(): gathered = lax.all_to_all(payload, CHIPS, 0, 0, tiled=True)  42.6 us
    all_to_all x1, blocking collectives, on_device(): shares = lax.all_to_all(share, ROW, 0, 0, tiled=True)  18.4 us
    all_to_all x1, waiting for transfers between devices, on_device(): arrived = lax.all_to_all(partial_tile, COL, 0, 0, tiled=True)  16.6 us
    all_to_all x1, waiting for transfers between devices, on_device(): stored = lax.all_to_all(stored, COL, 0, 0, tiled=True)  8.76 us
    all_to_all x1, starting transfers between devices, on_device(): stored = lax.all_to_all(stored, COL, 0, 0, tiled=True)  8.68 us
    ppermute x1, starting transfers between devices, on_device(): col_other = lax.ppermute(col_own, 'core', swap)  7.27 us
    all_to_all x1, starting transfers between devices, on_device(): arrived = lax.all_to_all(partial_tile, COL, 0, 0, tiled=True)  3.61 us
    pallas_call x1, Pallas kernels, on_device(): call(window_kernel, f32(width, rows_here), [SMEM, VMEM, VMEM, VMEM], flop...  2.54 us
  transfers between devices with their start and end apart: 4, of which 4 were waited for; matrix products, arithmetic and copies ran while one was open for 1% of the time, Pallas kernels for 0%

profile of v1, /device:TPU:1, one launch (start us, length us, event | category | flops | bytes accessed | tf_op | source)
XLA Modules:
  0.0 122.3 jit_solution(15814602732243516645)
XLA Ops:
  0.6 1.4 %broadcast_in_dim.6 = f32[16,16,256]{2,1,0:T(8,128)} broadcast(f32[16,256]{1,0:T(8,128)} %bitcast.5), dimensions={1,2} | broadcast | bytes 278528 | tf_op jit(solution)/shard_map/broadcast_in_dim | solution.py:144
  2.1 8.7 %all-to-all-start = ((f32[16,16,256]{2,1,0:T(8,128)}), f32[16,16,256]{2,1,0:T(8,128)S(1)}, u32[]{:S(2)}, u32[]{:S(2)}) async-start(f32[16,16,256]{2,1,0:T(8,128)} %broadcast_in_dim.6), calls=%async_computation | async-start | bytes 524288 | tf_op jit(solution)/shard_map/all_to_all | solution.py:145
  10.8 0.7 broadcast_add_fusion.2
  11.4 0.2 convert_reduce_fusion
  11.6 0.1 select_reduce_fusion
  11.7 8.8 %all-to-all-done.stored = f32[16,16,256]{2,1,0:T(8,128)S(1)} async-done(((f32[16,16,256]{2,1,0:T(8,128)}), f32[16,16,256]{2,1,0:T(8,128)S(1)}, u32[]{:S(2)}, u32[]{:S(2)}) %all-to-all-start) | async-done | bytes 262176 | tf_op jit(solution)/shard_map/all_to_all | solution.py:145
  20.5 0.0 copy-start.1
  20.5 0.8 copy-done.1
  21.3 0.8 shard_map.68
  22.1 42.6 %all_to_all.20 = f32[16,16,1280]{2,1,0:T(8,128)S(1)} all-to-all(f32[16,16,1280]{2,1,0:T(8,128)S(1)} %shard_map.68), channel_id=1, replica_groups=mesh['x_hi'=2,'z'=8,'core'=2,'y'=8,'x_lo'=2] {'x_hi','z'}, dimensions={0} | all-to-all | bytes 2621440 | tf_op jit(solution)/shard_map/all_to_all | solution.py:152
  64.6 0.0 copy-start
  64.6 1.0 shard_map.69
  65.7 7.3 %collective-permute-start.1 = (f32[512,384]{1,0:T(8,128)S(1)}, f32[512,384]{1,0:T(8,128)S(1)}, u32[]{:S(2)}, u32[]{:S(2)}) collective-permute-start(f32[512,384]{1,0:T(8,128)S(1)} %get-tuple-element.7.own), channel_id=1, source_target_pairs={{0,16},{16,0},{1,17},{17,1},{2,18},{18,2},{3,19},{19,3},{4,20},{20... | collective-permute-start | bytes 2359304 | tf_op jit(solution)/shard_map/ppermute | solution.py:162
  73.0 0.1 dynamic-slice_subtract_fusion
  73.0 1.8 %collective-permute-done.1.other = f32[512,384]{1,0:T(8,128)S(1)} collective-permute-done((f32[512,384]{1,0:T(8,128)S(1)}, f32[512,384]{1,0:T(8,128)S(1)}, u32[]{:S(2)}, u32[]{:S(2)}) %collective-permute-start.1) | collective-permute-done | bytes 786464 | tf_op jit(solution)/shard_map/ppermute | solution.py:162
  74.8 0.0 copy-done
  74.8 2.5 %shard_map.70 = f32[512,384]{1,0:T(8,128)} custom-call(s32[3]{0:T(128)S(1)} %get-tuple-element.12.blocks, f32[512,384]{1,0:T(8,128)S(1)} %get-tuple-element.7.own, f32[512,384]{1,0:T(8,128)S(1)} %collective-permute-done.1.other, f32[384,768]{1,0:T(8,128)S(1)} %copy-done), custom_call_target="tpu_custom_call" | custom-call | flops 452984832 | bytes 3145728 | tf_op jit(solution)/shard_map/pallas_call | solution.py:164
  77.4 3.6 %all-to-all-start.2 = ((f32[16,32,384]{2,1,0:T(8,128)}), f32[16,32,384]{2,1,0:T(8,128)S(1)}, u32[]{:S(2)}, u32[]{:S(2)}) async-start(f32[16,32,384]{2,1,0:T(8,128)} %bitcast.3), calls=%async_computation.2 | async-start | bytes 1572864 | tf_op jit(solution)/shard_map/all_to_all | solution.py:172
  81.0 2.3 %collective-permute-start = (f32[512,384]{1,0:T(8,128)S(1)}, f32[512,384]{1,0:T(8,128)S(1)}, u32[]{:S(2)}, u32[]{:S(2)}) collective-permute-start(f32[512,384]{1,0:T(8,128)S(1)} %get-tuple-element.6.own), channel_id=1, source_target_pairs={{0,16},{16,0},{1,17},{17,1},{2,18},{18,2},{3,19},{19,3},{4,20},{20... | collective-permute-start | bytes 2359304 | tf_op jit(solution)/shard_map/ppermute | solution.py:163
  83.3 1.9 %collective-permute-done.other = f32[512,384]{1,0:T(8,128)S(1)} collective-permute-done((f32[512,384]{1,0:T(8,128)S(1)}, f32[512,384]{1,0:T(8,128)S(1)}, u32[]{:S(2)}, u32[]{:S(2)}) %collective-permute-start) | collective-permute-done | bytes 786464 | tf_op jit(solution)/shard_map/ppermute | solution.py:163
  85.2 16.6 %all-to-all-done.2.arrived = f32[16,32,384]{2,1,0:T(8,128)S(1)} async-done(((f32[16,32,384]{2,1,0:T(8,128)}), f32[16,32,384]{2,1,0:T(8,128)S(1)}, u32[]{:S(2)}, u32[]{:S(2)}) %all-to-all-start.2) | async-done | bytes 786464 | tf_op jit(solution)/shard_map/all_to_all | solution.py:172
  101.8 0.0 copy-start.2
  101.8 1.4 %shard_map.71 = (f32[32,384]{1,0:T(8,128)}, f32[32,8,128]{2,1,0:T(8,128)S(1)}) custom-call(s32[3]{0:T(128)S(1)} %get-tuple-element.13.blocks, f32[512,384]{1,0:T(8,128)S(1)} %get-tuple-element.6.own, f32[512,384]{1,0:T(8,128)S(1)} %collective-permute-done.other, f32[16,32,384]{2,1,0:T(8,128)S(1)} %all-to-all-done.2.arrived), custom_call_target="tpu_custom_call" | custom-call | flops 37748736 | bytes 3145728 | tf_op jit(solution)/shard_map/pallas_call | solution.py:174
  103.2 18.4 %all_to_all.21.arrived = f32[32,8,128]{2,1,0:T(8,128)S(1)} all-to-all(f32[32,8,128]{2,1,0:T(8,128)S(1)} %get-tuple-element.9), channel_id=1, replica_groups=mesh['x_hi'=2,'z'=8,'core'=2,'y'=8,'x_lo'=2] {'x_hi','z','core'}, dimensions={0} | all-to-all | bytes 262144 | tf_op jit(solution)/shard_map/all_to_all | solution.py:181
  121.6 0.0 copy-done.2
  121.6 0.7 shard_map.72
  (3 shorter events, 0.0 us)
Async XLA Ops:
  2.1 18.4 %all-to-all-start = ((f32[16,16,256]{2,1,0:T(8,128)}), f32[16,16,256]{2,1,0:T(8,128)S(1)}, u32[]{:S(2)}, u32[]{:S(2)}) async-start(f32[16,16,256]{2,1,0:T(8,128)} %broadcast_in_dim.6), calls=%async_computation | async-start | bytes 524288 | tf_op jit(solution)/shard_map/all_to_all | solution.py:145
  20.5 0.8 copy-start.1
  64.6 10.2 %copy-start = (f32[384,768]{1,0:T(8,128)S(1)}, f32[384,768]{1,0:T(8,128)}, u32[]{:S(2)}) copy-start(f32[384,768]{1,0:T(8,128)} %inverse.1) | copy-start | bytes 3538948
  65.7 9.2 %collective-permute-start.1 = (f32[512,384]{1,0:T(8,128)S(1)}, f32[512,384]{1,0:T(8,128)S(1)}, u32[]{:S(2)}, u32[]{:S(2)}) collective-permute-start(f32[512,384]{1,0:T(8,128)S(1)} %get-tuple-element.7.own), channel_id=1, source_target_pairs={{0,16},{16,0},{1,17},{17,1},{2,18},{18,2},{3,19},{19,3},{4,20},{20... | collective-permute-start | bytes 2359304 | tf_op jit(solution)/shard_map/ppermute | solution.py:162
  77.4 24.4 %all-to-all-start.2 = ((f32[16,32,384]{2,1,0:T(8,128)}), f32[16,32,384]{2,1,0:T(8,128)S(1)}, u32[]{:S(2)}, u32[]{:S(2)}) async-start(f32[16,32,384]{2,1,0:T(8,128)} %bitcast.3), calls=%async_computation.2 | async-start | bytes 1572864 | tf_op jit(solution)/shard_map/all_to_all | solution.py:172
  81.0 4.2 %collective-permute-start = (f32[512,384]{1,0:T(8,128)S(1)}, f32[512,384]{1,0:T(8,128)S(1)}, u32[]{:S(2)}, u32[]{:S(2)}) collective-permute-start(f32[512,384]{1,0:T(8,128)S(1)} %get-tuple-element.6.own), channel_id=1, source_target_pairs={{0,16},{16,0},{1,17},{17,1},{2,18},{18,2},{3,19},{19,3},{4,20},{20... | collective-permute-start | bytes 2359304 | tf_op jit(solution)/shard_map/ppermute | solution.py:163
  101.8 19.8 %copy-start.2 = (f32[16,32]{1,0:T(8,128)S(1)}, f32[16,32]{1,0:T(8,128)}, u32[]{:S(2)}) copy-start(f32[16,32]{1,0:T(8,128)} %pivot.1) | copy-start | bytes 6148

commit v2 on v1

--- a/solution.py
+++ b/solution.py
@@ -22,52 +22,81 @@
     return high, low
 
 
-def product(left, right, dims):
-    left_high, left_low = split(left)
-    right_high, right_low = split(right)
-
-    def dot(a, b):
-        return lax.dot_general(a, b, (dims, ((), ())), preferred_element_type=jnp.float32)
-
-    return dot(left_high, right_high) + (dot(left_high, right_low) + dot(left_low, right_high))
-
-
-def pack_kernel(slots, place, stored, unit, out):
-    here = place[0]
-    chips, rows, _ = out.shape
-    span = SLOTS * BLK
-
-    def block(slot):
+def left_parts(value):
+    high, low = split(value)
+    return jnp.concatenate([high, high, low], axis=1)
+
+
+def right_parts(value):
+    high, low = split(value)
+    return jnp.concatenate([high, low, high], axis=0)
+
+
+def dot(left, right):
+    return jnp.dot(left, right, preferred_element_type=jnp.float32)
+
+
+def pack_kernel(slots, place, stored, out):
+    here, half = place[0], place[1]
+    chips = out.shape[0]
+    rows = stored.shape[1]
+
+    def block(slot, start, count):
         index = slots[slot]
         safe = jnp.maximum(index, 0)
         lane = pl.multiple_of(lax.rem(safe, 2) * BLK, BLK)
-        value = stored[lax.div(safe, 2), :, pl.ds(lane, BLK)]
+        value = stored[lax.div(safe, 2), pl.ds(start, count), pl.ds(lane, BLK)]
         return jnp.where(index >= 0, value, 0.0)
 
-    mine = jnp.concatenate([block(here * SLOTS + s) for s in range(SLOTS)], axis=1)
-    unit_rows = unit[...]
+    mine = jnp.concatenate([block(here * SLOTS + s, 0, rows) for s in range(SLOTS)], axis=1)
+    start = pl.multiple_of(half * (rows // 2), rows // 2)
     for chip in range(chips):
-        out[chip, :, 0:span] = mine
-        out[chip, :, 2 * span :] = unit_rows
+        out[chip, 0:rows, :] = mine
         for s in range(SLOTS):
-            out[chip, :, span + s * BLK : span + (s + 1) * BLK] = block(chip * SLOTS + s)
-
-
-def normal_kernel(gathered, col_out, row_out):
-    span = SLOTS * BLK
-    unit = gathered[:, 2 * span :].T
-    col_out[...] = product(unit, gathered[:, :span], ((1,), (0,)))
-    row_out[...] = product(unit, gathered[:, span : 2 * span], ((1,), (0,)))
-
-
-def window_kernel(blocks, own, other, inverse, out):
-    total = None
+            out[chip, rows:, s * BLK : (s + 1) * BLK] = block(chip * SLOTS + s, start, rows // 2)
+
+
+def inverse_kernel(blocks, inverse, out):
+    listed = []
     for s in range(SLOTS):
         lane = pl.multiple_of(jnp.maximum(blocks[s], 0) * BLK, BLK)
-        at = slice(s * BLK, (s + 1) * BLK)
-        value = product(own[:, at] + other[:, at], inverse[:, pl.ds(lane, BLK)], ((1,), (1,)))
-        total = value if total is None else total + value
-    out[...] = total
+        listed.append(inverse[:, pl.ds(lane, BLK)].T)
+    out[...] = right_parts(jnp.concatenate(listed, axis=0))
+
+
+def unit_kernel(place, near, far, out):
+    chip = place[2]
+    count = near.shape[0]
+    pieces = []
+    for source in range(2 * count):
+        bits = lax.bitwise_xor(chip, source)
+        at = (
+            lax.bitwise_and(lax.shift_right_logical(bits, 2), 1)
+            + lax.bitwise_and(bits, 2)
+            + lax.bitwise_and(bits, 1) * 4
+        )
+        value = jnp.where(bits < count, near[at], far[at])
+        pieces.append(value.T)
+    out[...] = left_parts(jnp.concatenate(pieces, axis=1))
+
+
+def normal_kernel(unit, gathered, out):
+    chips, _, span = gathered.shape
+    rows = unit.shape[1] // (3 * chips)
+    out[...] = dot(unit[...], right_parts(gathered[:, :rows, :].reshape(chips * rows, span)))
+
+
+def row_normal_kernel(place, unit, own, other, out):
+    chips, half, span = own.shape
+    first = place[1] == 0
+    low = jnp.where(first, own[...], other[...])
+    high = jnp.where(first, other[...], own[...])
+    listed = jnp.concatenate([low, high], axis=1).reshape(chips * 2 * half, span)
+    out[...] = dot(unit[...], right_parts(listed))
+
+
+def window_kernel(inverse, own, other, out):
+    out[...] = dot(left_parts(own[...] + other[...]), inverse[...])
 
 
 def diagonal_kernel(blocks, own, other, arrived, tile_out, out):
@@ -75,14 +104,12 @@
     for c in range(1, arrived.shape[0]):
         tile = tile + arrived[c]
     tile_out[...] = -tile
-    total = None
+    listed = []
     for s in range(SLOTS):
         place = blocks[s]
         lane = pl.multiple_of(jnp.maximum(place, 0) * BLK, BLK)
-        at = slice(s * BLK, (s + 1) * BLK)
-        listed = jnp.where(place >= 0, tile_out[:, pl.ds(lane, BLK)], 0.0)
-        value = product(own[:, at] + other[:, at], listed, ((1,), (1,)))
-        total = value if total is None else total + value
+        listed.append(jnp.where(place >= 0, tile_out[:, pl.ds(lane, BLK)], 0.0).T)
+    total = dot(left_parts(own[...] + other[...]), right_parts(jnp.concatenate(listed, axis=0)))
     rows = out.shape[0]
     width = total.shape[1]
     total = total.reshape(rows, 2, 8, width)
@@ -139,35 +166,56 @@
     own_blocks = lax.dynamic_slice(window, (chip * SLOTS,), (SLOTS,))
     own_blocks = own_blocks - chip * range_blocks - core * row_blocks
     own_blocks = jnp.where(own_blocks < row_blocks, own_blocks, -1)
-    place = col.reshape(1).astype(jnp.int32)
+    x_lo = lax.axis_index("x_lo")
+    place = jnp.stack([col, x_lo, chip]).astype(jnp.int32)
+    swap = [(0, 1), (1, 0)]
 
     stored = jnp.broadcast_to(panel.T[None], (cols, panel.shape[1], panel.shape[0]))
     stored = lax.all_to_all(stored, COL, 0, 0, tiled=True)
+
+    near = unit_inverse[None]
+    for step in (4, 2, 1):
+        pairs = [(z, z ^ step) for z in range(lax.axis_size("z"))]
+        near = jnp.concatenate([near, lax.ppermute(near, "z", pairs)], axis=0)
+        if step == 2:
+            near, stored = lax.optimization_barrier((near, stored))
+    far = lax.ppermute(near, "x_hi", swap)
+
     payload = call(
         pack_kernel,
-        f32(chips, unit_rows, 2 * span + width),
-        [SMEM, SMEM, VMEM, VMEM],
+        f32(chips, unit_rows + unit_rows // 2, span),
+        [SMEM, SMEM, VMEM],
+        moved=1024 * 1024,
+    )(slots, place, stored)
+    gathered = lax.all_to_all(payload, CHIPS, 0, 0, tiled=True)
+    inverse = call(
+        inverse_kernel,
+        jax.ShapeDtypeStruct((3 * span, rows_here), jnp.bfloat16),
+        [SMEM, VMEM],
+        moved=3 * 1024 * 1024,
+    )(col_blocks, ancestor_inverse)
+    unit = call(
+        unit_kernel,
+        jax.ShapeDtypeStruct((width, 3 * chips * unit_rows), jnp.bfloat16),
+        [SMEM, VMEM, VMEM],
         moved=2 * 1024 * 1024,
-    )(slots, place, stored, unit_inverse)
-    gathered = lax.all_to_all(payload, CHIPS, 0, 0, tiled=True)
-    gathered = gathered.reshape(chips * unit_rows, 2 * span + width)
-    col_own, row_own = call(
-        normal_kernel,
-        (f32(width, span), f32(width, span)),
-        [VMEM],
-        flops=2 * 3 * chips * unit_rows * width * 2 * span,
-        moved=3 * 1024 * 1024,
-    )(gathered)
-    swap = [(0, 1), (1, 0)]
+    )(place, near, far)
+    flops = 2 * 3 * chips * unit_rows * width * span
+    col_own = call(normal_kernel, f32(width, span), [VMEM, VMEM], flops, 2 * 1024 * 1024)(unit, gathered)
     col_other = lax.ppermute(col_own, "core", swap)
-    row_other = lax.ppermute(row_own, "core", swap)
     partial_tile = call(
         window_kernel,
         f32(width, rows_here),
-        [SMEM, VMEM, VMEM, VMEM],
+        [VMEM, VMEM, VMEM],
         flops=2 * 3 * width * span * rows_here,
         moved=3 * 1024 * 1024,
-    )(col_blocks, col_own, col_other, ancestor_inverse)
+    )(inverse, col_own, col_other)
+    partial_tile, half_own = lax.optimization_barrier((partial_tile, gathered[:, unit_rows:, :]))
+    half_other = lax.ppermute(half_own, "x_lo", swap)
+    row_own = call(
+        row_normal_kernel, f32(width, span), [SMEM, VMEM, VMEM, VMEM], flops, 2 * 1024 * 1024
+    )(place, unit, half_own, half_other)
+    row_other = lax.ppermute(row_own, "core", swap)
     partial_tile = partial_tile.reshape(cols, width // cols, rows_here)
     arrived = lax.all_to_all(partial_tile, COL, 0, 0, tiled=True)
     row_count = lax.axis_size(ROW)

time: 123 us -> 131 us (1.065)
  blocking collectives: 60.9 us -> 22.8 us
  starting transfers between devices: 21.8 us -> 56.7 us
  Pallas kernels: 6.45 us -> 11.9 us
  waiting for transfers between devices: 29.1 us -> 33.7 us
  other arithmetic: 1.04 us -> 2.66 us
    all_to_all x1 -> x0, blocking collectives: 42.6 us -> none  [on_device(): gathered = lax.all_to_all(payload, CHIPS, 0, 0, tiled=True)]
    ppermute x0 -> x5, starting transfers between devices: none -> 26.7 us  [the longest x3 18.7 us: on_device(): near = jnp.concatenate([near, lax.ppermute(near, 'z', pairs)], axis=0)]
    ppermute x0 -> x5, waiting for transfers between devices: none -> 23.1 us  [the longest x3 14.6 us: on_device(): near = jnp.concatenate([near, lax.ppermute(near, 'z', pairs)], axis=0)]
    all_to_all x1, waiting for transfers between devices: 16.6 us -> 6.24 us  [on_device(): arrived = lax.all_to_all(partial_tile, COL, 0, 0, tiled=True)]
    all_to_all x1, waiting for transfers between devices: 8.76 us -> 1.3 us  [on_device(): stored = lax.all_to_all(stored, COL, 0, 0, tiled=True)]
    all_to_all x0 -> x1, starting transfers between devices: none -> 6.56 us  [on_device(): gathered = lax.all_to_all(payload, CHIPS, 0, 0, tiled=True)]
    pallas_call x3 -> x6, Pallas kernels: 4.36 us -> 9.68 us  [the longest x1 2.85 us: on_device(): call(window_kernel, f32(width, rows_here), [VMEM, VMEM, VMEM], flops=2 *...]
    all_to_all x1, blocking collectives: 18.4 us -> 22.8 us  [on_device(): shares = lax.all_to_all(share, ROW, 0, 0, tiled=True)]
  transfers between devices with their start and end apart: 4 -> 10, of which waited for: 4 -> 8; matrix products, arithmetic and copies ran while one was open for 1% -> 3% of each run, Pallas kernels for 0% -> 4%
where the time goes in v2:
time: 131 us; the launch traced here: 130 us
  starting transfers between devices  56.7 us (43%)
  waiting for transfers between devices  33.7 us (26%)
  blocking collectives  22.8 us (17%)
  Pallas kernels  11.9 us (9%)
  other arithmetic  2.66 us (2%)
  local copies, waits for them, and re-layouts  1.49 us (1%)
    all_to_all x1, blocking collectives, on_device(): shares = lax.all_to_all(share, ROW, 0, 0, tiled=True)  22.8 us
    ppermute x3, starting transfers between devices, on_device(): near = jnp.concatenate([near, lax.ppermute(near, 'z', pairs)], axis=0)  18.7 us
    ppermute x3, waiting for transfers between devices, on_device(): near = jnp.concatenate([near, lax.ppermute(near, 'z', pairs)], axis=0)  14.6 us
    all_to_all x1, starting transfers between devices, on_device(): stored = lax.all_to_all(stored, COL, 0, 0, tiled=True)  7.85 us
    all_to_all x1, starting transfers between devices, on_device(): gathered = lax.all_to_all(payload, CHIPS, 0, 0, tiled=True)  6.56 us
    all_to_all x1, waiting for transfers between devices, on_device(): arrived = lax.all_to_all(partial_tile, COL, 0, 0, tiled=True)  6.24 us
    all_to_all x1, starting transfers between devices, on_device(): arrived = lax.all_to_all(partial_tile, COL, 0, 0, tiled=True)  6.04 us
    ppermute x1, starting transfers between devices, on_device(): col_other = lax.ppermute(col_own, 'core', swap)  5.88 us
  transfers between devices with their start and end apart: 10, of which 8 were waited for; matrix products, arithmetic and copies ran while one was open for 3% of the time, Pallas kernels for 4%

profile of v2, /device:TPU:1, one launch (start us, length us, event | category | flops | bytes accessed | tf_op | source)
XLA Modules:
  0.0 130.1 jit_solution(7276578254653089928)
XLA Ops:
  0.6 11.5 %collective-permute-start = (f32[1,16,512]{2,1,0:T(8,128)}, f32[1,16,512]{2,1,0:T(8,128)S(1)}, u32[]{:S(2)}, u32[]{:S(2)}) collective-permute-start(f32[1,16,512]{2,1,0:T(8,128)} %bitcast.6), channel_id=1, source_target_pairs={{0,128},{32,160},{64,192},{96,224},{128,0},{160,32},{192,64},{224,... | collective-permute-start | bytes 98312 | tf_op jit(solution)/shard_map/ppermute | solution.py:179
  12.1 1.4 %broadcast_in_dim.10 = f32[16,16,256]{2,1,0:T(8,128)} broadcast(f32[16,256]{1,0:T(8,128)} %bitcast.9), dimensions={1,2} | broadcast | bytes 278528 | tf_op jit(solution)/shard_map/broadcast_in_dim | solution.py:173
  13.6 7.9 %all-to-all-start = ((f32[16,16,256]{2,1,0:T(8,128)}), f32[16,16,256]{2,1,0:T(8,128)S(1)}, u32[]{:S(2)}, u32[]{:S(2)}) async-start(f32[16,16,256]{2,1,0:T(8,128)} %broadcast_in_dim.10), calls=%async_computation | async-start | bytes 524288 | tf_op jit(solution)/shard_map/all_to_all | solution.py:174
  21.4 0.7 broadcast_add_fusion.2
  22.1 0.2 convert_reduce_fusion
  22.4 0.8 pad_maximum_fusion.1
  23.2 4.0 %collective-permute-start.1 = (f32[2,16,512]{2,1,0:T(8,128)S(1)}, f32[2,16,512]{2,1,0:T(8,128)S(1)}, u32[]{:S(2)}, u32[]{:S(2)}) collective-permute-start(f32[2,16,512]{2,1,0:T(8,128)S(1)} %pad_maximum_fusion.1), channel_id=1, source_target_pairs={{0,64},{32,96},{64,0},{96,32},{128,192},{160,224},{192,128},{224,1... | collective-permute-start | bytes 196616 | tf_op jit(solution)/shard_map/ppermute | solution.py:179
  27.3 2.1 %collective-permute-done.1 = f32[2,16,512]{2,1,0:T(8,128)S(1)} collective-permute-done((f32[2,16,512]{2,1,0:T(8,128)S(1)}, f32[2,16,512]{2,1,0:T(8,128)S(1)}, u32[]{:S(2)}, u32[]{:S(2)}) %collective-permute-start.1) | collective-permute-done | bytes 65568 | tf_op jit(solution)/shard_map/ppermute | solution.py:179
  29.4 0.8 pad_maximum_fusion
  30.1 1.3 %all-to-all-done.stored = f32[16,16,256]{2,1,0:T(8,128)S(1)} async-done(((f32[16,16,256]{2,1,0:T(8,128)}), f32[16,16,256]{2,1,0:T(8,128)S(1)}, u32[]{:S(2)}, u32[]{:S(2)}) %all-to-all-start) | async-done | bytes 262176 | tf_op jit(solution)/shard_map/all_to_all | solution.py:174
  31.4 1.6 %shard_map.70 = f32[16,24,384]{2,1,0:T(8,128)} custom-call(s32[48]{0:T(128)S(1)} %broadcast_add_fusion.slots, s32[3]{0:T(128)S(1)} %pad_add_fusion.place, f32[16,16,256]{2,1,0:T(8,128)S(1)} %all-to-all-done.stored), custom_call_target="tpu_custom_call" | custom-call | bytes 1048576 | tf_op jit(solution)/shard_map/pallas_call | solution.py:184
  33.0 6.6 %all-to-all-start.1 = ((f32[16,24,384]{2,1,0:T(8,128)}), f32[16,24,384]{2,1,0:T(8,128)S(1)}, u32[]{:S(2)}, u32[]{:S(2)}) async-start(f32[16,24,384]{2,1,0:T(8,128)} %shard_map.70), calls=%async_computation.1 | async-start | bytes 1179648 | tf_op jit(solution)/shard_map/all_to_all | solution.py:190
  39.6 3.3 %collective-permute-start.2 = (f32[4,16,512]{2,1,0:T(8,128)S(1)}, f32[4,16,512]{2,1,0:T(8,128)S(1)}, u32[]{:S(2)}, u32[]{:S(2)}) collective-permute-start(f32[4,16,512]{2,1,0:T(8,128)S(1)} %pad_maximum_fusion), channel_id=1, source_target_pairs={{0,32},{32,0},{64,96},{96,64},{128,160},{160,128},{192,224},{224,1... | collective-permute-start | bytes 393224 | tf_op jit(solution)/shard_map/ppermute | solution.py:179
  42.9 12.5 %collective-permute-done.2 = f32[4,16,512]{2,1,0:T(8,128)S(1)} collective-permute-done((f32[4,16,512]{2,1,0:T(8,128)S(1)}, f32[4,16,512]{2,1,0:T(8,128)S(1)}, u32[]{:S(2)}, u32[]{:S(2)}) %collective-permute-start.2) | collective-permute-done | bytes 131104 | tf_op jit(solution)/shard_map/ppermute | solution.py:179
  55.5 4.7 %collective-permute-start.3 = (f32[8,16,512]{2,1,0:T(8,128)S(1)}, f32[8,16,512]{2,1,0:T(8,128)S(1)}, u32[]{:S(2)}, u32[]{:S(2)}) collective-permute-start(f32[8,16,512]{2,1,0:T(8,128)S(1)} %constant_dynamic-update-slice_fusion.near), channel_id=1, source_target_pairs={{0,256},{256,0},{1,257},{257,1},{2,258},{258,2},{3,259},{259,3},{4... | collective-permute-start | bytes 786440 | tf_op jit(solution)/shard_map/ppermute | solution.py:182
  60.2 3.9 %collective-permute-done.3.far = f32[8,16,512]{2,1,0:T(8,128)S(1)} collective-permute-done((f32[8,16,512]{2,1,0:T(8,128)S(1)}, f32[8,16,512]{2,1,0:T(8,128)S(1)}, u32[]{:S(2)}, u32[]{:S(2)}) %collective-permute-start.3) | collective-permute-done | bytes 262176 | tf_op jit(solution)/shard_map/ppermute | solution.py:182
  64.1 2.8 %shard_map.68.unit = bf16[512,768]{1,0:T(8,128)(2,1)S(1)} custom-call(s32[3]{0:T(128)S(1)} %pad_add_fusion.place, f32[8,16,512]{2,1,0:T(8,128)S(1)} %constant_dynamic-update-slice_fusion.near, f32[8,16,512]{2,1,0:T(8,128)S(1)} %collective-permute-done.3.far), custom_call_target="tpu_custom_call" | custom-call | bytes 2097152 | tf_op jit(solution)/shard_map/pallas_call | solution.py:197
  66.9 0.6 shard_map.71.own
  67.4 5.9 %collective-permute-start.4 = (f32[512,384]{1,0:T(8,128)S(1)}, f32[512,384]{1,0:T(8,128)}, u32[]{:S(2)}, u32[]{:S(2)}) collective-permute-start(f32[512,384]{1,0:T(8,128)S(1)} %shard_map.71.own), channel_id=1, source_target_pairs={{0,16},{16,0},{1,17},{17,1},{2,18},{18,2},{3,19},{19,3},{4,20},{20... | collective-permute-start | bytes 2359304 | tf_op jit(solution)/shard_map/ppermute | solution.py:205
  73.4 0.8 shard_map.69.inverse
  74.2 1.1 collective-permute-done.4.other
  75.4 2.8 %shard_map.72 = f32[512,384]{1,0:T(8,128)} custom-call(bf16[1152,384]{1,0:T(8,128)(2,1)S(1)} %shard_map.69.inverse, f32[512,384]{1,0:T(8,128)S(1)} %shard_map.71.own, f32[512,384]{1,0:T(8,128)} %collective-permute-done.4.other), custom_call_target="tpu_custom_call" | custom-call | flops 452984832 | bytes 3145728 | tf_op jit(solution)/shard_map/pallas_call | solution.py:206
  78.2 6.0 %all-to-all-start.2 = ((f32[16,32,384]{2,1,0:T(8,128)}), f32[16,32,384]{2,1,0:T(8,128)S(1)}, u32[]{:S(2)}, u32[]{:S(2)}) async-start(f32[16,32,384]{2,1,0:T(8,128)} %bitcast.5), calls=%async_computation.2 | async-start | bytes 1572864 | tf_op jit(solution)/shard_map/all_to_all | solution.py:220
  84.2 3.3 %collective-permute-start.5 = (f32[16,8,384]{2,1,0:T(8,128)S(1)}, f32[16,8,384]{2,1,0:T(8,128)S(1)}, u32[]{:S(2)}, u32[]{:S(2)}) collective-permute-start(f32[16,8,384]{2,1,0:T(8,128)S(1)} %slice.4.own), channel_id=1, source_target_pairs={{0,1},{1,0},{2,3},{3,2},{4,5},{5,4},{6,7},{7,6},{8,9},{9,8},{10,11... | collective-permute-start | bytes 589832 | tf_op jit(solution)/shard_map/ppermute | solution.py:214
  87.5 4.6 %collective-permute-done.5.other = f32[16,8,384]{2,1,0:T(8,128)S(1)} collective-permute-done((f32[16,8,384]{2,1,0:T(8,128)S(1)}, f32[16,8,384]{2,1,0:T(8,128)S(1)}, u32[]{:S(2)}, u32[]{:S(2)}) %collective-permute-start.5) | collective-permute-done | bytes 196640 | tf_op jit(solution)/shard_map/ppermute | solution.py:214
  92.1 1.1 shard_map.73.own
  93.2 3.7 %collective-permute-start.6 = (f32[512,384]{1,0:T(8,128)S(1)}, f32[512,384]{1,0:T(8,128)S(1)}, u32[]{:S(2)}, u32[]{:S(2)}) collective-permute-start(f32[512,384]{1,0:T(8,128)S(1)} %shard_map.73.own), channel_id=1, source_target_pairs={{0,16},{16,0},{1,17},{17,1},{2,18},{18,2},{3,19},{19,3},{4,20},{20... | collective-permute-start | bytes 2359304 | tf_op jit(solution)/shard_map/ppermute | solution.py:218
  96.9 1.9 %collective-permute-done.6.other = f32[512,384]{1,0:T(8,128)S(1)} collective-permute-done((f32[512,384]{1,0:T(8,128)S(1)}, f32[512,384]{1,0:T(8,128)S(1)}, u32[]{:S(2)}, u32[]{:S(2)}) %collective-permute-start.6) | collective-permute-done | bytes 786464 | tf_op jit(solution)/shard_map/ppermute | solution.py:218
  98.8 6.2 %all-to-all-done.2.arrived = f32[16,32,384]{2,1,0:T(8,128)S(1)} async-done(((f32[16,32,384]{2,1,0:T(8,128)}), f32[16,32,384]{2,1,0:T(8,128)S(1)}, u32[]{:S(2)}, u32[]{:S(2)}) %all-to-all-start.2) | async-done | bytes 786464 | tf_op jit(solution)/shard_map/all_to_all | solution.py:220
  105.1 1.5 %shard_map.74 = (f32[32,384]{1,0:T(8,128)}, f32[32,8,128]{2,1,0:T(8,128)S(1)}) custom-call(s32[3]{0:T(128)S(1)} %get-tuple-element.17.blocks, f32[512,384]{1,0:T(8,128)S(1)} %shard_map.73.own, f32[512,384]{1,0:T(8,128)S(1)} %collective-permute-done.6.other, f32[16,32,384]{2,1,0:T(8,128)S(1)} %all-to-all-done.2.arrived), custom_call_target="tpu_custom_call" | custom-call | flops 37748736 | bytes 3145728 | tf_op jit(solution)/shard_map/pallas_call | solution.py:222
  106.6 22.8 %all_to_all.20.arrived = f32[32,8,128]{2,1,0:T(8,128)S(1)} all-to-all(f32[32,8,128]{2,1,0:T(8,128)S(1)} %get-tuple-element.13), channel_id=1, replica_groups=mesh['x_hi'=2,'z'=8,'core'=2,'y'=8,'x_lo'=2] {'x_hi','z','core'}, dimensions={0} | all-to-all | bytes 262144 | tf_op jit(solution)/shard_map/all_to_all | solution.py:229
  129.4 0.7 shard_map.75
  (15 shorter events, 0.3 us)
Async XLA Ops:
  0.6 21.8 %collective-permute-start = (f32[1,16,512]{2,1,0:T(8,128)}, f32[1,16,512]{2,1,0:T(8,128)S(1)}, u32[]{:S(2)}, u32[]{:S(2)}) collective-permute-start(f32[1,16,512]{2,1,0:T(8,128)} %bitcast.6), channel_id=1, source_target_pairs={{0,128},{32,160},{64,192},{96,224},{128,0},{160,32},{192,64},{224,... | collective-permute-start | bytes 98312 | tf_op jit(solution)/shard_map/ppermute | solution.py:179
  13.6 17.9 %all-to-all-start = ((f32[16,16,256]{2,1,0:T(8,128)}), f32[16,16,256]{2,1,0:T(8,128)S(1)}, u32[]{:S(2)}, u32[]{:S(2)}) async-start(f32[16,16,256]{2,1,0:T(8,128)} %broadcast_in_dim.10), calls=%async_computation | async-start | bytes 524288 | tf_op jit(solution)/shard_map/all_to_all | solution.py:174
  23.2 6.2 %collective-permute-start.1 = (f32[2,16,512]{2,1,0:T(8,128)S(1)}, f32[2,16,512]{2,1,0:T(8,128)S(1)}, u32[]{:S(2)}, u32[]{:S(2)}) collective-permute-start(f32[2,16,512]{2,1,0:T(8,128)S(1)} %pad_maximum_fusion.1), channel_id=1, source_target_pairs={{0,64},{32,96},{64,0},{96,32},{128,192},{160,224},{192,128},{224,1... | collective-permute-start | bytes 196616 | tf_op jit(solution)/shard_map/ppermute | solution.py:179
  33.0 33.8 %all-to-all-start.1 = ((f32[16,24,384]{2,1,0:T(8,128)}), f32[16,24,384]{2,1,0:T(8,128)S(1)}, u32[]{:S(2)}, u32[]{:S(2)}) async-start(f32[16,24,384]{2,1,0:T(8,128)} %shard_map.70), calls=%async_computation.1 | async-start | bytes 1179648 | tf_op jit(solution)/shard_map/all_to_all | solution.py:190
  39.6 15.8 %collective-permute-start.2 = (f32[4,16,512]{2,1,0:T(8,128)S(1)}, f32[4,16,512]{2,1,0:T(8,128)S(1)}, u32[]{:S(2)}, u32[]{:S(2)}) collective-permute-start(f32[4,16,512]{2,1,0:T(8,128)S(1)} %pad_maximum_fusion), channel_id=1, source_target_pairs={{0,32},{32,0},{64,96},{96,64},{128,160},{160,128},{192,224},{224,1... | collective-permute-start | bytes 393224 | tf_op jit(solution)/shard_map/ppermute | solution.py:179
  55.5 8.6 %collective-permute-start.3 = (f32[8,16,512]{2,1,0:T(8,128)S(1)}, f32[8,16,512]{2,1,0:T(8,128)S(1)}, u32[]{:S(2)}, u32[]{:S(2)}) collective-permute-start(f32[8,16,512]{2,1,0:T(8,128)S(1)} %constant_dynamic-update-slice_fusion.near), channel_id=1, source_target_pairs={{0,256},{256,0},{1,257},{257,1},{2,258},{258,2},{3,259},{259,3},{4... | collective-permute-start | bytes 786440 | tf_op jit(solution)/shard_map/ppermute | solution.py:182
  66.8 6.6 %copy-start = (f32[384,768]{1,0:T(8,128)S(1)}, f32[384,768]{1,0:T(8,128)}, u32[]{:S(2)}) copy-start(f32[384,768]{1,0:T(8,128)} %inverse.1) | copy-start | bytes 3538948
  67.4 7.9 %collective-permute-start.4 = (f32[512,384]{1,0:T(8,128)S(1)}, f32[512,384]{1,0:T(8,128)}, u32[]{:S(2)}, u32[]{:S(2)}) collective-permute-start(f32[512,384]{1,0:T(8,128)S(1)} %shard_map.71.own), channel_id=1, source_target_pairs={{0,16},{16,0},{1,17},{17,1},{2,18},{18,2},{3,19},{19,3},{4,20},{20... | collective-permute-start | bytes 2359304 | tf_op jit(solution)/shard_map/ppermute | solution.py:205
  78.2 26.9 %all-to-all-start.2 = ((f32[16,32,384]{2,1,0:T(8,128)}), f32[16,32,384]{2,1,0:T(8,128)S(1)}, u32[]{:S(2)}, u32[]{:S(2)}) async-start(f32[16,32,384]{2,1,0:T(8,128)} %bitcast.5), calls=%async_computation.2 | async-start | bytes 1572864 | tf_op jit(solution)/shard_map/all_to_all | solution.py:220
  84.2 7.8 %collective-permute-start.5 = (f32[16,8,384]{2,1,0:T(8,128)S(1)}, f32[16,8,384]{2,1,0:T(8,128)S(1)}, u32[]{:S(2)}, u32[]{:S(2)}) collective-permute-start(f32[16,8,384]{2,1,0:T(8,128)S(1)} %slice.4.own), channel_id=1, source_target_pairs={{0,1},{1,0},{2,3},{3,2},{4,5},{5,4},{6,7},{7,6},{8,9},{9,8},{10,11... | collective-permute-start | bytes 589832 | tf_op jit(solution)/shard_map/ppermute | solution.py:214
  93.2 5.6 %collective-permute-start.6 = (f32[512,384]{1,0:T(8,128)S(1)}, f32[512,384]{1,0:T(8,128)S(1)}, u32[]{:S(2)}, u32[]{:S(2)}) collective-permute-start(f32[512,384]{1,0:T(8,128)S(1)} %shard_map.73.own), channel_id=1, source_target_pairs={{0,16},{16,0},{1,17},{17,1},{2,18},{18,2},{3,19},{19,3},{4,20},{20... | collective-permute-start | bytes 2359304 | tf_op jit(solution)/shard_map/ppermute | solution.py:218
  105.1 24.3 %copy-start.1 = (f32[16,32]{1,0:T(8,128)S(1)}, f32[16,32]{1,0:T(8,128)}, u32[]{:S(2)}) copy-start(f32[16,32]{1,0:T(8,128)} %pivot.1) | copy-start | bytes 6148

commit v3 on v2

v3 whole, which is shorter than its diff:
```python
import jax
import jax.numpy as jnp
from jax import lax
from jax.experimental import pallas as pl
from jax.experimental.pallas import tpu as pltpu
from jax.sharding import Mesh
from jax.sharding import PartitionSpec as P

BLK = 128
SLOTS = 3
ROW = ("x_hi", "z", "core")
CHIPS = ("x_hi", "z")
COL = ("y", "x_lo")
PARAMS = pltpu.CompilerParams(vmem_limit_bytes=12 * 1024 * 1024)
VMEM = pl.BlockSpec(memory_space=pltpu.VMEM)
SMEM = pl.BlockSpec(memory_space=pltpu.SMEM)


def split(value):
    high = value.astype(jnp.bfloat16)
    low = (value - high.astype(jnp.float32)).astype(jnp.bfloat16)
    return high, low


def left_parts(value):
    high, low = split(value)
    return jnp.concatenate([high, high, low], axis=1)


def right_parts(value):
    high, low = split(value)
    return jnp.concatenate([high, low, high], axis=0)


def dot(left, right):
    return jnp.dot(left, right, preferred_element_type=jnp.float32)


def spread_kernel(panel, out):
    value = panel[...]
    for col in range(out.shape[0]):
        out[col] = value


def unit_kernel(unit, out):
    rows, width = unit.shape
    half = rows // 2
    start = out.shape[2] - 2 * width
    value = unit[...]
    for chip in range(out.shape[0]):
        out[chip, :, start : start + width] = value[:half]
        out[chip, :, start + width :] = value[half:]


def pack_kernel(slots, place, stored, before, out):
    del before
    here, half = place[0], place[1]
    chips = out.shape[0]
    rows = stored.shape[1] // 2
    span = SLOTS * BLK

    def block(slot, start):
        index = slots[slot]
        safe = jnp.maximum(index, 0)
        lane = pl.multiple_of(lax.rem(safe, 2) * BLK, BLK)
        value = stored[lax.div(safe, 2), pl.ds(start, rows), pl.ds(lane, BLK)]
        return jnp.where(index >= 0, value, 0.0)

    mine = [block(here * SLOTS + s, part * rows) for part in range(2) for s in range(SLOTS)]
    mine = jnp.concatenate(mine, axis=1)
    start = pl.multiple_of(half * rows, rows)
    for chip in range(chips):
        out[chip, :, : 2 * span] = mine
        for s in range(SLOTS):
            at = 2 * span + s * BLK
            out[chip, :, at : at + BLK] = block(chip * SLOTS + s, start)


def unit_parts(gathered, width):
    start = gathered.shape[1] - 2 * width
    unit = jnp.concatenate([gathered[:, start : start + width], gathered[:, start + width :]], axis=0)
    return left_parts(unit.T)


def inverse_kernel(blocks, inverse, out):
    listed = []
    for s in range(SLOTS):
        lane = pl.multiple_of(jnp.maximum(blocks[s], 0) * BLK, BLK)
        listed.append(inverse[:, pl.ds(lane, BLK)].T)
    out[...] = right_parts(jnp.concatenate(listed, axis=0))


def normal_kernel(gathered, out):
    width, span = out.shape
    listed = jnp.concatenate([gathered[:, :span], gathered[:, span : 2 * span]], axis=0)
    out[...] = dot(unit_parts(gathered, width), right_parts(listed))


def row_normal_kernel(place, gathered, own, other, out):
    first = place[1] == 0
    low = jnp.where(first, own[...], other[...])
    high = jnp.where(first, other[...], own[...])
    listed = jnp.concatenate([low, high], axis=0)
    out[...] = dot(unit_parts(gathered, out.shape[0]), right_parts(listed))


def row_sum_kernel(own, other, out):
    out[...] = left_parts(own[...] + other[...])


def window_kernel(inverse, own, other, out):
    out[...] = dot(left_parts(own[...] + other[...]), inverse[...])


def diagonal_kernel(blocks, normal, arrived, tile_out, out):
    tile = arrived[0]
    for c in range(1, arrived.shape[0]):
        tile = tile + arrived[c]
    tile_out[...] = -tile
    listed = []
    for s in range(SLOTS):
        place = blocks[s]
        lane = pl.multiple_of(jnp.maximum(place, 0) * BLK, BLK)
        listed.append(jnp.where(place >= 0, tile_out[:, pl.ds(lane, BLK)], 0.0).T)
    total = dot(normal[...], right_parts(jnp.concatenate(listed, axis=0)))
    rows = out.shape[0]
    width = total.shape[1]
    total = total.reshape(rows, 2, 8, width)
    pad = jnp.zeros((rows, 8, 128 - 2 * width), jnp.float32)
    out[...] = jnp.concatenate([total[:, 0], total[:, 1], pad], axis=2)


def final_kernel(arrived, pivot, out):
    total = arrived[0]
    for r in range(1, arrived.shape[0]):
        total = total + arrived[r]
    width = out.shape[1]
    out[0:8, :] = pivot[0:8, :] - total[:, 0:width]
    out[8:16, :] = pivot[8:16, :] - total[:, width : 2 * width]


def call(kernel, shapes, specs, flops=0, moved=0, aliases=None):
    return pl.pallas_call(
        kernel,
        out_shape=shapes,
        in_specs=specs,
        out_specs=jax.tree.map(lambda _: VMEM, shapes),
        compiler_params=PARAMS,
        input_output_aliases=aliases or {},
        cost_estimate=pl.CostEstimate(flops=flops, bytes_accessed=moved, transcendentals=0),
    )


def f32(*shape):
    return jax.ShapeDtypeStruct(shape, jnp.float32)


def on_device(ancestor_inverse, panel, unit_inverse, pivot_inverse, panel_blocks):
    chip = lax.axis_index(CHIPS)
    core = lax.axis_index("core")
    col = lax.axis_index(COL)
    cols = lax.axis_size(COL)
    chips = lax.axis_size(CHIPS)
    rows_here, cols_here = ancestor_inverse.shape
    unit_rows, width = unit_inverse.shape
    range_blocks = cols_here // BLK
    row_blocks = rows_here // BLK
    span = SLOTS * BLK
    total_blocks = panel_blocks.shape[0]

    owner = panel_blocks // range_blocks
    order = jnp.arange(total_blocks, dtype=jnp.int32)
    same = (owner[:, None] == owner[None, :]) & (order[None, :] < order[:, None])
    slot_of = owner * SLOTS + jnp.sum(same.astype(jnp.int32), axis=1)
    all_slots = jnp.arange(cols * SLOTS, dtype=jnp.int32)
    hit = (slot_of[None, :] == all_slots[:, None]).astype(jnp.int32)
    slots = jnp.sum(hit * (order + 1)[None, :], axis=1) - 1
    window = jnp.sum(hit * (panel_blocks + 1)[None, :], axis=1) - 1
    col_blocks = lax.dynamic_slice(window, (col * SLOTS,), (SLOTS,)) - col * range_blocks
    own_blocks = lax.dynamic_slice(window, (chip * SLOTS,), (SLOTS,))
    own_blocks = own_blocks - chip * range_blocks - core * row_blocks
    own_blocks = jnp.where(own_blocks < row_blocks, own_blocks, -1)
    x_lo = lax.axis_index("x_lo")
    place = jnp.stack([col, x_lo]).astype(jnp.int32)
    swap = [(0, 1), (1, 0)]
    half = unit_rows // 2
    lanes = 3 * span + 2 * width

    stored = call(spread_kernel, f32(cols, panel.shape[1], panel.shape[0]), [VMEM])(panel.T)
    stored = lax.all_to_all(stored, COL, 0, 0, tiled=True)
    before = call(unit_kernel, f32(chips, half, lanes), [VMEM])(unit_inverse)
    payload = call(
        pack_kernel,
        f32(chips, half, lanes),
        [SMEM, SMEM, VMEM, VMEM],
        moved=1024 * 1024,
        aliases={3: 0},
    )(slots, place, stored, before)
    gathered = lax.all_to_all(payload, CHIPS, 0, 0, tiled=True)
    gathered = gathered.reshape(chips * half, lanes)
    inverse = call(
        inverse_kernel,
        jax.ShapeDtypeStruct((3 * span, rows_here), jnp.bfloat16),
        [SMEM, VMEM],
        moved=3 * 1024 * 1024,
    )(col_blocks, ancestor_inverse)
    flops = 2 * 3 * chips * unit_rows * width * span
    col_own = call(normal_kernel, f32(width, span), [VMEM], flops, 2 * 1024 * 1024)(gathered)
    col_other = lax.ppermute(col_own, "core", swap)
    partial_tile = call(
        window_kernel,
        f32(width, rows_here),
        [VMEM, VMEM, VMEM],
        flops=2 * 3 * width * span * rows_here,
        moved=3 * 1024 * 1024,
    )(inverse, col_own, col_other)
    half_own = gathered[:, 2 * span : 3 * span]
    partial_tile, half_own = lax.optimization_barrier((partial_tile, half_own))
    half_other = lax.ppermute(half_own, "x_lo", swap)
    row_own = call(
        row_normal_kernel, f32(width, span), [SMEM, VMEM, VMEM, VMEM], flops, 2 * 1024 * 1024
    )(place, gathered, half_own, half_other)
    row_other = lax.ppermute(row_own, "core", swap)
    row_normal = call(
        row_sum_kernel, jax.ShapeDtypeStruct((width, 3 * span), jnp.bfloat16), [VMEM, VMEM]
    )(row_own, row_other)
    partial_tile = partial_tile.reshape(cols, width // cols, rows_here)
    arrived = lax.all_to_all(partial_tile, COL, 0, 0, tiled=True)
    row_count = lax.axis_size(ROW)
    inverse_tile, share = call(
        diagonal_kernel,
        (f32(width // cols, rows_here), f32(row_count, 8, 128)),
        [SMEM, VMEM, VMEM],
        flops=2 * 3 * width * span * (width // cols),
        moved=3 * 1024 * 1024,
    )(own_blocks, row_normal, arrived)
    shares = lax.all_to_all(share, ROW, 0, 0, tiled=True)
    diagonal_block = call(
        final_kernel, f32(*pivot_inverse.shape), [VMEM, VMEM], moved=1024 * 128
    )(shares, pivot_inverse)
    return (inverse_tile, diagonal_block)


def solution(mesh):
    finer = Mesh(
        mesh.devices.reshape(2, mesh.shape["row"] // 4, 2, mesh.shape["col"] // 2, 2),
        (*ROW, *COL),
    )
    return jax.shard_map(
        on_device,
        mesh=finer,
        in_specs=(P(ROW, COL), P(COL, ROW), P(ROW, None), P(ROW, COL), P()),
        out_specs=(P(COL, ROW), P(ROW, COL)),
        check_vma=False,
    )
```

time: 131 us -> 118 us (0.901)
  blocking collectives: 22.8 us -> 57.1 us
  starting transfers between devices: 56.7 us -> 26.2 us
  waiting for transfers between devices: 33.7 us -> 21.7 us
  Pallas kernels: 11.9 us -> 9.02 us
  other arithmetic: 2.66 us -> 1.12 us
    all_to_all x0 -> x1, blocking collectives: none -> 40.3 us  [on_device(): gathered = lax.all_to_all(payload, CHIPS, 0, 0, tiled=True)]
    ppermute x4 -> x0, starting transfers between devices: 23.4 us -> none  [the longest x3 18.7 us: on_device(): near = jnp.concatenate([near, lax.ppermute(near, 'z', pairs)], axis=0)]
    ppermute x4 -> x0, waiting for transfers between devices: 18.6 us -> none  [the longest x3 14.6 us: on_device(): near = jnp.concatenate([near, lax.ppermute(near, 'z', pairs)], axis=0)]
    all_to_all x1, waiting for transfers between devices: 1.3 us -> 7.89 us  [on_device(): stored = lax.all_to_all(stored, COL, 0, 0, tiled=True)]
    all_to_all x1 -> x0, starting transfers between devices: 6.56 us -> none  [on_device(): gathered = lax.all_to_all(payload, CHIPS, 0, 0, tiled=True)]
    all_to_all x1, blocking collectives: 22.8 us -> 16.8 us  [on_device(): shares = lax.all_to_all(share, ROW, 0, 0, tiled=True)]
    pallas_call x3 -> x5, Pallas kernels: 4.93 us -> 2.31 us  [the longest x1 0.79 us: on_device(): call(pack_kernel, f32(chips, half, lanes), [SMEM, SMEM, VMEM, VMEM], move...]
    all_to_all x1, starting transfers between devices: 6.04 us -> 3.61 us  [on_device(): arrived = lax.all_to_all(partial_tile, COL, 0, 0, tiled=True)]
  transfers between devices with their start and end apart: 10 -> 5, of which waited for: 8 -> 5; matrix products, arithmetic and copies ran while one was open for 3% -> 1% of each run, Pallas kernels for 4% -> 2%
where the time goes in v3:
time: 118 us; the launch traced here: 117 us
  blocking collectives  57.1 us (48%)
  starting transfers between devices  26.2 us (22%)
  waiting for transfers between devices  21.7 us (18%)
  Pallas kernels  9.02 us (8%)
  local copies, waits for them, and re-layouts  1.49 us (1%)
    all_to_all x1, blocking collectives, on_device(): gathered = lax.all_to_all(payload, CHIPS, 0, 0, tiled=True)  40.3 us
    all_to_all x1, blocking collectives, on_device(): shares = lax.all_to_all(share, ROW, 0, 0, tiled=True)  16.8 us
    all_to_all x1, starting transfers between devices, on_device(): stored = lax.all_to_all(stored, COL, 0, 0, tiled=True)  8.68 us
    all_to_all x1, waiting for transfers between devices, on_device(): stored = lax.all_to_all(stored, COL, 0, 0, tiled=True)  7.89 us
    ppermute x1, starting transfers between devices, on_device(): col_other = lax.ppermute(col_own, 'core', swap)  7.13 us
    all_to_all x1, waiting for transfers between devices, on_device(): arrived = lax.all_to_all(partial_tile, COL, 0, 0, tiled=True)  6.03 us
    ppermute x1, waiting for transfers between devices, on_device(): half_other = lax.ppermute(half_own, 'x_lo', swap)  4.8 us
    all_to_all x1, starting transfers between devices, on_device(): arrived = lax.all_to_all(partial_tile, COL, 0, 0, tiled=True)  3.61 us
  transfers between devices with their start and end apart: 5, of which 5 were waited for; matrix products, arithmetic and copies ran while one was open for 1% of the time, Pallas kernels for 2%

profile of v3, /device:TPU:1, one launch (start us, length us, event | category | flops | bytes accessed | tf_op | source)
XLA Modules:
  0.0 117.3 jit_solution(7968251737040800260)
XLA Ops:
  0.6 0.0 copy-start.2
  0.6 0.7 copy-done.2
  1.3 0.7 shard_map.68
  2.1 8.7 %all-to-all-start = ((f32[16,16,256]{2,1,0:T(8,128)}), f32[16,16,256]{2,1,0:T(8,128)S(1)}, u32[]{:S(2)}, u32[]{:S(2)}) async-start(f32[16,16,256]{2,1,0:T(8,128)} %shard_map.68), calls=%async_computation | async-start | bytes 524288 | tf_op jit(solution)/shard_map/all_to_all | solution.py:190
  10.8 0.7 broadcast_add_fusion.2
  11.4 0.2 convert_reduce_fusion
  11.6 0.0 copy-start.1
  11.6 0.7 copy-done.1
  12.4 0.1 pad_add_fusion.place
  12.5 0.1 select_reduce_fusion
  12.6 7.9 %all-to-all-done.stored = f32[16,16,256]{2,1,0:T(8,128)S(1)} async-done(((f32[16,16,256]{2,1,0:T(8,128)}), f32[16,16,256]{2,1,0:T(8,128)S(1)}, u32[]{:S(2)}, u32[]{:S(2)}) %all-to-all-start) | async-done | bytes 262176 | tf_op jit(solution)/shard_map/all_to_all | solution.py:190
  20.5 0.8 shard_map.70
  21.3 40.3 %all_to_all.20 = f32[16,8,2176]{2,1,0:T(8,128)S(1)} all-to-all(f32[16,8,2176]{2,1,0:T(8,128)S(1)} %shard_map.70), channel_id=1, replica_groups=mesh['x_hi'=2,'z'=8,'core'=2,'y'=8,'x_lo'=2] {'x_hi','z'}, dimensions={0} | all-to-all | bytes 2228224 | tf_op jit(solution)/shard_map/all_to_all | solution.py:199
  61.6 0.6 shard_map.72.own
  62.2 7.1 %collective-permute-start = (f32[512,384]{1,0:T(8,128)S(1)}, f32[512,384]{1,0:T(8,128)}, u32[]{:S(2)}, u32[]{:S(2)}) collective-permute-start(f32[512,384]{1,0:T(8,128)S(1)} %shard_map.72.own), channel_id=1, source_target_pairs={{0,16},{16,0},{1,17},{17,1},{2,18},{18,2},{3,19},{19,3},{4,20},{20... | collective-permute-start | bytes 2359304 | tf_op jit(solution)/shard_map/ppermute | solution.py:209
  69.4 0.1 dynamic-slice_subtract_fusion
  69.5 0.0 copy-done
  69.5 0.8 shard_map.71.inverse
  70.3 1.1 collective-permute-done.other
  71.4 2.8 %shard_map.73 = f32[512,384]{1,0:T(8,128)} custom-call(bf16[1152,384]{1,0:T(8,128)(2,1)S(1)} %shard_map.71.inverse, f32[512,384]{1,0:T(8,128)S(1)} %shard_map.72.own, f32[512,384]{1,0:T(8,128)} %collective-permute-done.other), custom_call_target="tpu_custom_call" | custom-call | flops 452984832 | bytes 3145728 | tf_op jit(solution)/shard_map/pallas_call | solution.py:210
  74.2 3.6 %all-to-all-start.2 = ((f32[16,32,384]{2,1,0:T(8,128)}), f32[16,32,384]{2,1,0:T(8,128)S(1)}, u32[]{:S(2)}, u32[]{:S(2)}) async-start(f32[16,32,384]{2,1,0:T(8,128)} %bitcast.4), calls=%async_computation.2 | async-start | bytes 1572864 | tf_op jit(solution)/shard_map/all_to_all | solution.py:228
  77.8 3.2 %collective-permute-start.1 = (f32[128,384]{1,0:T(8,128)S(1)}, f32[128,384]{1,0:T(8,128)S(1)}, u32[]{:S(2)}, u32[]{:S(2)}) collective-permute-start(f32[128,384]{1,0:T(8,128)S(1)} %slice.4.own), channel_id=1, source_target_pairs={{0,1},{1,0},{2,3},{3,2},{4,5},{5,4},{6,7},{7,6},{8,9},{9,8},{10,11... | collective-permute-start | bytes 589832 | tf_op jit(solution)/shard_map/ppermute | solution.py:219
  81.0 4.8 %collective-permute-done.1.other = f32[128,384]{1,0:T(8,128)S(1)} collective-permute-done((f32[128,384]{1,0:T(8,128)S(1)}, f32[128,384]{1,0:T(8,128)S(1)}, u32[]{:S(2)}, u32[]{:S(2)}) %collective-permute-start.1) | collective-permute-done | bytes 196640 | tf_op jit(solution)/shard_map/ppermute | solution.py:219
  85.8 1.2 %shard_map.74.own = f32[512,384]{1,0:T(8,128)S(1)} custom-call(s32[2]{0:T(128)S(1)} %pad_add_fusion.place, f32[128,2176]{1,0:T(8,128)S(1)} %bitcast.7, f32[128,384]{1,0:T(8,128)S(1)} %slice.4.own, f32[128,384]{1,0:T(8,128)S(1)} %collective-permute-done.1.other), custom_call_target="tpu_custom_call" | custom-call | flops 301989888 | bytes 2097152 | tf_op jit(solution)/shard_map/pallas_call | solution.py:220
  87.0 3.6 %collective-permute-start.2 = (f32[512,384]{1,0:T(8,128)S(1)}, f32[512,384]{1,0:T(8,128)S(1)}, u32[]{:S(2)}, u32[]{:S(2)}) collective-permute-start(f32[512,384]{1,0:T(8,128)S(1)} %shard_map.74.own), channel_id=1, source_target_pairs={{0,16},{16,0},{1,17},{17,1},{2,18},{18,2},{3,19},{19,3},{4,20},{20... | collective-permute-start | bytes 2359304 | tf_op jit(solution)/shard_map/ppermute | solution.py:223
  90.6 1.9 %collective-permute-done.2.other = f32[512,384]{1,0:T(8,128)S(1)} collective-permute-done((f32[512,384]{1,0:T(8,128)S(1)}, f32[512,384]{1,0:T(8,128)S(1)}, u32[]{:S(2)}, u32[]{:S(2)}) %collective-permute-start.2) | collective-permute-done | bytes 786464 | tf_op jit(solution)/shard_map/ppermute | solution.py:223
  92.5 0.1 shard_map.75.normal
  92.6 6.0 %all-to-all-done.2.arrived = f32[16,32,384]{2,1,0:T(8,128)S(1)} async-done(((f32[16,32,384]{2,1,0:T(8,128)}), f32[16,32,384]{2,1,0:T(8,128)S(1)}, u32[]{:S(2)}, u32[]{:S(2)}) %all-to-all-start.2) | async-done | bytes 786464 | tf_op jit(solution)/shard_map/all_to_all | solution.py:228
  98.6 1.2 %shard_map.76 = (f32[32,384]{1,0:T(8,128)}, f32[32,8,128]{2,1,0:T(8,128)S(1)}) custom-call(s32[3]{0:T(128)S(1)} %get-tuple-element.13.blocks, bf16[512,1152]{1,0:T(8,128)(2,1)S(1)} %shard_map.75.normal, f32[16,32,384]{2,1,0:T(8,128)S(1)} %all-to-all-done.2.arrived), custom_call_target="tpu_custom_call" | custom-call | flops 37748736 | bytes 3145728 | tf_op jit(solution)/shard_map/pallas_call | solution.py:230
  99.9 16.8 %all_to_all.21.arrived = f32[32,8,128]{2,1,0:T(8,128)S(1)} all-to-all(f32[32,8,128]{2,1,0:T(8,128)S(1)} %get-tuple-element.9), channel_id=1, replica_groups=mesh['x_hi'=2,'z'=8,'core'=2,'y'=8,'x_lo'=2] {'x_hi','z','core'}, dimensions={0} | all-to-all | bytes 262144 | tf_op jit(solution)/shard_map/all_to_all | solution.py:237
  116.6 0.0 copy-done.3
  116.6 0.7 shard_map.77
  (7 shorter events, 0.1 us)
Async XLA Ops:
  0.6 0.7 copy-start.2
  2.1 18.4 %all-to-all-start = ((f32[16,16,256]{2,1,0:T(8,128)}), f32[16,16,256]{2,1,0:T(8,128)S(1)}, u32[]{:S(2)}, u32[]{:S(2)}) async-start(f32[16,16,256]{2,1,0:T(8,128)} %shard_map.68), calls=%async_computation | async-start | bytes 524288 | tf_op jit(solution)/shard_map/all_to_all | solution.py:190
  11.6 0.8 copy-start.1
  61.6 7.9 %copy-start = (f32[384,768]{1,0:T(8,128)S(1)}, f32[384,768]{1,0:T(8,128)}, u32[]{:S(2)}) copy-start(f32[384,768]{1,0:T(8,128)} %inverse.1) | copy-start | bytes 3538948
  62.2 9.2 %collective-permute-start = (f32[512,384]{1,0:T(8,128)S(1)}, f32[512,384]{1,0:T(8,128)}, u32[]{:S(2)}, u32[]{:S(2)}) collective-permute-start(f32[512,384]{1,0:T(8,128)S(1)} %shard_map.72.own), channel_id=1, source_target_pairs={{0,16},{16,0},{1,17},{17,1},{2,18},{18,2},{3,19},{19,3},{4,20},{20... | collective-permute-start | bytes 2359304 | tf_op jit(solution)/shard_map/ppermute | solution.py:209
  74.2 24.4 %all-to-all-start.2 = ((f32[16,32,384]{2,1,0:T(8,128)}), f32[16,32,384]{2,1,0:T(8,128)S(1)}, u32[]{:S(2)}, u32[]{:S(2)}) async-start(f32[16,32,384]{2,1,0:T(8,128)} %bitcast.4), calls=%async_computation.2 | async-start | bytes 1572864 | tf_op jit(solution)/shard_map/all_to_all | solution.py:228
  77.8 8.0 %collective-permute-start.1 = (f32[128,384]{1,0:T(8,128)S(1)}, f32[128,384]{1,0:T(8,128)S(1)}, u32[]{:S(2)}, u32[]{:S(2)}) collective-permute-start(f32[128,384]{1,0:T(8,128)S(1)} %slice.4.own), channel_id=1, source_target_pairs={{0,1},{1,0},{2,3},{3,2},{4,5},{5,4},{6,7},{7,6},{8,9},{9,8},{10,11... | collective-permute-start | bytes 589832 | tf_op jit(solution)/shard_map/ppermute | solution.py:219
  87.0 5.5 %collective-permute-start.2 = (f32[512,384]{1,0:T(8,128)S(1)}, f32[512,384]{1,0:T(8,128)S(1)}, u32[]{:S(2)}, u32[]{:S(2)}) collective-permute-start(f32[512,384]{1,0:T(8,128)S(1)} %shard_map.74.own), channel_id=1, source_target_pairs={{0,16},{16,0},{1,17},{17,1},{2,18},{18,2},{3,19},{19,3},{4,20},{20... | collective-permute-start | bytes 2359304 | tf_op jit(solution)/shard_map/ppermute | solution.py:223
  98.6 18.0 %copy-start.3 = (f32[16,32]{1,0:T(8,128)S(1)}, f32[16,32]{1,0:T(8,128)}, u32[]{:S(2)}) copy-start(f32[16,32]{1,0:T(8,128)} %pivot.1) | copy-start | bytes 6148

commit v4 on v3

--- a/solution.py
+++ b/solution.py
@@ -14,6 +14,8 @@
 PARAMS = pltpu.CompilerParams(vmem_limit_bytes=12 * 1024 * 1024)
 VMEM = pl.BlockSpec(memory_space=pltpu.VMEM)
 SMEM = pl.BlockSpec(memory_space=pltpu.SMEM)
+ANY = pl.BlockSpec(memory_space=pl.ANY)
+STEPS = 4
 
 
 def split(value):
@@ -36,20 +38,25 @@
     return jnp.dot(left, right, preferred_element_type=jnp.float32)
 
 
-def spread_kernel(panel, out):
-    value = panel[...]
-    for col in range(out.shape[0]):
-        out[col] = value
-
-
-def unit_kernel(unit, out):
+def spread_kernel(panel, out, sems):
+    copies = [pltpu.make_async_copy(panel, out.at[col], sems.at[col]) for col in range(out.shape[0])]
+    for copy in copies:
+        copy.start()
+    for copy in copies:
+        copy.wait()
+
+
+def unit_kernel(place, unit, tail, out):
     rows, width = unit.shape
     half = rows // 2
-    start = out.shape[2] - 2 * width
-    value = unit[...]
+    quarter = width // 4
+    start = out.shape[2] - 6 * quarter
+    own = unit[...]
+    third = jnp.where(place[2] == 0, tail[...], own[:, 2 * quarter : 3 * quarter])
+    value = jnp.concatenate([own[:, : 2 * quarter], third], axis=1)
     for chip in range(out.shape[0]):
-        out[chip, :, start : start + width] = value[:half]
-        out[chip, :, start + width :] = value[half:]
+        out[chip, :, start : start + 3 * quarter] = value[:half]
+        out[chip, :, start + 3 * quarter :] = value[half:]
 
 
 def pack_kernel(slots, place, stored, before, out):
@@ -77,9 +84,16 @@
 
 
 def unit_parts(gathered, width):
-    start = gathered.shape[1] - 2 * width
-    unit = jnp.concatenate([gathered[:, start : start + width], gathered[:, start + width :]], axis=0)
-    return left_parts(unit.T)
+    quarter = width // 4
+    start = gathered.shape[1] - 6 * quarter
+    middle = gathered.shape[0] // 2
+    zeros = jnp.zeros((middle, 2 * quarter), jnp.float32)
+    pieces = []
+    for at in (start, start + 3 * quarter):
+        pieces.append(jnp.concatenate([gathered[:middle, at : at + 2 * quarter], zeros], axis=1))
+        ends = gathered[:middle, at + 2 * quarter : at + 3 * quarter]
+        pieces.append(jnp.concatenate([gathered[middle:, at : at + 3 * quarter], ends], axis=1))
+    return left_parts(jnp.concatenate(pieces, axis=0).T)
 
 
 def inverse_kernel(blocks, inverse, out):
@@ -108,8 +122,17 @@
     out[...] = left_parts(own[...] + other[...])
 
 
-def window_kernel(inverse, own, other, out):
-    out[...] = dot(left_parts(own[...] + other[...]), inverse[...])
+def window_kernel(inverse, own, other, out, made, leave):
+    steps = made.shape[0]
+    rows = made.shape[1]
+    copies = []
+    for t in range(steps):
+        at = slice(t * rows, (t + 1) * rows)
+        made[t] = dot(left_parts(own[at] + other[at]), inverse[...])
+        copies.append(pltpu.make_async_copy(made.at[t], out.at[at], leave.at[t]))
+        copies[t].start()
+    for copy in copies:
+        copy.wait()
 
 
 def diagonal_kernel(blocks, normal, arrived, tile_out, out):
@@ -139,12 +162,13 @@
     out[8:16, :] = pivot[8:16, :] - total[:, width : 2 * width]
 
 
-def call(kernel, shapes, specs, flops=0, moved=0, aliases=None):
+def call(kernel, shapes, specs, flops=0, moved=0, aliases=None, outs=VMEM, scratch=()):
     return pl.pallas_call(
         kernel,
         out_shape=shapes,
         in_specs=specs,
-        out_specs=jax.tree.map(lambda _: VMEM, shapes),
+        out_specs=jax.tree.map(lambda _: outs, shapes),
+        scratch_shapes=scratch,
         compiler_params=PARAMS,
         input_output_aliases=aliases or {},
         cost_estimate=pl.CostEstimate(flops=flops, bytes_accessed=moved, transcendentals=0),
@@ -181,14 +205,30 @@
     own_blocks = own_blocks - chip * range_blocks - core * row_blocks
     own_blocks = jnp.where(own_blocks < row_blocks, own_blocks, -1)
     x_lo = lax.axis_index("x_lo")
-    place = jnp.stack([col, x_lo]).astype(jnp.int32)
+    x_hi = lax.axis_index("x_hi")
+    place = jnp.stack([col, x_lo, x_hi]).astype(jnp.int32)
     swap = [(0, 1), (1, 0)]
     half = unit_rows // 2
-    lanes = 3 * span + 2 * width
-
-    stored = call(spread_kernel, f32(cols, panel.shape[1], panel.shape[0]), [VMEM])(panel.T)
+    lanes = 3 * span + 3 * width // 2
+
+    stored = call(
+        spread_kernel,
+        f32(cols, panel.shape[1], panel.shape[0]),
+        [ANY],
+        outs=ANY,
+        scratch=[pltpu.SemaphoreType.DMA((cols,))],
+    )(panel.T)
     stored = lax.all_to_all(stored, COL, 0, 0, tiled=True)
-    before = call(unit_kernel, f32(chips, half, lanes), [VMEM])(unit_inverse)
+    tail, slots = lax.optimization_barrier((unit_inverse[:, 3 * width // 4 :], slots))
+    tail = lax.ppermute(tail, "x_hi", [(1, 0)])
+    before = call(unit_kernel, f32(chips, half, lanes), [SMEM, VMEM, VMEM])(place, unit_inverse, tail)
+    inverse = call(
+        inverse_kernel,
+        jax.ShapeDtypeStruct((3 * span, rows_here), jnp.bfloat16),
+        [SMEM, VMEM],
+        moved=3 * 1024 * 1024,
+    )(col_blocks, ancestor_inverse)
+    stored, inverse = lax.optimization_barrier((stored, inverse))
     payload = call(
         pack_kernel,
         f32(chips, half, lanes),
@@ -198,21 +238,21 @@
     )(slots, place, stored, before)
     gathered = lax.all_to_all(payload, CHIPS, 0, 0, tiled=True)
     gathered = gathered.reshape(chips * half, lanes)
-    inverse = call(
-        inverse_kernel,
-        jax.ShapeDtypeStruct((3 * span, rows_here), jnp.bfloat16),
-        [SMEM, VMEM],
-        moved=3 * 1024 * 1024,
-    )(col_blocks, ancestor_inverse)
     flops = 2 * 3 * chips * unit_rows * width * span
     col_own = call(normal_kernel, f32(width, span), [VMEM], flops, 2 * 1024 * 1024)(gathered)
     col_other = lax.ppermute(col_own, "core", swap)
+    step = (STEPS, width // STEPS, rows_here)
     partial_tile = call(
         window_kernel,
         f32(width, rows_here),
         [VMEM, VMEM, VMEM],
         flops=2 * 3 * width * span * rows_here,
         moved=3 * 1024 * 1024,
+        outs=ANY,
+        scratch=[
+            pltpu.VMEM(step, jnp.float32),
+            pltpu.SemaphoreType.DMA((STEPS,)),
+        ],
     )(inverse, col_own, col_other)
     half_own = gathered[:, 2 * span : 3 * span]
     partial_tile, half_own = lax.optimization_barrier((partial_tile, half_own))

time: 118 us -> 115 us (0.975)
  waiting for transfers between devices: 21.7 us -> 18.3 us
  blocking collectives: 57.1 us -> 55.2 us
  starting transfers between devices: 26.2 us -> 27.5 us
  local copies, waits for them, and re-layouts: 1.49 us -> 2.71 us
    all_to_all x1, waiting for transfers between devices: 7.89 us -> 0.98 us  [on_device(): stored = lax.all_to_all(stored, COL, 0, 0, tiled=True)]
    all_to_all x1, blocking collectives: 40.3 us -> 35.8 us  [on_device(): gathered = lax.all_to_all(payload, CHIPS, 0, 0, tiled=True)]
    ppermute x0 -> x1, waiting for transfers between devices: none -> 2.98 us  [on_device(): tail = lax.ppermute(tail, 'x_hi', [(1, 0)])]
    all_to_all x1, blocking collectives: 16.8 us -> 19.4 us  [on_device(): shares = lax.all_to_all(share, ROW, 0, 0, tiled=True)]
    pallas_call x1, Pallas kernels: 2.83 us -> 1.55 us  [on_device(): call(window_kernel, f32(width, rows_here), [VMEM, VMEM, VMEM], flops=2 *...]
    ppermute x0 -> x1, starting transfers between devices: none -> 1.28 us  [on_device(): tail = lax.ppermute(tail, 'x_hi', [(1, 0)])]
  transfers between devices with their start and end apart: 5 -> 6, of which waited for: 5 -> 6; matrix products, arithmetic and copies ran while one was open for 1% -> 2% of each run, Pallas kernels for 2% -> 2%
where the time goes in v4:
time: 115 us; the launch traced here: 114 us
  blocking collectives  55.2 us (48%)
  starting transfers between devices  27.5 us (24%)
  waiting for transfers between devices  18.3 us (16%)
  Pallas kernels  8.36 us (7%)
  local copies, waits for them, and re-layouts  2.71 us (2%)
    all_to_all x1, blocking collectives, on_device(): gathered = lax.all_to_all(payload, CHIPS, 0, 0, tiled=True)  35.8 us
    all_to_all x1, blocking collectives, on_device(): shares = lax.all_to_all(share, ROW, 0, 0, tiled=True)  19.4 us
    all_to_all x1, starting transfers between devices, on_device(): stored = lax.all_to_all(stored, COL, 0, 0, tiled=True)  8.69 us
    ppermute x1, starting transfers between devices, on_device(): col_other = lax.ppermute(col_own, 'core', swap)  6.57 us
    all_to_all x1, waiting for transfers between devices, on_device(): arrived = lax.all_to_all(partial_tile, COL, 0, 0, tiled=True)  6.02 us
    ppermute x1, waiting for transfers between devices, on_device(): half_other = lax.ppermute(half_own, 'x_lo', swap)  4.57 us
    all_to_all x1, starting transfers between devices, on_device(): arrived = lax.all_to_all(partial_tile, COL, 0, 0, tiled=True)  4.02 us
    ppermute x1, starting transfers between devices, on_device(): row_other = lax.ppermute(row_own, 'core', swap)  3.7 us
  transfers between devices with their start and end apart: 6, of which 6 were waited for; matrix products, arithmetic and copies ran while one was open for 2% of the time, Pallas kernels for 2%

profile of v4, /device:TPU:1, one launch (start us, length us, event | category | flops | bytes accessed | tf_op | source)
XLA Modules:
  0.0 114.0 jit_solution(7944485888134449134)
XLA Ops:
  0.6 0.7 copy-done.2
  1.3 0.8 shard_map.68
  2.2 8.7 %all-to-all-start = ((f32[16,16,256]{2,1,0:T(8,128)}), f32[16,16,256]{2,1,0:T(8,128)S(1)}, u32[]{:S(2)}, u32[]{:S(2)}) async-start(f32[16,16,256]{2,1,0:T(8,128)} %shard_map.68), calls=%async_computation | async-start | bytes 524288 | tf_op jit(solution)/shard_map/all_to_all | solution.py:221
  10.9 0.7 broadcast_add_fusion.2
  11.6 0.2 convert_reduce_fusion
  11.8 0.1 select_reduce_fusion
  11.9 0.7 slice.6
  12.6 1.3 %collective-permute-start = (f32[16,128]{1,0:T(8,128)S(1)}, f32[16,128]{1,0:T(8,128)S(1)}, u32[]{:S(2)}, u32[]{:S(2)}) collective-permute-start(f32[16,128]{1,0:T(8,128)S(1)} %slice.6), channel_id=1, source_target_pairs={{256,0},{257,1},{258,2},{259,3},{260,4},{261,5},{262,6},{263,7},{2... | collective-permute-start | bytes 24584 | tf_op jit(solution)/shard_map/ppermute | solution.py:223
  13.9 0.1 dynamic-slice_subtract_fusion
  14.0 0.1 pad_add_fusion.place
  14.0 1.3 %copy-done = f32[384,768]{1,0:T(8,128)S(1)} copy-done((f32[384,768]{1,0:T(8,128)S(1)}, f32[384,768]{1,0:T(8,128)}, u32[]{:S(2)}) %copy-start) | copy-done | bytes 1179672
  15.3 0.8 shard_map.69.inverse
  16.1 3.0 %collective-permute-done.tail = f32[16,128]{1,0:T(8,128)S(1)} collective-permute-done((f32[16,128]{1,0:T(8,128)S(1)}, f32[16,128]{1,0:T(8,128)S(1)}, u32[]{:S(2)}, u32[]{:S(2)}) %collective-permute-start) | collective-permute-done | bytes 8224 | tf_op jit(solution)/shard_map/ppermute | solution.py:223
  19.1 0.6 shard_map.70.before
  19.7 1.0 all-to-all-done.stored
  20.6 0.8 shard_map.71
  21.4 35.8 %all_to_all.20 = f32[16,8,1920]{2,1,0:T(8,128)S(1)} all-to-all(f32[16,8,1920]{2,1,0:T(8,128)S(1)} %shard_map.71), channel_id=1, replica_groups=mesh['x_hi'=2,'z'=8,'core'=2,'y'=8,'x_lo'=2] {'x_hi','z'}, dimensions={0} | all-to-all | bytes 1966080 | tf_op jit(solution)/shard_map/all_to_all | solution.py:239
  57.2 0.6 shard_map.72.own
  57.8 6.6 %collective-permute-start.1 = (f32[512,384]{1,0:T(8,128)S(1)}, f32[512,384]{1,0:T(8,128)S(1)}, u32[]{:S(2)}, u32[]{:S(2)}) collective-permute-start(f32[512,384]{1,0:T(8,128)S(1)} %shard_map.72.own), channel_id=1, source_target_pairs={{0,16},{16,0},{1,17},{17,1},{2,18},{18,2},{3,19},{19,3},{4,20},{20... | collective-permute-start | bytes 2359304 | tf_op jit(solution)/shard_map/ppermute | solution.py:243
  64.4 1.9 %collective-permute-done.1.other = f32[512,384]{1,0:T(8,128)S(1)} collective-permute-done((f32[512,384]{1,0:T(8,128)S(1)}, f32[512,384]{1,0:T(8,128)S(1)}, u32[]{:S(2)}, u32[]{:S(2)}) %collective-permute-start.1) | collective-permute-done | bytes 786464 | tf_op jit(solution)/shard_map/ppermute | solution.py:243
  66.3 1.6 %shard_map.73 = f32[512,384]{1,0:T(8,128)} custom-call(bf16[1152,384]{1,0:T(8,128)(2,1)S(1)} %shard_map.69.inverse, f32[512,384]{1,0:T(8,128)S(1)} %shard_map.72.own, f32[512,384]{1,0:T(8,128)S(1)} %collective-permute-done.1.other), custom_call_target="tpu_custom_call" | custom-call | flops 452984832 | bytes 3145728 | tf_op jit(solution)/shard_map/pallas_call | solution.py:245
  67.8 4.0 %all-to-all-start.2 = ((f32[16,32,384]{2,1,0:T(8,128)}), f32[16,32,384]{2,1,0:T(8,128)S(1)}, u32[]{:S(2)}, u32[]{:S(2)}) async-start(f32[16,32,384]{2,1,0:T(8,128)} %bitcast.5), calls=%async_computation.2 | async-start | bytes 1572864 | tf_op jit(solution)/shard_map/all_to_all | solution.py:268
  71.9 3.3 %collective-permute-start.2 = (f32[128,384]{1,0:T(8,128)S(1)}, f32[128,384]{1,0:T(8,128)S(1)}, u32[]{:S(2)}, u32[]{:S(2)}) collective-permute-start(f32[128,384]{1,0:T(8,128)S(1)} %slice.8.own), channel_id=1, source_target_pairs={{0,1},{1,0},{2,3},{3,2},{4,5},{5,4},{6,7},{7,6},{8,9},{9,8},{10,11... | collective-permute-start | bytes 589832 | tf_op jit(solution)/shard_map/ppermute | solution.py:259
  75.1 4.6 %collective-permute-done.2.other = f32[128,384]{1,0:T(8,128)S(1)} collective-permute-done((f32[128,384]{1,0:T(8,128)S(1)}, f32[128,384]{1,0:T(8,128)S(1)}, u32[]{:S(2)}, u32[]{:S(2)}) %collective-permute-start.2) | collective-permute-done | bytes 196640 | tf_op jit(solution)/shard_map/ppermute | solution.py:259
  79.7 1.2 %shard_map.74.own = f32[512,384]{1,0:T(8,128)S(1)} custom-call(s32[3]{0:T(128)S(1)} %pad_add_fusion.place, f32[128,1920]{1,0:T(8,128)S(1)} %bitcast.8, f32[128,384]{1,0:T(8,128)S(1)} %slice.8.own, f32[128,384]{1,0:T(8,128)S(1)} %collective-permute-done.2.other), custom_call_target="tpu_custom_call" | custom-call | flops 301989888 | bytes 2097152 | tf_op jit(solution)/shard_map/pallas_call | solution.py:260
  80.9 3.7 %collective-permute-start.3 = (f32[512,384]{1,0:T(8,128)S(1)}, f32[512,384]{1,0:T(8,128)S(1)}, u32[]{:S(2)}, u32[]{:S(2)}) collective-permute-start(f32[512,384]{1,0:T(8,128)S(1)} %shard_map.74.own), channel_id=1, source_target_pairs={{0,16},{16,0},{1,17},{17,1},{2,18},{18,2},{3,19},{19,3},{4,20},{20... | collective-permute-start | bytes 2359304 | tf_op jit(solution)/shard_map/ppermute | solution.py:263
  84.6 1.9 %collective-permute-done.3.other = f32[512,384]{1,0:T(8,128)S(1)} collective-permute-done((f32[512,384]{1,0:T(8,128)S(1)}, f32[512,384]{1,0:T(8,128)S(1)}, u32[]{:S(2)}, u32[]{:S(2)}) %collective-permute-start.3) | collective-permute-done | bytes 786464 | tf_op jit(solution)/shard_map/ppermute | solution.py:263
  86.5 0.1 shard_map.75.normal
  86.6 6.0 %all-to-all-done.2.arrived = f32[16,32,384]{2,1,0:T(8,128)S(1)} async-done(((f32[16,32,384]{2,1,0:T(8,128)}), f32[16,32,384]{2,1,0:T(8,128)S(1)}, u32[]{:S(2)}, u32[]{:S(2)}) %all-to-all-start.2) | async-done | bytes 786464 | tf_op jit(solution)/shard_map/all_to_all | solution.py:268
  92.7 1.2 %shard_map.76 = (f32[32,384]{1,0:T(8,128)}, f32[32,8,128]{2,1,0:T(8,128)S(1)}) custom-call(s32[3]{0:T(128)S(1)} %get-tuple-element.21.blocks, bf16[512,1152]{1,0:T(8,128)(2,1)S(1)} %shard_map.75.normal, f32[16,32,384]{2,1,0:T(8,128)S(1)} %all-to-all-done.2.arrived), custom_call_target="tpu_custom_call" | custom-call | flops 37748736 | bytes 3145728 | tf_op jit(solution)/shard_map/pallas_call | solution.py:270
  93.9 19.4 %all_to_all.21.arrived = f32[32,8,128]{2,1,0:T(8,128)S(1)} all-to-all(f32[32,8,128]{2,1,0:T(8,128)S(1)} %get-tuple-element.17), channel_id=1, replica_groups=mesh['x_hi'=2,'z'=8,'core'=2,'y'=8,'x_lo'=2] {'x_hi','z','core'}, dimensions={0} | all-to-all | bytes 262144 | tf_op jit(solution)/shard_map/all_to_all | solution.py:277
  113.3 0.7 shard_map.77
  (10 shorter events, 0.0 us)
Async XLA Ops:
  0.6 0.7 copy-start.2
  2.2 18.4 %all-to-all-start = ((f32[16,16,256]{2,1,0:T(8,128)}), f32[16,16,256]{2,1,0:T(8,128)S(1)}, u32[]{:S(2)}, u32[]{:S(2)}) async-start(f32[16,16,256]{2,1,0:T(8,128)} %shard_map.68), calls=%async_computation | async-start | bytes 524288 | tf_op jit(solution)/shard_map/all_to_all | solution.py:221
  10.9 8.2 %copy-start.1 = (f32[16,512]{1,0:T(8,128)S(1)}, f32[16,512]{1,0:T(8,128)}, u32[]{:S(2)}) copy-start(f32[16,512]{1,0:T(8,128)} %unit.1) | copy-start | bytes 98308
  12.6 6.5 %collective-permute-start = (f32[16,128]{1,0:T(8,128)S(1)}, f32[16,128]{1,0:T(8,128)S(1)}, u32[]{:S(2)}, u32[]{:S(2)}) collective-permute-start(f32[16,128]{1,0:T(8,128)S(1)} %slice.6), channel_id=1, source_target_pairs={{256,0},{257,1},{258,2},{259,3},{260,4},{261,5},{262,6},{263,7},{2... | collective-permute-start | bytes 24584 | tf_op jit(solution)/shard_map/ppermute | solution.py:223
  14.0 1.3 %copy-start = (f32[384,768]{1,0:T(8,128)S(1)}, f32[384,768]{1,0:T(8,128)}, u32[]{:S(2)}) copy-start(f32[384,768]{1,0:T(8,128)} %inverse.1) | copy-start | bytes 3538948
  57.8 8.5 %collective-permute-start.1 = (f32[512,384]{1,0:T(8,128)S(1)}, f32[512,384]{1,0:T(8,128)S(1)}, u32[]{:S(2)}, u32[]{:S(2)}) collective-permute-start(f32[512,384]{1,0:T(8,128)S(1)} %shard_map.72.own), channel_id=1, source_target_pairs={{0,16},{16,0},{1,17},{17,1},{2,18},{18,2},{3,19},{19,3},{4,20},{20... | collective-permute-start | bytes 2359304 | tf_op jit(solution)/shard_map/ppermute | solution.py:243
  67.8 24.8 %all-to-all-start.2 = ((f32[16,32,384]{2,1,0:T(8,128)}), f32[16,32,384]{2,1,0:T(8,128)S(1)}, u32[]{:S(2)}, u32[]{:S(2)}) async-start(f32[16,32,384]{2,1,0:T(8,128)} %bitcast.5), calls=%async_computation.2 | async-start | bytes 1572864 | tf_op jit(solution)/shard_map/all_to_all | solution.py:268
  71.9 7.8 %collective-permute-start.2 = (f32[128,384]{1,0:T(8,128)S(1)}, f32[128,384]{1,0:T(8,128)S(1)}, u32[]{:S(2)}, u32[]{:S(2)}) collective-permute-start(f32[128,384]{1,0:T(8,128)S(1)} %slice.8.own), channel_id=1, source_target_pairs={{0,1},{1,0},{2,3},{3,2},{4,5},{5,4},{6,7},{7,6},{8,9},{9,8},{10,11... | collective-permute-start | bytes 589832 | tf_op jit(solution)/shard_map/ppermute | solution.py:259
  80.9 5.6 %collective-permute-start.3 = (f32[512,384]{1,0:T(8,128)S(1)}, f32[512,384]{1,0:T(8,128)S(1)}, u32[]{:S(2)}, u32[]{:S(2)}) collective-permute-start(f32[512,384]{1,0:T(8,128)S(1)} %shard_map.74.own), channel_id=1, source_target_pairs={{0,16},{16,0},{1,17},{17,1},{2,18},{18,2},{3,19},{19,3},{4,20},{20... | collective-permute-start | bytes 2359304 | tf_op jit(solution)/shard_map/ppermute | solution.py:263
  86.6 26.7 %copy-start.3 = (f32[16,32]{1,0:T(8,128)S(1)}, f32[16,32]{1,0:T(8,128)}, u32[]{:S(2)}) copy-start(f32[16,32]{1,0:T(8,128)} %pivot.1) | copy-start | bytes 6148

commit v5 on v4

--- a/solution.py
+++ b/solution.py
@@ -11,11 +11,14 @@
 ROW = ("x_hi", "z", "core")
 CHIPS = ("x_hi", "z")
 COL = ("y", "x_lo")
-PARAMS = pltpu.CompilerParams(vmem_limit_bytes=12 * 1024 * 1024)
+SMALL = 12 * 1024 * 1024
+LARGE = 56 * 1024 * 1024
 VMEM = pl.BlockSpec(memory_space=pltpu.VMEM)
 SMEM = pl.BlockSpec(memory_space=pltpu.SMEM)
 ANY = pl.BlockSpec(memory_space=pl.ANY)
 STEPS = 4
+SHARE_ROWS = 16
+SHARE_PARTS = 4
 
 
 def split(value):
@@ -46,17 +49,21 @@
         copy.wait()
 
 
-def unit_kernel(place, unit, tail, out):
+def unit_kernel(place, unit, far, out):
     rows, width = unit.shape
     half = rows // 2
     quarter = width // 4
-    start = out.shape[2] - 6 * quarter
+    kept = 5 * quarter // 2
+    group = place[2]
     own = unit[...]
-    third = jnp.where(place[2] == 0, tail[...], own[:, 2 * quarter : 3 * quarter])
-    value = jnp.concatenate([own[:, : 2 * quarter], third], axis=1)
+    other = far[...]
+    first = jnp.concatenate([own[:, :quarter], other[:, kept:]], axis=1)
+    second = jnp.concatenate([own[:, : 2 * quarter], other[:, kept : 3 * quarter]], axis=1)
+    value = jnp.where(group == 0, first, jnp.where(group == 1, second, own[:, :kept]))
+    value = jnp.concatenate([value[:half], value[half:]], axis=1)
+    start = out.shape[2] - 2 * kept
     for chip in range(out.shape[0]):
-        out[chip, :, start : start + 3 * quarter] = value[:half]
-        out[chip, :, start + 3 * quarter :] = value[half:]
+        out[chip, :, start:] = value
 
 
 def pack_kernel(slots, place, stored, before, out):
@@ -85,23 +92,36 @@
 
 def unit_parts(gathered, width):
     quarter = width // 4
-    start = gathered.shape[1] - 6 * quarter
-    middle = gathered.shape[0] // 2
-    zeros = jnp.zeros((middle, 2 * quarter), jnp.float32)
+    kept = 5 * quarter // 2
+    both = gathered[:, gathered.shape[1] - 2 * kept :]
+    count = both.shape[0] // 4
+
+    def zeros(lanes):
+        return jnp.zeros((count, lanes), jnp.float32)
+
     pieces = []
-    for at in (start, start + 3 * quarter):
-        pieces.append(jnp.concatenate([gathered[:middle, at : at + 2 * quarter], zeros], axis=1))
-        ends = gathered[:middle, at + 2 * quarter : at + 3 * quarter]
-        pieces.append(jnp.concatenate([gathered[middle:, at : at + 3 * quarter], ends], axis=1))
+    for value in (both[:, :kept], both[:, kept:]):
+        g0, g1, g2, g3 = (value[g * count : (g + 1) * count] for g in range(4))
+        pieces.append(jnp.concatenate([g0[:, :quarter], zeros(3 * quarter)], axis=1))
+        pieces.append(jnp.concatenate([g1[:, : 2 * quarter], zeros(2 * quarter)], axis=1))
+        pieces.append(jnp.concatenate([g2, g1[:, 2 * quarter :], zeros(quarter)], axis=1))
+        pieces.append(jnp.concatenate([g3, g0[:, quarter:]], axis=1))
     return left_parts(jnp.concatenate(pieces, axis=0).T)
 
 
-def inverse_kernel(blocks, inverse, out):
-    listed = []
+def inverse_kernel(blocks, inverse, out, held, sems):
+    copies = []
     for s in range(SLOTS):
         lane = pl.multiple_of(jnp.maximum(blocks[s], 0) * BLK, BLK)
-        listed.append(inverse[:, pl.ds(lane, BLK)].T)
-    out[...] = right_parts(jnp.concatenate(listed, axis=0))
+        copies.append(pltpu.make_async_copy(inverse.at[:, pl.ds(lane, BLK)], held.at[s], sems.at[s]))
+    for copy in copies:
+        copy.start()
+    span = SLOTS * BLK
+    for s in range(SLOTS):
+        copies[s].wait()
+        high, low = split(held[s].T)
+        for part, value in enumerate((high, low, high)):
+            out[part * span + s * BLK : part * span + (s + 1) * BLK, :] = value
 
 
 def normal_kernel(gathered, out):
@@ -118,8 +138,18 @@
     out[...] = dot(unit_parts(gathered, out.shape[0]), right_parts(listed))
 
 
-def row_sum_kernel(own, other, out):
-    out[...] = left_parts(own[...] + other[...])
+def row_sum_kernel(own, other, out, total, ordered):
+    width = own.shape[0]
+    count = width // SHARE_ROWS
+    each = SHARE_ROWS // SHARE_PARTS
+    for s in range(SLOTS):
+        at = slice(s * BLK, (s + 1) * BLK)
+        total[s] = own[:, at] + other[:, at]
+        for row in range(SHARE_ROWS):
+            part, place = row // each, row % each
+            value = total[s, pl.ds(row, count, stride=SHARE_ROWS), :]
+            ordered[s, pl.ds(part * count * each + place, count, stride=each), :] = value
+    out[...] = left_parts(jnp.concatenate([ordered[s] for s in range(SLOTS)], axis=1))
 
 
 def window_kernel(inverse, own, other, out, made, leave):
@@ -147,29 +177,27 @@
         listed.append(jnp.where(place >= 0, tile_out[:, pl.ds(lane, BLK)], 0.0).T)
     total = dot(normal[...], right_parts(jnp.concatenate(listed, axis=0)))
     rows = out.shape[0]
-    width = total.shape[1]
-    total = total.reshape(rows, 2, 8, width)
-    pad = jnp.zeros((rows, 8, 128 - 2 * width), jnp.float32)
-    out[...] = jnp.concatenate([total[:, 0], total[:, 1], pad], axis=2)
+    out[...] = jnp.concatenate([total[p * rows : (p + 1) * rows] for p in range(SHARE_PARTS)], axis=1)
 
 
 def final_kernel(arrived, pivot, out):
     total = arrived[0]
     for r in range(1, arrived.shape[0]):
         total = total + arrived[r]
-    width = out.shape[1]
-    out[0:8, :] = pivot[0:8, :] - total[:, 0:width]
-    out[8:16, :] = pivot[8:16, :] - total[:, width : 2 * width]
-
-
-def call(kernel, shapes, specs, flops=0, moved=0, aliases=None, outs=VMEM, scratch=()):
+    rows, width = total.shape[0], out.shape[1]
+    for p in range(SHARE_PARTS):
+        at = slice(p * rows, (p + 1) * rows)
+        out[at, :] = pivot[at, :] - total[:, p * width : (p + 1) * width]
+
+
+def call(kernel, shapes, specs, flops=0, moved=0, aliases=None, outs=VMEM, scratch=(), limit=SMALL):
     return pl.pallas_call(
         kernel,
         out_shape=shapes,
         in_specs=specs,
         out_specs=jax.tree.map(lambda _: outs, shapes),
         scratch_shapes=scratch,
-        compiler_params=PARAMS,
+        compiler_params=pltpu.CompilerParams(vmem_limit_bytes=limit),
         input_output_aliases=aliases or {},
         cost_estimate=pl.CostEstimate(flops=flops, bytes_accessed=moved, transcendentals=0),
     )
@@ -205,11 +233,12 @@
     own_blocks = own_blocks - chip * range_blocks - core * row_blocks
     own_blocks = jnp.where(own_blocks < row_blocks, own_blocks, -1)
     x_lo = lax.axis_index("x_lo")
-    x_hi = lax.axis_index("x_hi")
-    place = jnp.stack([col, x_lo, x_hi]).astype(jnp.int32)
+    heights = lax.axis_size("z")
+    group = chip // (heights // 2)
+    place = jnp.stack([col, x_lo, group]).astype(jnp.int32)
     swap = [(0, 1), (1, 0)]
     half = unit_rows // 2
-    lanes = 3 * span + 3 * width // 2
+    lanes = 3 * span + 5 * width // 4
 
     stored = call(
         spread_kernel,
@@ -217,16 +246,20 @@
         [ANY],
         outs=ANY,
         scratch=[pltpu.SemaphoreType.DMA((cols,))],
+        limit=LARGE,
     )(panel.T)
     stored = lax.all_to_all(stored, COL, 0, 0, tiled=True)
-    tail, slots = lax.optimization_barrier((unit_inverse[:, 3 * width // 4 :], slots))
-    tail = lax.ppermute(tail, "x_hi", [(1, 0)])
-    before = call(unit_kernel, f32(chips, half, lanes), [SMEM, VMEM, VMEM])(place, unit_inverse, tail)
+    unit, slots = lax.optimization_barrier((unit_inverse, slots))
+    across = [(heights + z, z ^ (heights // 2)) for z in range(heights)]
+    far = lax.ppermute(unit, CHIPS, across)
+    before = call(unit_kernel, f32(chips, half, lanes), [SMEM, VMEM, VMEM])(place, unit, far)
     inverse = call(
         inverse_kernel,
         jax.ShapeDtypeStruct((3 * span, rows_here), jnp.bfloat16),
-        [SMEM, VMEM],
+        [SMEM, ANY],
         moved=3 * 1024 * 1024,
+        scratch=[pltpu.VMEM((SLOTS, rows_here, BLK), jnp.float32), pltpu.SemaphoreType.DMA((SLOTS,))],
+        limit=LARGE,
     )(col_blocks, ancestor_inverse)
     stored, inverse = lax.optimization_barrier((stored, inverse))
     payload = call(
@@ -262,18 +295,22 @@
     )(place, gathered, half_own, half_other)
     row_other = lax.ppermute(row_own, "core", swap)
     row_normal = call(
-        row_sum_kernel, jax.ShapeDtypeStruct((width, 3 * span), jnp.bfloat16), [VMEM, VMEM]
+        row_sum_kernel,
+        jax.ShapeDtypeStruct((width, 3 * span), jnp.bfloat16),
+        [VMEM, VMEM],
+        scratch=[pltpu.VMEM((SLOTS, width, BLK), jnp.float32)] * 2,
     )(row_own, row_other)
     partial_tile = partial_tile.reshape(cols, width // cols, rows_here)
     arrived = lax.all_to_all(partial_tile, COL, 0, 0, tiled=True)
     row_count = lax.axis_size(ROW)
     inverse_tile, share = call(
         diagonal_kernel,
-        (f32(width // cols, rows_here), f32(row_count, 8, 128)),
+        (f32(width // cols, rows_here), f32(width // SHARE_PARTS, BLK)),
         [SMEM, VMEM, VMEM],
         flops=2 * 3 * width * span * (width // cols),
         moved=3 * 1024 * 1024,
     )(own_blocks, row_normal, arrived)
+    share = share.reshape(row_count, -1, BLK)
     shares = lax.all_to_all(share, ROW, 0, 0, tiled=True)
     diagonal_block = call(
         final_kernel, f32(*pivot_inverse.shape), [VMEM, VMEM], moved=1024 * 128

time: 115 us -> 124 us (1.078)
  Pallas kernels: 8.36 us -> 19.6 us
  blocking collectives: 55.2 us -> 48.1 us
  waiting for transfers between devices: 18.3 us -> 22.7 us
  starting transfers between devices: 27.5 us -> 30.7 us
  local copies, waits for them, and re-layouts: 2.71 us -> 0.03 us
    pallas_call x1, Pallas kernels: 0.84 us -> 9.18 us  [on_device(): call(spread_kernel, f32(cols, panel.shape[1], panel.shape[0]), [ANY], out...]
    all_to_all x1, blocking collectives: 35.8 us -> 29.8 us  [on_device(): gathered = lax.all_to_all(payload, CHIPS, 0, 0, tiled=True)]
    ppermute x1, waiting for transfers between devices: 2.98 us -> 8.76 us  [on_device(): far = lax.ppermute(unit, CHIPS, across)]
    all_to_all x1, starting transfers between devices: 4.02 us -> 7.6 us  [on_device(): arrived = lax.all_to_all(partial_tile, COL, 0, 0, tiled=True)]
    pallas_call x1, Pallas kernels: 0.78 us -> 2.96 us  [on_device(): call(inverse_kernel, jax.ShapeDtypeStruct((3 * span, rows_here), jnp.bflo...]
    unnamed x8 -> x6, local copies, waits for them, and re-layouts: 2 us -> 0.02 us
  transfers between devices with their start and end apart: 6 -> 6, of which waited for: 6 -> 5; matrix products, arithmetic and copies ran while one was open for 2% -> 1% of each run, Pallas kernels for 2% -> 4%
where the time goes in v5:
time: 124 us; the launch traced here: 123 us
  blocking collectives  48.1 us (39%)
  starting transfers between devices  30.7 us (25%)
  waiting for transfers between devices  22.7 us (18%)
  Pallas kernels  19.6 us (16%)
  other arithmetic  1.62 us (1%)
    all_to_all x1, blocking collectives, on_device(): gathered = lax.all_to_all(payload, CHIPS, 0, 0, tiled=True)  29.8 us
    all_to_all x1, blocking collectives, on_device(): shares = lax.all_to_all(share, ROW, 0, 0, tiled=True)  18.2 us
    pallas_call x1, Pallas kernels, on_device(): call(spread_kernel, f32(cols, panel.shape[1], panel.shape[0]), [ANY], out...  9.18 us
    ppermute x1, waiting for transfers between devices, on_device(): far = lax.ppermute(unit, CHIPS, across)  8.76 us
    all_to_all x1, starting transfers between devices, on_device(): stored = lax.all_to_all(stored, COL, 0, 0, tiled=True)  8.69 us
    all_to_all x1, starting transfers between devices, on_device(): arrived = lax.all_to_all(partial_tile, COL, 0, 0, tiled=True)  7.6 us
    ppermute x1, starting transfers between devices, on_device(): col_other = lax.ppermute(col_own, 'core', swap)  6.12 us
    all_to_all x1, waiting for transfers between devices, on_device(): arrived = lax.all_to_all(partial_tile, COL, 0, 0, tiled=True)  5.58 us
  transfers between devices with their start and end apart: 6, of which 5 were waited for; matrix products, arithmetic and copies ran while one was open for 1% of the time, Pallas kernels for 4%

profile of v5, /device:TPU:1, one launch (start us, length us, event | category | flops | bytes accessed | tf_op | source)
XLA Modules:
  0.0 123.4 jit_solution(3831908200742810400)
XLA Ops:
  0.6 9.2 %shard_map.68 = f32[16,16,256]{2,1,0:T(8,128)} custom-call(f32[16,256]{1,0:T(8,128)} %bitcast.11), custom_call_target="tpu_custom_call" | custom-call | tf_op jit(solution)/shard_map/pallas_call | solution.py:243
  9.8 8.7 %all-to-all-start = ((f32[16,16,256]{2,1,0:T(8,128)}), f32[16,16,256]{2,1,0:T(8,128)S(1)}, u32[]{:S(2)}, u32[]{:S(2)}) async-start(f32[16,16,256]{2,1,0:T(8,128)} %shard_map.68), calls=%async_computation | async-start | bytes 524288 | tf_op jit(solution)/shard_map/all_to_all | solution.py:251
  18.5 0.0 copy-start.1
  18.5 0.7 broadcast_add_fusion.2
  19.2 0.2 convert_reduce_fusion
  19.4 0.1 select_reduce_fusion
  19.5 1.3 %collective-permute-start = (f32[16,512]{1,0:T(8,128)}, f32[16,512]{1,0:T(8,128)S(1)}, u32[]{:S(2)}, u32[]{:S(2)}) collective-permute-start(f32[16,512]{1,0:T(8,128)} %unit), channel_id=1, source_target_pairs={{256,128},{288,160},{320,192},{352,224},{384,0},{416,32},{448,64},... | collective-permute-start | bytes 98312 | tf_op jit(solution)/shard_map/ppermute | solution.py:254
  20.8 0.6 dynamic-slice_subtract_fusion
  21.4 0.1 pad_add_fusion.place
  21.5 3.0 %shard_map.69.inverse = bf16[1152,384]{1,0:T(8,128)(2,1)} custom-call(s32[3]{0:T(128)} %get-tuple-element.20.blocks, f32[384,768]{1,0:T(8,128)} %inverse.1), custom_call_target="tpu_custom_call" | custom-call | bytes 3145728 | tf_op jit(solution)/shard_map/pallas_call | solution.py:256
  24.5 8.8 %collective-permute-done.far = f32[16,512]{1,0:T(8,128)S(1)} collective-permute-done((f32[16,512]{1,0:T(8,128)}, f32[16,512]{1,0:T(8,128)S(1)}, u32[]{:S(2)}, u32[]{:S(2)}) %collective-permute-start) | collective-permute-done | bytes 32800 | tf_op jit(solution)/shard_map/ppermute | solution.py:254
  33.2 0.7 shard_map.70.before
  33.9 0.0 all-to-all-done.stored
  33.9 0.8 shard_map.71
  34.7 29.8 %all_to_all.20 = f32[16,8,1792]{2,1,0:T(8,128)S(1)} all-to-all(f32[16,8,1792]{2,1,0:T(8,128)S(1)} %shard_map.71), channel_id=1, replica_groups=mesh['x_hi'=2,'z'=8,'core'=2,'y'=8,'x_lo'=2] {'x_hi','z'}, dimensions={0} | all-to-all | bytes 1835008 | tf_op jit(solution)/shard_map/all_to_all | solution.py:272
  64.6 0.7 shard_map.72.own
  65.2 6.1 %collective-permute-start.1 = (f32[512,384]{1,0:T(8,128)S(1)}, f32[512,384]{1,0:T(8,128)S(1)}, u32[]{:S(2)}, u32[]{:S(2)}) collective-permute-start(f32[512,384]{1,0:T(8,128)S(1)} %shard_map.72.own), channel_id=1, source_target_pairs={{0,16},{16,0},{1,17},{17,1},{2,18},{18,2},{3,19},{19,3},{4,20},{20... | collective-permute-start | bytes 2359304 | tf_op jit(solution)/shard_map/ppermute | solution.py:276
  71.4 1.9 %collective-permute-done.1.other = f32[512,384]{1,0:T(8,128)S(1)} collective-permute-done((f32[512,384]{1,0:T(8,128)S(1)}, f32[512,384]{1,0:T(8,128)S(1)}, u32[]{:S(2)}, u32[]{:S(2)}) %collective-permute-start.1) | collective-permute-done | bytes 786464 | tf_op jit(solution)/shard_map/ppermute | solution.py:276
  73.3 1.5 %shard_map.73 = f32[512,384]{1,0:T(8,128)} custom-call(bf16[1152,384]{1,0:T(8,128)(2,1)S(1)} %copy-done, f32[512,384]{1,0:T(8,128)S(1)} %shard_map.72.own, f32[512,384]{1,0:T(8,128)S(1)} %collective-permute-done.1.other), custom_call_target="tpu_custom_call" | custom-call | flops 452984832 | bytes 3145728 | tf_op jit(solution)/shard_map/pallas_call | solution.py:278
  74.8 7.6 %all-to-all-start.2 = ((f32[16,32,384]{2,1,0:T(8,128)}), f32[16,32,384]{2,1,0:T(8,128)S(1)}, u32[]{:S(2)}, u32[]{:S(2)}) async-start(f32[16,32,384]{2,1,0:T(8,128)} %bitcast.5), calls=%async_computation.2 | async-start | bytes 1572864 | tf_op jit(solution)/shard_map/all_to_all | solution.py:304
  82.4 3.3 %collective-permute-start.2 = (f32[128,384]{1,0:T(8,128)S(1)}, f32[128,384]{1,0:T(8,128)S(1)}, u32[]{:S(2)}, u32[]{:S(2)}) collective-permute-start(f32[128,384]{1,0:T(8,128)S(1)} %slice.4.own), channel_id=1, source_target_pairs={{0,1},{1,0},{2,3},{3,2},{4,5},{5,4},{6,7},{7,6},{8,9},{9,8},{10,11... | collective-permute-start | bytes 589832 | tf_op jit(solution)/shard_map/ppermute | solution.py:292
  85.7 4.6 %collective-permute-done.2.other = f32[128,384]{1,0:T(8,128)S(1)} collective-permute-done((f32[128,384]{1,0:T(8,128)S(1)}, f32[128,384]{1,0:T(8,128)S(1)}, u32[]{:S(2)}, u32[]{:S(2)}) %collective-permute-start.2) | collective-permute-done | bytes 196640 | tf_op jit(solution)/shard_map/ppermute | solution.py:292
  90.3 1.2 %shard_map.74.own = f32[512,384]{1,0:T(8,128)S(1)} custom-call(s32[3]{0:T(128)S(1)} %pad_add_fusion.place, f32[128,1792]{1,0:T(8,128)S(1)} %bitcast.9, f32[128,384]{1,0:T(8,128)S(1)} %slice.4.own, f32[128,384]{1,0:T(8,128)S(1)} %collective-permute-done.2.other), custom_call_target="tpu_custom_call" | custom-call | flops 301989888 | bytes 2097152 | tf_op jit(solution)/shard_map/pallas_call | solution.py:293
  91.5 3.7 %collective-permute-start.3 = (f32[512,384]{1,0:T(8,128)S(1)}, f32[512,384]{1,0:T(8,128)S(1)}, u32[]{:S(2)}, u32[]{:S(2)}) collective-permute-start(f32[512,384]{1,0:T(8,128)S(1)} %shard_map.74.own), channel_id=1, source_target_pairs={{0,16},{16,0},{1,17},{17,1},{2,18},{18,2},{3,19},{19,3},{4,20},{20... | collective-permute-start | bytes 2359304 | tf_op jit(solution)/shard_map/ppermute | solution.py:296
  95.2 1.9 %collective-permute-done.3.other = f32[512,384]{1,0:T(8,128)S(1)} collective-permute-done((f32[512,384]{1,0:T(8,128)S(1)}, f32[512,384]{1,0:T(8,128)S(1)}, u32[]{:S(2)}, u32[]{:S(2)}) %collective-permute-start.3) | collective-permute-done | bytes 786464 | tf_op jit(solution)/shard_map/ppermute | solution.py:296
  97.1 0.5 shard_map.75.normal
  97.7 0.0 copy-start.2
  97.7 5.6 %all-to-all-done.2.arrived = f32[16,32,384]{2,1,0:T(8,128)S(1)} async-done(((f32[16,32,384]{2,1,0:T(8,128)}), f32[16,32,384]{2,1,0:T(8,128)S(1)}, u32[]{:S(2)}, u32[]{:S(2)}) %all-to-all-start.2) | async-done | bytes 786464 | tf_op jit(solution)/shard_map/all_to_all | solution.py:304
  103.3 1.2 shard_map.76
  104.5 18.2 %all_to_all.21.arrived = f32[32,4,128]{2,1,0:T(4,128)S(1)} all-to-all(f32[32,4,128]{2,1,0:T(4,128)S(1)} %bitcast.10), channel_id=1, replica_groups=mesh['x_hi'=2,'z'=8,'core'=2,'y'=8,'x_lo'=2] {'x_hi','z','core'}, dimensions={0} | all-to-all | bytes 131072 | tf_op jit(solution)/shard_map/all_to_all | solution.py:314
  122.7 0.0 copy-done.2
  122.7 0.7 shard_map.77
  (7 shorter events, 0.0 us)
Async XLA Ops:
  9.8 24.1 %all-to-all-start = ((f32[16,16,256]{2,1,0:T(8,128)}), f32[16,16,256]{2,1,0:T(8,128)S(1)}, u32[]{:S(2)}, u32[]{:S(2)}) async-start(f32[16,16,256]{2,1,0:T(8,128)} %shard_map.68), calls=%async_computation | async-start | bytes 524288 | tf_op jit(solution)/shard_map/all_to_all | solution.py:251
  18.5 14.7 %copy-start.1 = (f32[16,512]{1,0:T(8,128)S(1)}, f32[16,512]{1,0:T(8,128)}, u32[]{:S(2)}) copy-start(f32[16,512]{1,0:T(8,128)} %unit) | copy-start | bytes 98308
  19.5 13.7 %collective-permute-start = (f32[16,512]{1,0:T(8,128)}, f32[16,512]{1,0:T(8,128)S(1)}, u32[]{:S(2)}, u32[]{:S(2)}) collective-permute-start(f32[16,512]{1,0:T(8,128)} %unit), channel_id=1, source_target_pairs={{256,128},{288,160},{320,192},{352,224},{384,0},{416,32},{448,64},... | collective-permute-start | bytes 98312 | tf_op jit(solution)/shard_map/ppermute | solution.py:254
  64.6 8.7 %copy-start = (bf16[1152,384]{1,0:T(8,128)(2,1)S(1)}, bf16[1152,384]{1,0:T(8,128)(2,1)}, u32[]{:S(2)}) copy-start(bf16[1152,384]{1,0:T(8,128)(2,1)} %shard_map.69.inverse) | copy-start | bytes 2654212
  65.2 8.0 %collective-permute-start.1 = (f32[512,384]{1,0:T(8,128)S(1)}, f32[512,384]{1,0:T(8,128)S(1)}, u32[]{:S(2)}, u32[]{:S(2)}) collective-permute-start(f32[512,384]{1,0:T(8,128)S(1)} %shard_map.72.own), channel_id=1, source_target_pairs={{0,16},{16,0},{1,17},{17,1},{2,18},{18,2},{3,19},{19,3},{4,20},{20... | collective-permute-start | bytes 2359304 | tf_op jit(solution)/shard_map/ppermute | solution.py:276
  74.8 28.4 %all-to-all-start.2 = ((f32[16,32,384]{2,1,0:T(8,128)}), f32[16,32,384]{2,1,0:T(8,128)S(1)}, u32[]{:S(2)}, u32[]{:S(2)}) async-start(f32[16,32,384]{2,1,0:T(8,128)} %bitcast.5), calls=%async_computation.2 | async-start | bytes 1572864 | tf_op jit(solution)/shard_map/all_to_all | solution.py:304
  82.4 7.8 %collective-permute-start.2 = (f32[128,384]{1,0:T(8,128)S(1)}, f32[128,384]{1,0:T(8,128)S(1)}, u32[]{:S(2)}, u32[]{:S(2)}) collective-permute-start(f32[128,384]{1,0:T(8,128)S(1)} %slice.4.own), channel_id=1, source_target_pairs={{0,1},{1,0},{2,3},{3,2},{4,5},{5,4},{6,7},{7,6},{8,9},{9,8},{10,11... | collective-permute-start | bytes 589832 | tf_op jit(solution)/shard_map/ppermute | solution.py:292
  91.5 5.6 %collective-permute-start.3 = (f32[512,384]{1,0:T(8,128)S(1)}, f32[512,384]{1,0:T(8,128)S(1)}, u32[]{:S(2)}, u32[]{:S(2)}) collective-permute-start(f32[512,384]{1,0:T(8,128)S(1)} %shard_map.74.own), channel_id=1, source_target_pairs={{0,16},{16,0},{1,17},{17,1},{2,18},{18,2},{3,19},{19,3},{4,20},{20... | collective-permute-start | bytes 2359304 | tf_op jit(solution)/shard_map/ppermute | solution.py:296
  97.7 25.1 %copy-start.2 = (f32[16,32]{1,0:T(8,128)S(1)}, f32[16,32]{1,0:T(8,128)}, u32[]{:S(2)}) copy-start(f32[16,32]{1,0:T(8,128)} %pivot.1) | copy-start | bytes 6148

commit v6 on v5

--- a/solution.py
+++ b/solution.py
@@ -11,8 +11,7 @@
 ROW = ("x_hi", "z", "core")
 CHIPS = ("x_hi", "z")
 COL = ("y", "x_lo")
-SMALL = 12 * 1024 * 1024
-LARGE = 56 * 1024 * 1024
+LIMIT = 12 * 1024 * 1024
 VMEM = pl.BlockSpec(memory_space=pltpu.VMEM)
 SMEM = pl.BlockSpec(memory_space=pltpu.SMEM)
 ANY = pl.BlockSpec(memory_space=pl.ANY)
@@ -109,19 +108,12 @@
     return left_parts(jnp.concatenate(pieces, axis=0).T)
 
 
-def inverse_kernel(blocks, inverse, out, held, sems):
-    copies = []
+def inverse_kernel(blocks, inverse, out):
+    listed = []
     for s in range(SLOTS):
         lane = pl.multiple_of(jnp.maximum(blocks[s], 0) * BLK, BLK)
-        copies.append(pltpu.make_async_copy(inverse.at[:, pl.ds(lane, BLK)], held.at[s], sems.at[s]))
-    for copy in copies:
-        copy.start()
-    span = SLOTS * BLK
-    for s in range(SLOTS):
-        copies[s].wait()
-        high, low = split(held[s].T)
-        for part, value in enumerate((high, low, high)):
-            out[part * span + s * BLK : part * span + (s + 1) * BLK, :] = value
+        listed.append(inverse[:, pl.ds(lane, BLK)].T)
+    out[...] = right_parts(jnp.concatenate(listed, axis=0))
 
 
 def normal_kernel(gathered, out):
@@ -190,14 +182,14 @@
         out[at, :] = pivot[at, :] - total[:, p * width : (p + 1) * width]
 
 
-def call(kernel, shapes, specs, flops=0, moved=0, aliases=None, outs=VMEM, scratch=(), limit=SMALL):
+def call(kernel, shapes, specs, flops=0, moved=0, aliases=None, outs=VMEM, scratch=()):
     return pl.pallas_call(
         kernel,
         out_shape=shapes,
         in_specs=specs,
         out_specs=jax.tree.map(lambda _: outs, shapes),
         scratch_shapes=scratch,
-        compiler_params=pltpu.CompilerParams(vmem_limit_bytes=limit),
+        compiler_params=pltpu.CompilerParams(vmem_limit_bytes=LIMIT),
         input_output_aliases=aliases or {},
         cost_estimate=pl.CostEstimate(flops=flops, bytes_accessed=moved, transcendentals=0),
     )
@@ -243,10 +235,9 @@
     stored = call(
         spread_kernel,
         f32(cols, panel.shape[1], panel.shape[0]),
-        [ANY],
+        [VMEM],
         outs=ANY,
         scratch=[pltpu.SemaphoreType.DMA((cols,))],
-        limit=LARGE,
     )(panel.T)
     stored = lax.all_to_all(stored, COL, 0, 0, tiled=True)
     unit, slots = lax.optimization_barrier((unit_inverse, slots))
@@ -256,10 +247,8 @@
     inverse = call(
         inverse_kernel,
         jax.ShapeDtypeStruct((3 * span, rows_here), jnp.bfloat16),
-        [SMEM, ANY],
+        [SMEM, VMEM],
         moved=3 * 1024 * 1024,
-        scratch=[pltpu.VMEM((SLOTS, rows_here, BLK), jnp.float32), pltpu.SemaphoreType.DMA((SLOTS,))],
-        limit=LARGE,
     )(col_blocks, ancestor_inverse)
     stored, inverse = lax.optimization_barrier((stored, inverse))
     payload = call(

time: 124 us -> 116 us (0.935)
  Pallas kernels: 19.6 us -> 9.02 us
  local copies, waits for them, and re-layouts: 0.03 us -> 2.01 us
  waiting for transfers between devices: 22.7 us -> 24.1 us
    pallas_call x1, Pallas kernels: 9.18 us -> 0.84 us  [on_device(): call(spread_kernel, f32(cols, panel.shape[1], panel.shape[0]), [VMEM], ou...]
    pallas_call x1, Pallas kernels: 2.96 us -> 0.78 us  [on_device(): call(inverse_kernel, jax.ShapeDtypeStruct((3 * span, rows_here), jnp.bflo...]
    unnamed x6 -> x8, local copies, waits for them, and re-layouts: 0.02 us -> 2 us
    ppermute x1, waiting for transfers between devices: 8.76 us -> 10.2 us  [on_device(): far = lax.ppermute(unit, CHIPS, across)]
  transfers between devices with their start and end apart: 6 -> 6, of which waited for: 5 -> 5; matrix products, arithmetic and copies ran while one was open for 1% -> 1% of each run, Pallas kernels for 4% -> 3%
where the time goes in v6:
time: 116 us
  blocking collectives  48.1 us (41%)
  starting transfers between devices  30.7 us (26%)
  waiting for transfers between devices  24.1 us (21%)
  Pallas kernels  9.02 us (8%)
  local copies, waits for them, and re-layouts  2.01 us (2%)
    all_to_all x1, blocking collectives, on_device(): gathered = lax.all_to_all(payload, CHIPS, 0, 0, tiled=True)  29.8 us
    all_to_all x1, blocking collectives, on_device(): shares = lax.all_to_all(share, ROW, 0, 0, tiled=True)  18.3 us
    ppermute x1, waiting for transfers between devices, on_device(): far = lax.ppermute(unit, CHIPS, across)  10.2 us
    all_to_all x1, starting transfers between devices, on_device(): stored = lax.all_to_all(stored, COL, 0, 0, tiled=True)  8.69 us
    all_to_all x1, starting transfers between devices, on_device(): arrived = lax.all_to_all(partial_tile, COL, 0, 0, tiled=True)  7.6 us
    ppermute x1, starting transfers between devices, on_device(): col_other = lax.ppermute(col_own, 'core', swap)  6.12 us
    all_to_all x1, waiting for transfers between devices, on_device(): arrived = lax.all_to_all(partial_tile, COL, 0, 0, tiled=True)  5.58 us
    ppermute x1, waiting for transfers between devices, on_device(): half_other = lax.ppermute(half_own, 'x_lo', swap)  4.57 us
  transfers between devices with their start and end apart: 6, of which 5 were waited for; matrix products, arithmetic and copies ran while one was open for 1% of the time, Pallas kernels for 3%

profile of v6, /device:TPU:1, one launch (start us, length us, event | category | flops | bytes accessed | tf_op | source)
XLA Modules:
  0.0 115.8 jit_solution(18390521543308962406)
XLA Ops:
  0.6 0.7 copy-done.2
  1.3 0.8 shard_map.68
  2.2 8.7 %all-to-all-start = ((f32[16,16,256]{2,1,0:T(8,128)}), f32[16,16,256]{2,1,0:T(8,128)S(1)}, u32[]{:S(2)}, u32[]{:S(2)}) async-start(f32[16,16,256]{2,1,0:T(8,128)} %shard_map.68), calls=%async_computation | async-start | bytes 524288 | tf_op jit(solution)/shard_map/all_to_all | solution.py:242
  10.9 0.0 copy-start.1
  10.9 0.7 broadcast_add_fusion.2
  11.6 0.2 convert_reduce_fusion
  11.8 0.1 select_reduce_fusion
  11.9 1.3 %collective-permute-start = (f32[16,512]{1,0:T(8,128)}, f32[16,512]{1,0:T(8,128)S(1)}, u32[]{:S(2)}, u32[]{:S(2)}) collective-permute-start(f32[16,512]{1,0:T(8,128)} %unit), channel_id=1, source_target_pairs={{256,128},{288,160},{320,192},{352,224},{384,0},{416,32},{448,64},... | collective-permute-start | bytes 98312 | tf_op jit(solution)/shard_map/ppermute | solution.py:245
  13.2 0.1 dynamic-slice_subtract_fusion
  13.3 0.1 pad_add_fusion.place
  13.4 1.3 %copy-done = f32[384,768]{1,0:T(8,128)S(1)} copy-done((f32[384,768]{1,0:T(8,128)S(1)}, f32[384,768]{1,0:T(8,128)}, u32[]{:S(2)}) %copy-start) | copy-done | bytes 1179672
  14.6 0.8 shard_map.69.inverse
  15.4 10.2 %collective-permute-done.far = f32[16,512]{1,0:T(8,128)S(1)} collective-permute-done((f32[16,512]{1,0:T(8,128)}, f32[16,512]{1,0:T(8,128)S(1)}, u32[]{:S(2)}, u32[]{:S(2)}) %collective-permute-start) | collective-permute-done | bytes 32800 | tf_op jit(solution)/shard_map/ppermute | solution.py:245
  25.6 0.7 shard_map.70.before
  26.3 0.8 shard_map.71
  27.1 29.8 %all_to_all.20 = f32[16,8,1792]{2,1,0:T(8,128)S(1)} all-to-all(f32[16,8,1792]{2,1,0:T(8,128)S(1)} %shard_map.71), channel_id=1, replica_groups=mesh['x_hi'=2,'z'=8,'core'=2,'y'=8,'x_lo'=2] {'x_hi','z'}, dimensions={0} | all-to-all | bytes 1835008 | tf_op jit(solution)/shard_map/all_to_all | solution.py:261
  56.9 0.7 shard_map.72.own
  57.6 6.1 %collective-permute-start.1 = (f32[512,384]{1,0:T(8,128)S(1)}, f32[512,384]{1,0:T(8,128)S(1)}, u32[]{:S(2)}, u32[]{:S(2)}) collective-permute-start(f32[512,384]{1,0:T(8,128)S(1)} %shard_map.72.own), channel_id=1, source_target_pairs={{0,16},{16,0},{1,17},{17,1},{2,18},{18,2},{3,19},{19,3},{4,20},{20... | collective-permute-start | bytes 2359304 | tf_op jit(solution)/shard_map/ppermute | solution.py:265
  63.8 1.9 %collective-permute-done.1.other = f32[512,384]{1,0:T(8,128)S(1)} collective-permute-done((f32[512,384]{1,0:T(8,128)S(1)}, f32[512,384]{1,0:T(8,128)S(1)}, u32[]{:S(2)}, u32[]{:S(2)}) %collective-permute-start.1) | collective-permute-done | bytes 786464 | tf_op jit(solution)/shard_map/ppermute | solution.py:265
  65.6 1.6 %shard_map.73 = f32[512,384]{1,0:T(8,128)} custom-call(bf16[1152,384]{1,0:T(8,128)(2,1)S(1)} %shard_map.69.inverse, f32[512,384]{1,0:T(8,128)S(1)} %shard_map.72.own, f32[512,384]{1,0:T(8,128)S(1)} %collective-permute-done.1.other), custom_call_target="tpu_custom_call" | custom-call | flops 452984832 | bytes 3145728 | tf_op jit(solution)/shard_map/pallas_call | solution.py:267
  67.2 7.6 %all-to-all-start.2 = ((f32[16,32,384]{2,1,0:T(8,128)}), f32[16,32,384]{2,1,0:T(8,128)S(1)}, u32[]{:S(2)}, u32[]{:S(2)}) async-start(f32[16,32,384]{2,1,0:T(8,128)} %bitcast.5), calls=%async_computation.2 | async-start | bytes 1572864 | tf_op jit(solution)/shard_map/all_to_all | solution.py:293
  74.8 3.3 %collective-permute-start.2 = (f32[128,384]{1,0:T(8,128)S(1)}, f32[128,384]{1,0:T(8,128)S(1)}, u32[]{:S(2)}, u32[]{:S(2)}) collective-permute-start(f32[128,384]{1,0:T(8,128)S(1)} %slice.4.own), channel_id=1, source_target_pairs={{0,1},{1,0},{2,3},{3,2},{4,5},{5,4},{6,7},{7,6},{8,9},{9,8},{10,11... | collective-permute-start | bytes 589832 | tf_op jit(solution)/shard_map/ppermute | solution.py:281
  78.1 4.6 %collective-permute-done.2.other = f32[128,384]{1,0:T(8,128)S(1)} collective-permute-done((f32[128,384]{1,0:T(8,128)S(1)}, f32[128,384]{1,0:T(8,128)S(1)}, u32[]{:S(2)}, u32[]{:S(2)}) %collective-permute-start.2) | collective-permute-done | bytes 196640 | tf_op jit(solution)/shard_map/ppermute | solution.py:281
  82.6 1.2 %shard_map.74.own = f32[512,384]{1,0:T(8,128)S(1)} custom-call(s32[3]{0:T(128)S(1)} %pad_add_fusion.place, f32[128,1792]{1,0:T(8,128)S(1)} %bitcast.9, f32[128,384]{1,0:T(8,128)S(1)} %slice.4.own, f32[128,384]{1,0:T(8,128)S(1)} %collective-permute-done.2.other), custom_call_target="tpu_custom_call" | custom-call | flops 301989888 | bytes 2097152 | tf_op jit(solution)/shard_map/pallas_call | solution.py:282
  83.9 3.7 %collective-permute-start.3 = (f32[512,384]{1,0:T(8,128)S(1)}, f32[512,384]{1,0:T(8,128)S(1)}, u32[]{:S(2)}, u32[]{:S(2)}) collective-permute-start(f32[512,384]{1,0:T(8,128)S(1)} %shard_map.74.own), channel_id=1, source_target_pairs={{0,16},{16,0},{1,17},{17,1},{2,18},{18,2},{3,19},{19,3},{4,20},{20... | collective-permute-start | bytes 2359304 | tf_op jit(solution)/shard_map/ppermute | solution.py:285
  87.6 1.9 %collective-permute-done.3.other = f32[512,384]{1,0:T(8,128)S(1)} collective-permute-done((f32[512,384]{1,0:T(8,128)S(1)}, f32[512,384]{1,0:T(8,128)S(1)}, u32[]{:S(2)}, u32[]{:S(2)}) %collective-permute-start.3) | collective-permute-done | bytes 786464 | tf_op jit(solution)/shard_map/ppermute | solution.py:285
  89.5 0.5 shard_map.75.normal
  90.0 0.0 copy-start.3
  90.0 5.6 %all-to-all-done.2.arrived = f32[16,32,384]{2,1,0:T(8,128)S(1)} async-done(((f32[16,32,384]{2,1,0:T(8,128)}), f32[16,32,384]{2,1,0:T(8,128)S(1)}, u32[]{:S(2)}, u32[]{:S(2)}) %all-to-all-start.2) | async-done | bytes 786464 | tf_op jit(solution)/shard_map/all_to_all | solution.py:293
  95.6 1.2 %shard_map.76 = (f32[32,384]{1,0:T(8,128)}, f32[128,128]{1,0:T(8,128)S(1)}) custom-call(s32[3]{0:T(128)S(1)} %get-tuple-element.21.blocks, bf16[512,1152]{1,0:T(8,128)(2,1)S(1)} %shard_map.75.normal, f32[16,32,384]{2,1,0:T(8,128)S(1)} %all-to-all-done.2.arrived), custom_call_target="tpu_custom_call" | custom-call | flops 37748736 | bytes 3145728 | tf_op jit(solution)/shard_map/pallas_call | solution.py:295
  96.8 18.3 %all_to_all.21.arrived = f32[32,4,128]{2,1,0:T(4,128)S(1)} all-to-all(f32[32,4,128]{2,1,0:T(4,128)S(1)} %bitcast.10), channel_id=1, replica_groups=mesh['x_hi'=2,'z'=8,'core'=2,'y'=8,'x_lo'=2] {'x_hi','z','core'}, dimensions={0} | all-to-all | bytes 131072 | tf_op jit(solution)/shard_map/all_to_all | solution.py:303
  115.1 0.7 shard_map.77
  (9 shorter events, 0.0 us)
Async XLA Ops:
  0.6 0.7 copy-start.2
  2.2 24.1 %all-to-all-start = ((f32[16,16,256]{2,1,0:T(8,128)}), f32[16,16,256]{2,1,0:T(8,128)S(1)}, u32[]{:S(2)}, u32[]{:S(2)}) async-start(f32[16,16,256]{2,1,0:T(8,128)} %shard_map.68), calls=%async_computation | async-start | bytes 524288 | tf_op jit(solution)/shard_map/all_to_all | solution.py:242
  10.9 14.7 %copy-start.1 = (f32[16,512]{1,0:T(8,128)S(1)}, f32[16,512]{1,0:T(8,128)}, u32[]{:S(2)}) copy-start(f32[16,512]{1,0:T(8,128)} %unit) | copy-start | bytes 98308
  11.9 13.7 %collective-permute-start = (f32[16,512]{1,0:T(8,128)}, f32[16,512]{1,0:T(8,128)S(1)}, u32[]{:S(2)}, u32[]{:S(2)}) collective-permute-start(f32[16,512]{1,0:T(8,128)} %unit), channel_id=1, source_target_pairs={{256,128},{288,160},{320,192},{352,224},{384,0},{416,32},{448,64},... | collective-permute-start | bytes 98312 | tf_op jit(solution)/shard_map/ppermute | solution.py:245
  13.4 1.3 %copy-start = (f32[384,768]{1,0:T(8,128)S(1)}, f32[384,768]{1,0:T(8,128)}, u32[]{:S(2)}) copy-start(f32[384,768]{1,0:T(8,128)} %inverse.1) | copy-start | bytes 3538948
  57.6 8.0 %collective-permute-start.1 = (f32[512,384]{1,0:T(8,128)S(1)}, f32[512,384]{1,0:T(8,128)S(1)}, u32[]{:S(2)}, u32[]{:S(2)}) collective-permute-start(f32[512,384]{1,0:T(8,128)S(1)} %shard_map.72.own), channel_id=1, source_target_pairs={{0,16},{16,0},{1,17},{17,1},{2,18},{18,2},{3,19},{19,3},{4,20},{20... | collective-permute-start | bytes 2359304 | tf_op jit(solution)/shard_map/ppermute | solution.py:265
  67.2 28.4 %all-to-all-start.2 = ((f32[16,32,384]{2,1,0:T(8,128)}), f32[16,32,384]{2,1,0:T(8,128)S(1)}, u32[]{:S(2)}, u32[]{:S(2)}) async-start(f32[16,32,384]{2,1,0:T(8,128)} %bitcast.5), calls=%async_computation.2 | async-start | bytes 1572864 | tf_op jit(solution)/shard_map/all_to_all | solution.py:293
  74.8 7.8 %collective-permute-start.2 = (f32[128,384]{1,0:T(8,128)S(1)}, f32[128,384]{1,0:T(8,128)S(1)}, u32[]{:S(2)}, u32[]{:S(2)}) collective-permute-start(f32[128,384]{1,0:T(8,128)S(1)} %slice.4.own), channel_id=1, source_target_pairs={{0,1},{1,0},{2,3},{3,2},{4,5},{5,4},{6,7},{7,6},{8,9},{9,8},{10,11... | collective-permute-start | bytes 589832 | tf_op jit(solution)/shard_map/ppermute | solution.py:281
  83.9 5.6 %collective-permute-start.3 = (f32[512,384]{1,0:T(8,128)S(1)}, f32[512,384]{1,0:T(8,128)S(1)}, u32[]{:S(2)}, u32[]{:S(2)}) collective-permute-start(f32[512,384]{1,0:T(8,128)S(1)} %shard_map.74.own), channel_id=1, source_target_pairs={{0,16},{16,0},{1,17},{17,1},{2,18},{18,2},{3,19},{19,3},{4,20},{20... | collective-permute-start | bytes 2359304 | tf_op jit(solution)/shard_map/ppermute | solution.py:285
  90.0 25.1 %copy-start.3 = (f32[16,32]{1,0:T(8,128)S(1)}, f32[16,32]{1,0:T(8,128)}, u32[]{:S(2)}) copy-start(f32[16,32]{1,0:T(8,128)} %pivot.1) | copy-start | bytes 6148

commit v7 on v6

--- a/solution.py
+++ b/solution.py
@@ -11,7 +11,8 @@
 ROW = ("x_hi", "z", "core")
 CHIPS = ("x_hi", "z")
 COL = ("y", "x_lo")
-LIMIT = 12 * 1024 * 1024
+SMALL = 12 * 1024 * 1024
+LARGE = 56 * 1024 * 1024
 VMEM = pl.BlockSpec(memory_space=pltpu.VMEM)
 SMEM = pl.BlockSpec(memory_space=pltpu.SMEM)
 ANY = pl.BlockSpec(memory_space=pl.ANY)
@@ -40,8 +41,11 @@
     return jnp.dot(left, right, preferred_element_type=jnp.float32)
 
 
-def spread_kernel(panel, out, sems):
-    copies = [pltpu.make_async_copy(panel, out.at[col], sems.at[col]) for col in range(out.shape[0])]
+def spread_kernel(panel, out, held, sems):
+    first = pltpu.make_async_copy(panel, held, sems.at[0])
+    first.start()
+    first.wait()
+    copies = [pltpu.make_async_copy(held, out.at[col], sems.at[1 + col]) for col in range(out.shape[0])]
     for copy in copies:
         copy.start()
     for copy in copies:
@@ -52,17 +56,12 @@
     rows, width = unit.shape
     half = rows // 2
     quarter = width // 4
-    kept = 5 * quarter // 2
-    group = place[2]
-    own = unit[...]
-    other = far[...]
-    first = jnp.concatenate([own[:, :quarter], other[:, kept:]], axis=1)
-    second = jnp.concatenate([own[:, : 2 * quarter], other[:, kept : 3 * quarter]], axis=1)
-    value = jnp.where(group == 0, first, jnp.where(group == 1, second, own[:, :kept]))
-    value = jnp.concatenate([value[:half], value[half:]], axis=1)
-    start = out.shape[2] - 2 * kept
+    start = out.shape[2] - 6 * quarter
+    third = jnp.where(place[2] == 0, far[:, 3 * quarter :], unit[:, 2 * quarter : 3 * quarter])
+    value = jnp.concatenate([unit[:, : 2 * quarter], third], axis=1)
     for chip in range(out.shape[0]):
-        out[chip, :, start:] = value
+        out[chip, :, start : start + 3 * quarter] = value[:half]
+        out[chip, :, start + 3 * quarter :] = value[half:]
 
 
 def pack_kernel(slots, place, stored, before, out):
@@ -91,20 +90,14 @@
 
 def unit_parts(gathered, width):
     quarter = width // 4
-    kept = 5 * quarter // 2
-    both = gathered[:, gathered.shape[1] - 2 * kept :]
-    count = both.shape[0] // 4
-
-    def zeros(lanes):
-        return jnp.zeros((count, lanes), jnp.float32)
-
+    start = gathered.shape[1] - 6 * quarter
+    middle = gathered.shape[0] // 2
+    zeros = jnp.zeros((middle, 2 * quarter), jnp.float32)
     pieces = []
-    for value in (both[:, :kept], both[:, kept:]):
-        g0, g1, g2, g3 = (value[g * count : (g + 1) * count] for g in range(4))
-        pieces.append(jnp.concatenate([g0[:, :quarter], zeros(3 * quarter)], axis=1))
-        pieces.append(jnp.concatenate([g1[:, : 2 * quarter], zeros(2 * quarter)], axis=1))
-        pieces.append(jnp.concatenate([g2, g1[:, 2 * quarter :], zeros(quarter)], axis=1))
-        pieces.append(jnp.concatenate([g3, g0[:, quarter:]], axis=1))
+    for at in (start, start + 3 * quarter):
+        pieces.append(jnp.concatenate([gathered[:middle, at : at + 2 * quarter], zeros], axis=1))
+        ends = gathered[:middle, at + 2 * quarter : at + 3 * quarter]
+        pieces.append(jnp.concatenate([gathered[middle:, at : at + 3 * quarter], ends], axis=1))
     return left_parts(jnp.concatenate(pieces, axis=0).T)
 
 
@@ -182,14 +175,14 @@
         out[at, :] = pivot[at, :] - total[:, p * width : (p + 1) * width]
 
 
-def call(kernel, shapes, specs, flops=0, moved=0, aliases=None, outs=VMEM, scratch=()):
+def call(kernel, shapes, specs, flops=0, moved=0, aliases=None, outs=VMEM, scratch=(), limit=SMALL):
     return pl.pallas_call(
         kernel,
         out_shape=shapes,
         in_specs=specs,
         out_specs=jax.tree.map(lambda _: outs, shapes),
         scratch_shapes=scratch,
-        compiler_params=pltpu.CompilerParams(vmem_limit_bytes=LIMIT),
+        compiler_params=pltpu.CompilerParams(vmem_limit_bytes=limit),
         input_output_aliases=aliases or {},
         cost_estimate=pl.CostEstimate(flops=flops, bytes_accessed=moved, transcendentals=0),
     )
@@ -225,25 +218,26 @@
     own_blocks = own_blocks - chip * range_blocks - core * row_blocks
     own_blocks = jnp.where(own_blocks < row_blocks, own_blocks, -1)
     x_lo = lax.axis_index("x_lo")
-    heights = lax.axis_size("z")
-    group = chip // (heights // 2)
-    place = jnp.stack([col, x_lo, group]).astype(jnp.int32)
+    x_hi = lax.axis_index("x_hi")
+    place = jnp.stack([col, x_lo, x_hi]).astype(jnp.int32)
     swap = [(0, 1), (1, 0)]
     half = unit_rows // 2
-    lanes = 3 * span + 5 * width // 4
+    lanes = 3 * span + 3 * width // 2
 
     stored = call(
         spread_kernel,
         f32(cols, panel.shape[1], panel.shape[0]),
-        [VMEM],
+        [ANY],
         outs=ANY,
-        scratch=[pltpu.SemaphoreType.DMA((cols,))],
+        scratch=[
+            pltpu.VMEM((panel.shape[1], panel.shape[0]), jnp.float32),
+            pltpu.SemaphoreType.DMA((1 + cols,)),
+        ],
+        limit=LARGE,
     )(panel.T)
     stored = lax.all_to_all(stored, COL, 0, 0, tiled=True)
-    unit, slots = lax.optimization_barrier((unit_inverse, slots))
-    across = [(heights + z, z ^ (heights // 2)) for z in range(heights)]
-    far = lax.ppermute(unit, CHIPS, across)
-    before = call(unit_kernel, f32(chips, half, lanes), [SMEM, VMEM, VMEM])(place, unit, far)
+    far = lax.ppermute(unit_inverse, "x_hi", [(1, 0)])
+    before = call(unit_kernel, f32(chips, half, lanes), [SMEM, VMEM, VMEM])(place, unit_inverse, far)
     inverse = call(
         inverse_kernel,
         jax.ShapeDtypeStruct((3 * span, rows_here), jnp.bfloat16),

time: 116 us -> 113 us (0.974)
  blocking collectives: 48.1 us -> 53.9 us
  waiting for transfers between devices: 24.1 us -> 19.1 us
  starting transfers between devices: 30.7 us -> 26.7 us
    ppermute x1, waiting for transfers between devices: 10.2 us -> 2.22 us  [on_device(): far = lax.ppermute(unit_inverse, 'x_hi', [(1, 0)])]
    all_to_all x1, blocking collectives: 29.8 us -> 35.8 us  [on_device(): gathered = lax.all_to_all(payload, CHIPS, 0, 0, tiled=True)]
    all_to_all x1, starting transfers between devices: 7.6 us -> 3.62 us  [on_device(): arrived = lax.all_to_all(partial_tile, COL, 0, 0, tiled=True)]
    all_to_all x1, waiting for transfers between devices: 0.01 us -> 2.43 us  [on_device(): stored = lax.all_to_all(stored, COL, 0, 0, tiled=True)]
  transfers between devices with their start and end apart: 6 -> 6, of which waited for: 5 -> 6; matrix products, arithmetic and copies ran while one was open for 1% -> 1% of each run, Pallas kernels for 3% -> 3%
where the time goes in v7:
time: 113 us; the launch traced here: 112 us
  blocking collectives  53.9 us (48%)
  starting transfers between devices  26.7 us (24%)
  waiting for transfers between devices  19.1 us (17%)
  Pallas kernels  9.55 us (8%)
  local copies, waits for them, and re-layouts  1.3 us (1%)
    all_to_all x1, blocking collectives, on_device(): gathered = lax.all_to_all(payload, CHIPS, 0, 0, tiled=True)  35.8 us
    all_to_all x1, blocking collectives, on_device(): shares = lax.all_to_all(share, ROW, 0, 0, tiled=True)  18.1 us
    all_to_all x1, starting transfers between devices, on_device(): stored = lax.all_to_all(stored, COL, 0, 0, tiled=True)  8.69 us
    ppermute x1, starting transfers between devices, on_device(): col_other = lax.ppermute(col_own, 'core', swap)  6.57 us
    all_to_all x1, waiting for transfers between devices, on_device(): arrived = lax.all_to_all(partial_tile, COL, 0, 0, tiled=True)  5.7 us
    ppermute x1, waiting for transfers between devices, on_device(): half_other = lax.ppermute(half_own, 'x_lo', swap)  4.95 us
    all_to_all x1, starting transfers between devices, on_device(): arrived = lax.all_to_all(partial_tile, COL, 0, 0, tiled=True)  3.62 us
    ppermute x1, starting transfers between devices, on_device(): row_other = lax.ppermute(row_own, 'core', swap)  3.39 us
  transfers between devices with their start and end apart: 6, of which 6 were waited for; matrix products, arithmetic and copies ran while one was open for 1% of the time, Pallas kernels for 3%

profile of v7, /device:TPU:1, one launch (start us, length us, event | category | flops | bytes accessed | tf_op | source)
XLA Modules:
  0.0 112.4 jit_solution(8298409489657229019)
XLA Ops:
  0.6 1.6 %shard_map.68 = f32[16,16,256]{2,1,0:T(8,128)} custom-call(f32[16,256]{1,0:T(8,128)} %bitcast.11), custom_call_target="tpu_custom_call" | custom-call | tf_op jit(solution)/shard_map/pallas_call | solution.py:227
  2.2 8.7 %all-to-all-start = ((f32[16,16,256]{2,1,0:T(8,128)}), f32[16,16,256]{2,1,0:T(8,128)S(1)}, u32[]{:S(2)}, u32[]{:S(2)}) async-start(f32[16,16,256]{2,1,0:T(8,128)} %shard_map.68), calls=%async_computation | async-start | bytes 524288 | tf_op jit(solution)/shard_map/all_to_all | solution.py:238
  10.9 0.0 copy-start.1
  10.9 1.3 %collective-permute-start = (f32[16,512]{1,0:T(8,128)}, f32[16,512]{1,0:T(8,128)S(1)}, u32[]{:S(2)}, u32[]{:S(2)}) collective-permute-start(f32[16,512]{1,0:T(8,128)} %unit.1), channel_id=1, source_target_pairs={{256,0},{257,1},{258,2},{259,3},{260,4},{261,5},{262,6},{263,7},{2... | collective-permute-start | bytes 98312 | tf_op jit(solution)/shard_map/ppermute | solution.py:239
  12.2 0.7 broadcast_add_fusion.2
  12.9 0.2 convert_reduce_fusion
  13.1 0.1 select_reduce_fusion
  13.2 0.1 dynamic-slice_subtract_fusion
  13.3 0.1 pad_add_fusion.place
  13.4 1.3 %copy-done = f32[384,768]{1,0:T(8,128)S(1)} copy-done((f32[384,768]{1,0:T(8,128)S(1)}, f32[384,768]{1,0:T(8,128)}, u32[]{:S(2)}) %copy-start) | copy-done | bytes 1179672
  14.6 0.8 shard_map.69.inverse
  15.4 2.2 %collective-permute-done.far = f32[16,512]{1,0:T(8,128)S(1)} collective-permute-done((f32[16,512]{1,0:T(8,128)}, f32[16,512]{1,0:T(8,128)S(1)}, u32[]{:S(2)}, u32[]{:S(2)}) %collective-permute-start) | collective-permute-done | bytes 32800 | tf_op jit(solution)/shard_map/ppermute | solution.py:239
  17.6 0.6 shard_map.70.before
  18.2 2.4 %all-to-all-done.stored = f32[16,16,256]{2,1,0:T(8,128)S(1)} async-done(((f32[16,16,256]{2,1,0:T(8,128)}), f32[16,16,256]{2,1,0:T(8,128)S(1)}, u32[]{:S(2)}, u32[]{:S(2)}) %all-to-all-start) | async-done | bytes 262176 | tf_op jit(solution)/shard_map/all_to_all | solution.py:238
  20.6 0.8 shard_map.71
  21.4 35.8 %all_to_all.20 = f32[16,8,1920]{2,1,0:T(8,128)S(1)} all-to-all(f32[16,8,1920]{2,1,0:T(8,128)S(1)} %shard_map.71), channel_id=1, replica_groups=mesh['x_hi'=2,'z'=8,'core'=2,'y'=8,'x_lo'=2] {'x_hi','z'}, dimensions={0} | all-to-all | bytes 1966080 | tf_op jit(solution)/shard_map/all_to_all | solution.py:255
  57.2 0.6 shard_map.72.own
  57.8 6.6 %collective-permute-start.1 = (f32[512,384]{1,0:T(8,128)S(1)}, f32[512,384]{1,0:T(8,128)S(1)}, u32[]{:S(2)}, u32[]{:S(2)}) collective-permute-start(f32[512,384]{1,0:T(8,128)S(1)} %shard_map.72.own), channel_id=1, source_target_pairs={{0,16},{16,0},{1,17},{17,1},{2,18},{18,2},{3,19},{19,3},{4,20},{20... | collective-permute-start | bytes 2359304 | tf_op jit(solution)/shard_map/ppermute | solution.py:259
  64.4 1.9 %collective-permute-done.1.other = f32[512,384]{1,0:T(8,128)S(1)} collective-permute-done((f32[512,384]{1,0:T(8,128)S(1)}, f32[512,384]{1,0:T(8,128)S(1)}, u32[]{:S(2)}, u32[]{:S(2)}) %collective-permute-start.1) | collective-permute-done | bytes 786464 | tf_op jit(solution)/shard_map/ppermute | solution.py:259
  66.3 1.6 %shard_map.73 = f32[512,384]{1,0:T(8,128)} custom-call(bf16[1152,384]{1,0:T(8,128)(2,1)S(1)} %shard_map.69.inverse, f32[512,384]{1,0:T(8,128)S(1)} %shard_map.72.own, f32[512,384]{1,0:T(8,128)S(1)} %collective-permute-done.1.other), custom_call_target="tpu_custom_call" | custom-call | flops 452984832 | bytes 3145728 | tf_op jit(solution)/shard_map/pallas_call | solution.py:261
  67.9 3.6 %all-to-all-start.2 = ((f32[16,32,384]{2,1,0:T(8,128)}), f32[16,32,384]{2,1,0:T(8,128)S(1)}, u32[]{:S(2)}, u32[]{:S(2)}) async-start(f32[16,32,384]{2,1,0:T(8,128)} %bitcast.5), calls=%async_computation.2 | async-start | bytes 1572864 | tf_op jit(solution)/shard_map/all_to_all | solution.py:287
  71.5 3.1 %collective-permute-start.2 = (f32[128,384]{1,0:T(8,128)S(1)}, f32[128,384]{1,0:T(8,128)S(1)}, u32[]{:S(2)}, u32[]{:S(2)}) collective-permute-start(f32[128,384]{1,0:T(8,128)S(1)} %slice.4.own), channel_id=1, source_target_pairs={{0,1},{1,0},{2,3},{3,2},{4,5},{5,4},{6,7},{7,6},{8,9},{9,8},{10,11... | collective-permute-start | bytes 589832 | tf_op jit(solution)/shard_map/ppermute | solution.py:275
  74.7 4.9 %collective-permute-done.2.other = f32[128,384]{1,0:T(8,128)S(1)} collective-permute-done((f32[128,384]{1,0:T(8,128)S(1)}, f32[128,384]{1,0:T(8,128)S(1)}, u32[]{:S(2)}, u32[]{:S(2)}) %collective-permute-start.2) | collective-permute-done | bytes 196640 | tf_op jit(solution)/shard_map/ppermute | solution.py:275
  79.6 1.2 %shard_map.74.own = f32[512,384]{1,0:T(8,128)S(1)} custom-call(s32[3]{0:T(128)S(1)} %pad_add_fusion.place, f32[128,1920]{1,0:T(8,128)S(1)} %bitcast.9, f32[128,384]{1,0:T(8,128)S(1)} %slice.4.own, f32[128,384]{1,0:T(8,128)S(1)} %collective-permute-done.2.other), custom_call_target="tpu_custom_call" | custom-call | flops 301989888 | bytes 2097152 | tf_op jit(solution)/shard_map/pallas_call | solution.py:276
  80.8 3.4 %collective-permute-start.3 = (f32[512,384]{1,0:T(8,128)S(1)}, f32[512,384]{1,0:T(8,128)S(1)}, u32[]{:S(2)}, u32[]{:S(2)}) collective-permute-start(f32[512,384]{1,0:T(8,128)S(1)} %shard_map.74.own), channel_id=1, source_target_pairs={{0,16},{16,0},{1,17},{17,1},{2,18},{18,2},{3,19},{19,3},{4,20},{20... | collective-permute-start | bytes 2359304 | tf_op jit(solution)/shard_map/ppermute | solution.py:279
  84.2 1.9 %collective-permute-done.3.other = f32[512,384]{1,0:T(8,128)S(1)} collective-permute-done((f32[512,384]{1,0:T(8,128)S(1)}, f32[512,384]{1,0:T(8,128)S(1)}, u32[]{:S(2)}, u32[]{:S(2)}) %collective-permute-start.3) | collective-permute-done | bytes 786464 | tf_op jit(solution)/shard_map/ppermute | solution.py:279
  86.1 0.5 shard_map.75.normal
  86.6 0.0 copy-start.2
  86.6 5.7 %all-to-all-done.2.arrived = f32[16,32,384]{2,1,0:T(8,128)S(1)} async-done(((f32[16,32,384]{2,1,0:T(8,128)}), f32[16,32,384]{2,1,0:T(8,128)S(1)}, u32[]{:S(2)}, u32[]{:S(2)}) %all-to-all-start.2) | async-done | bytes 786464 | tf_op jit(solution)/shard_map/all_to_all | solution.py:287
  92.3 1.2 %shard_map.76 = (f32[32,384]{1,0:T(8,128)}, f32[128,128]{1,0:T(8,128)S(1)}) custom-call(s32[3]{0:T(128)S(1)} %get-tuple-element.17.blocks, bf16[512,1152]{1,0:T(8,128)(2,1)S(1)} %shard_map.75.normal, f32[16,32,384]{2,1,0:T(8,128)S(1)} %all-to-all-done.2.arrived), custom_call_target="tpu_custom_call" | custom-call | flops 37748736 | bytes 3145728 | tf_op jit(solution)/shard_map/pallas_call | solution.py:289
  93.6 18.1 %all_to_all.21.arrived = f32[32,4,128]{2,1,0:T(4,128)S(1)} all-to-all(f32[32,4,128]{2,1,0:T(4,128)S(1)} %bitcast.10), channel_id=1, replica_groups=mesh['x_hi'=2,'z'=8,'core'=2,'y'=8,'x_lo'=2] {'x_hi','z','core'}, dimensions={0} | all-to-all | bytes 131072 | tf_op jit(solution)/shard_map/all_to_all | solution.py:297
  111.7 0.7 shard_map.77
  (7 shorter events, 0.0 us)
Async XLA Ops:
  2.2 18.4 %all-to-all-start = ((f32[16,16,256]{2,1,0:T(8,128)}), f32[16,16,256]{2,1,0:T(8,128)S(1)}, u32[]{:S(2)}, u32[]{:S(2)}) async-start(f32[16,16,256]{2,1,0:T(8,128)} %shard_map.68), calls=%async_computation | async-start | bytes 524288 | tf_op jit(solution)/shard_map/all_to_all | solution.py:238
  10.9 6.7 %copy-start.1 = (f32[16,512]{1,0:T(8,128)S(1)}, f32[16,512]{1,0:T(8,128)}, u32[]{:S(2)}) copy-start(f32[16,512]{1,0:T(8,128)} %unit.1) | copy-start | bytes 98308
  10.9 6.7 %collective-permute-start = (f32[16,512]{1,0:T(8,128)}, f32[16,512]{1,0:T(8,128)S(1)}, u32[]{:S(2)}, u32[]{:S(2)}) collective-permute-start(f32[16,512]{1,0:T(8,128)} %unit.1), channel_id=1, source_target_pairs={{256,0},{257,1},{258,2},{259,3},{260,4},{261,5},{262,6},{263,7},{2... | collective-permute-start | bytes 98312 | tf_op jit(solution)/shard_map/ppermute | solution.py:239
  13.4 1.3 %copy-start = (f32[384,768]{1,0:T(8,128)S(1)}, f32[384,768]{1,0:T(8,128)}, u32[]{:S(2)}) copy-start(f32[384,768]{1,0:T(8,128)} %inverse.1) | copy-start | bytes 3538948
  57.8 8.5 %collective-permute-start.1 = (f32[512,384]{1,0:T(8,128)S(1)}, f32[512,384]{1,0:T(8,128)S(1)}, u32[]{:S(2)}, u32[]{:S(2)}) collective-permute-start(f32[512,384]{1,0:T(8,128)S(1)} %shard_map.72.own), channel_id=1, source_target_pairs={{0,16},{16,0},{1,17},{17,1},{2,18},{18,2},{3,19},{19,3},{4,20},{20... | collective-permute-start | bytes 2359304 | tf_op jit(solution)/shard_map/ppermute | solution.py:259
  67.9 24.4 %all-to-all-start.2 = ((f32[16,32,384]{2,1,0:T(8,128)}), f32[16,32,384]{2,1,0:T(8,128)S(1)}, u32[]{:S(2)}, u32[]{:S(2)}) async-start(f32[16,32,384]{2,1,0:T(8,128)} %bitcast.5), calls=%async_computation.2 | async-start | bytes 1572864 | tf_op jit(solution)/shard_map/all_to_all | solution.py:287
  71.5 8.1 %collective-permute-start.2 = (f32[128,384]{1,0:T(8,128)S(1)}, f32[128,384]{1,0:T(8,128)S(1)}, u32[]{:S(2)}, u32[]{:S(2)}) collective-permute-start(f32[128,384]{1,0:T(8,128)S(1)} %slice.4.own), channel_id=1, source_target_pairs={{0,1},{1,0},{2,3},{3,2},{4,5},{5,4},{6,7},{7,6},{8,9},{9,8},{10,11... | collective-permute-start | bytes 589832 | tf_op jit(solution)/shard_map/ppermute | solution.py:275
  80.8 5.3 %collective-permute-start.3 = (f32[512,384]{1,0:T(8,128)S(1)}, f32[512,384]{1,0:T(8,128)S(1)}, u32[]{:S(2)}, u32[]{:S(2)}) collective-permute-start(f32[512,384]{1,0:T(8,128)S(1)} %shard_map.74.own), channel_id=1, source_target_pairs={{0,16},{16,0},{1,17},{17,1},{2,18},{18,2},{3,19},{19,3},{4,20},{20... | collective-permute-start | bytes 2359304 | tf_op jit(solution)/shard_map/ppermute | solution.py:279
  86.6 25.1 %copy-start.2 = (f32[16,32]{1,0:T(8,128)S(1)}, f32[16,32]{1,0:T(8,128)}, u32[]{:S(2)}) copy-start(f32[16,32]{1,0:T(8,128)} %pivot.1) | copy-start | bytes 6148

commit v8 on v7

--- a/solution.py
+++ b/solution.py
@@ -137,16 +137,18 @@
     out[...] = left_parts(jnp.concatenate([ordered[s] for s in range(SLOTS)], axis=1))
 
 
-def window_kernel(inverse, own, other, out, made, leave):
-    steps = made.shape[0]
-    rows = made.shape[1]
-    copies = []
+def window_kernel(inverse, own, other, out, held, made, arrive, leave):
+    steps, rows = made.shape[0], made.shape[1]
+    at = [slice(t * rows, (t + 1) * rows) for t in range(steps)]
+    into = [pltpu.make_async_copy(other.at[at[t]], held.at[t], arrive.at[t]) for t in range(steps)]
+    back = [pltpu.make_async_copy(made.at[t], out.at[at[t]], leave.at[t]) for t in range(steps)]
+    for copy in into:
+        copy.start()
     for t in range(steps):
-        at = slice(t * rows, (t + 1) * rows)
-        made[t] = dot(left_parts(own[at] + other[at]), inverse[...])
-        copies.append(pltpu.make_async_copy(made.at[t], out.at[at], leave.at[t]))
-        copies[t].start()
-    for copy in copies:
+        into[t].wait()
+        made[t] = dot(left_parts(own[at[t]] + held[t]), inverse[...])
+        back[t].start()
+    for copy in back:
         copy.wait()
 
 
@@ -244,7 +246,6 @@
         [SMEM, VMEM],
         moved=3 * 1024 * 1024,
     )(col_blocks, ancestor_inverse)
-    stored, inverse = lax.optimization_barrier((stored, inverse))
     payload = call(
         pack_kernel,
         f32(chips, half, lanes),
@@ -261,12 +262,14 @@
     partial_tile = call(
         window_kernel,
         f32(width, rows_here),
-        [VMEM, VMEM, VMEM],
+        [VMEM, VMEM, ANY],
         flops=2 * 3 * width * span * rows_here,
         moved=3 * 1024 * 1024,
         outs=ANY,
         scratch=[
+            pltpu.VMEM((STEPS, width // STEPS, span), jnp.float32),
             pltpu.VMEM(step, jnp.float32),
+            pltpu.SemaphoreType.DMA((STEPS,)),
             pltpu.SemaphoreType.DMA((STEPS,)),
         ],
     )(inverse, col_own, col_other)

time: 113 us -> 115 us (1.018)
  Pallas kernels: 9.55 us -> 11 us
    ppermute x1, waiting for transfers between devices: 2.22 us -> 4.37 us  [on_device(): far = lax.ppermute(unit_inverse, 'x_hi', [(1, 0)])]
    pallas_call x1, Pallas kernels: 1.58 us -> 3.02 us  [on_device(): call(window_kernel, f32(width, rows_here), [VMEM, VMEM, ANY], flops=2 * 3...]
where the time goes in v8:
time: 115 us; the launch traced here: 114 us
  blocking collectives  54.2 us (47%)
  starting transfers between devices  27.1 us (24%)
  waiting for transfers between devices  19.3 us (17%)
  Pallas kernels  11 us (10%)
    all_to_all x1, blocking collectives, on_device(): gathered = lax.all_to_all(payload, CHIPS, 0, 0, tiled=True)  35.8 us
    all_to_all x1, blocking collectives, on_device(): shares = lax.all_to_all(share, ROW, 0, 0, tiled=True)  18.4 us
    all_to_all x1, starting transfers between devices, on_device(): stored = lax.all_to_all(stored, COL, 0, 0, tiled=True)  8.69 us
    ppermute x1, starting transfers between devices, on_device(): col_other = lax.ppermute(col_own, 'core', swap)  6.56 us
    all_to_all x1, waiting for transfers between devices, on_device(): arrived = lax.all_to_all(partial_tile, COL, 0, 0, tiled=True)  5.64 us
    ppermute x1, waiting for transfers between devices, on_device(): half_other = lax.ppermute(half_own, 'x_lo', swap)  4.64 us
    ppermute x1, waiting for transfers between devices, on_device(): far = lax.ppermute(unit_inverse, 'x_hi', [(1, 0)])  4.37 us
    ppermute x1, starting transfers between devices, on_device(): row_other = lax.ppermute(row_own, 'core', swap)  3.66 us
  transfers between devices with their start and end apart: 6, of which 6 were waited for; matrix products, arithmetic and copies ran while one was open for 1% of the time, Pallas kernels for 3%

profile of v8, /device:TPU:1, one launch (start us, length us, event | category | flops | bytes accessed | tf_op | source)
XLA Modules:
  0.0 114.3 jit_solution(9802050599497341062)
XLA Ops:
  0.6 1.6 %shard_map.68 = f32[16,16,256]{2,1,0:T(8,128)} custom-call(f32[16,256]{1,0:T(8,128)} %bitcast.11), custom_call_target="tpu_custom_call" | custom-call | tf_op jit(solution)/shard_map/pallas_call | solution.py:229
  2.2 8.7 %all-to-all-start = ((f32[16,16,256]{2,1,0:T(8,128)}), f32[16,16,256]{2,1,0:T(8,128)S(1)}, u32[]{:S(2)}, u32[]{:S(2)}) async-start(f32[16,16,256]{2,1,0:T(8,128)} %shard_map.68), calls=%async_computation | async-start | bytes 524288 | tf_op jit(solution)/shard_map/all_to_all | solution.py:240
  10.9 1.3 %collective-permute-start = (f32[16,512]{1,0:T(8,128)}, f32[16,512]{1,0:T(8,128)S(1)}, u32[]{:S(2)}, u32[]{:S(2)}) collective-permute-start(f32[16,512]{1,0:T(8,128)} %unit.1), channel_id=1, source_target_pairs={{256,0},{257,1},{258,2},{259,3},{260,4},{261,5},{262,6},{263,7},{2... | collective-permute-start | bytes 98312 | tf_op jit(solution)/shard_map/ppermute | solution.py:241
  12.2 0.7 broadcast_add_fusion.2
  12.9 0.2 convert_reduce_fusion
  13.1 0.1 select_reduce_fusion
  13.2 0.1 pad_add_fusion.place
  13.3 4.4 %collective-permute-done.far = f32[16,512]{1,0:T(8,128)S(1)} collective-permute-done((f32[16,512]{1,0:T(8,128)}, f32[16,512]{1,0:T(8,128)S(1)}, u32[]{:S(2)}, u32[]{:S(2)}) %collective-permute-start) | collective-permute-done | bytes 32800 | tf_op jit(solution)/shard_map/ppermute | solution.py:241
  17.6 0.8 copy-done.1
  18.4 0.6 shard_map.69.before
  19.0 1.7 %all-to-all-done.stored = f32[16,16,256]{2,1,0:T(8,128)S(1)} async-done(((f32[16,16,256]{2,1,0:T(8,128)}), f32[16,16,256]{2,1,0:T(8,128)S(1)}, u32[]{:S(2)}, u32[]{:S(2)}) %all-to-all-start) | async-done | bytes 262176 | tf_op jit(solution)/shard_map/all_to_all | solution.py:240
  20.6 0.8 shard_map.70
  21.4 35.8 %all_to_all.20 = f32[16,8,1920]{2,1,0:T(8,128)S(1)} all-to-all(f32[16,8,1920]{2,1,0:T(8,128)S(1)} %shard_map.70), channel_id=1, replica_groups=mesh['x_hi'=2,'z'=8,'core'=2,'y'=8,'x_lo'=2] {'x_hi','z'}, dimensions={0} | all-to-all | bytes 1966080 | tf_op jit(solution)/shard_map/all_to_all | solution.py:256
  57.2 0.6 shard_map.72.own
  57.8 6.6 %collective-permute-start.1 = (f32[512,384]{1,0:T(8,128)S(1)}, f32[512,384]{1,0:T(8,128)}, u32[]{:S(2)}, u32[]{:S(2)}) collective-permute-start(f32[512,384]{1,0:T(8,128)S(1)} %shard_map.72.own), channel_id=1, source_target_pairs={{0,16},{16,0},{1,17},{17,1},{2,18},{18,2},{3,19},{19,3},{4,20},{20... | collective-permute-start | bytes 2359304 | tf_op jit(solution)/shard_map/ppermute | solution.py:260
  64.4 0.1 dynamic-slice_subtract_fusion
  64.5 0.0 copy-done
  64.5 0.8 shard_map.71.inverse
  65.3 1.1 collective-permute-done.1.other
  66.4 3.0 %shard_map.73 = f32[512,384]{1,0:T(8,128)} custom-call(bf16[1152,384]{1,0:T(8,128)(2,1)S(1)} %shard_map.71.inverse, f32[512,384]{1,0:T(8,128)S(1)} %shard_map.72.own, f32[512,384]{1,0:T(8,128)} %collective-permute-done.1.other), custom_call_target="tpu_custom_call" | custom-call | flops 452984832 | bytes 3145728 | tf_op jit(solution)/shard_map/pallas_call | solution.py:262
  69.5 3.6 %all-to-all-start.2 = ((f32[16,32,384]{2,1,0:T(8,128)}), f32[16,32,384]{2,1,0:T(8,128)S(1)}, u32[]{:S(2)}, u32[]{:S(2)}) async-start(f32[16,32,384]{2,1,0:T(8,128)} %bitcast.5), calls=%async_computation.2 | async-start | bytes 1572864 | tf_op jit(solution)/shard_map/all_to_all | solution.py:290
  73.1 3.2 %collective-permute-start.2 = (f32[128,384]{1,0:T(8,128)S(1)}, f32[128,384]{1,0:T(8,128)S(1)}, u32[]{:S(2)}, u32[]{:S(2)}) collective-permute-start(f32[128,384]{1,0:T(8,128)S(1)} %slice.4.own), channel_id=1, source_target_pairs={{0,1},{1,0},{2,3},{3,2},{4,5},{5,4},{6,7},{7,6},{8,9},{9,8},{10,11... | collective-permute-start | bytes 589832 | tf_op jit(solution)/shard_map/ppermute | solution.py:278
  76.4 4.6 %collective-permute-done.2.other = f32[128,384]{1,0:T(8,128)S(1)} collective-permute-done((f32[128,384]{1,0:T(8,128)S(1)}, f32[128,384]{1,0:T(8,128)S(1)}, u32[]{:S(2)}, u32[]{:S(2)}) %collective-permute-start.2) | collective-permute-done | bytes 196640 | tf_op jit(solution)/shard_map/ppermute | solution.py:278
  81.0 1.2 %shard_map.74.own = f32[512,384]{1,0:T(8,128)S(1)} custom-call(s32[3]{0:T(128)S(1)} %pad_add_fusion.place, f32[128,1920]{1,0:T(8,128)S(1)} %bitcast.9, f32[128,384]{1,0:T(8,128)S(1)} %slice.4.own, f32[128,384]{1,0:T(8,128)S(1)} %collective-permute-done.2.other), custom_call_target="tpu_custom_call" | custom-call | flops 301989888 | bytes 2097152 | tf_op jit(solution)/shard_map/pallas_call | solution.py:279
  82.2 3.7 %collective-permute-start.3 = (f32[512,384]{1,0:T(8,128)S(1)}, f32[512,384]{1,0:T(8,128)S(1)}, u32[]{:S(2)}, u32[]{:S(2)}) collective-permute-start(f32[512,384]{1,0:T(8,128)S(1)} %shard_map.74.own), channel_id=1, source_target_pairs={{0,16},{16,0},{1,17},{17,1},{2,18},{18,2},{3,19},{19,3},{4,20},{20... | collective-permute-start | bytes 2359304 | tf_op jit(solution)/shard_map/ppermute | solution.py:282
  85.8 1.9 %collective-permute-done.3.other = f32[512,384]{1,0:T(8,128)S(1)} collective-permute-done((f32[512,384]{1,0:T(8,128)S(1)}, f32[512,384]{1,0:T(8,128)S(1)}, u32[]{:S(2)}, u32[]{:S(2)}) %collective-permute-start.3) | collective-permute-done | bytes 786464 | tf_op jit(solution)/shard_map/ppermute | solution.py:282
  87.7 0.5 shard_map.75.normal
  88.3 0.0 copy-start.2
  88.3 5.6 %all-to-all-done.2.arrived = f32[16,32,384]{2,1,0:T(8,128)S(1)} async-done(((f32[16,32,384]{2,1,0:T(8,128)}), f32[16,32,384]{2,1,0:T(8,128)S(1)}, u32[]{:S(2)}, u32[]{:S(2)}) %all-to-all-start.2) | async-done | bytes 786464 | tf_op jit(solution)/shard_map/all_to_all | solution.py:290
  93.9 1.2 %shard_map.76 = (f32[32,384]{1,0:T(8,128)}, f32[128,128]{1,0:T(8,128)S(1)}) custom-call(s32[3]{0:T(128)S(1)} %get-tuple-element.13.blocks, bf16[512,1152]{1,0:T(8,128)(2,1)S(1)} %shard_map.75.normal, f32[16,32,384]{2,1,0:T(8,128)S(1)} %all-to-all-done.2.arrived), custom_call_target="tpu_custom_call" | custom-call | flops 37748736 | bytes 3145728 | tf_op jit(solution)/shard_map/pallas_call | solution.py:292
  95.1 18.4 %all_to_all.21.arrived = f32[32,4,128]{2,1,0:T(4,128)S(1)} all-to-all(f32[32,4,128]{2,1,0:T(4,128)S(1)} %bitcast.10), channel_id=1, replica_groups=mesh['x_hi'=2,'z'=8,'core'=2,'y'=8,'x_lo'=2] {'x_hi','z','core'}, dimensions={0} | all-to-all | bytes 131072 | tf_op jit(solution)/shard_map/all_to_all | solution.py:300
  113.6 0.7 shard_map.77
  (7 shorter events, 0.0 us)
Async XLA Ops:
  2.2 18.4 %all-to-all-start = ((f32[16,16,256]{2,1,0:T(8,128)}), f32[16,16,256]{2,1,0:T(8,128)S(1)}, u32[]{:S(2)}, u32[]{:S(2)}) async-start(f32[16,16,256]{2,1,0:T(8,128)} %shard_map.68), calls=%async_computation | async-start | bytes 524288 | tf_op jit(solution)/shard_map/all_to_all | solution.py:240
  10.9 6.7 %collective-permute-start = (f32[16,512]{1,0:T(8,128)}, f32[16,512]{1,0:T(8,128)S(1)}, u32[]{:S(2)}, u32[]{:S(2)}) collective-permute-start(f32[16,512]{1,0:T(8,128)} %unit.1), channel_id=1, source_target_pairs={{256,0},{257,1},{258,2},{259,3},{260,4},{261,5},{262,6},{263,7},{2... | collective-permute-start | bytes 98312 | tf_op jit(solution)/shard_map/ppermute | solution.py:241
  17.6 0.8 copy-start.1
  57.2 7.3 %copy-start = (f32[384,768]{1,0:T(8,128)S(1)}, f32[384,768]{1,0:T(8,128)}, u32[]{:S(2)}) copy-start(f32[384,768]{1,0:T(8,128)} %inverse.1) | copy-start | bytes 3538948
  57.8 8.6 %collective-permute-start.1 = (f32[512,384]{1,0:T(8,128)S(1)}, f32[512,384]{1,0:T(8,128)}, u32[]{:S(2)}, u32[]{:S(2)}) collective-permute-start(f32[512,384]{1,0:T(8,128)S(1)} %shard_map.72.own), channel_id=1, source_target_pairs={{0,16},{16,0},{1,17},{17,1},{2,18},{18,2},{3,19},{19,3},{4,20},{20... | collective-permute-start | bytes 2359304 | tf_op jit(solution)/shard_map/ppermute | solution.py:260
  69.5 24.4 %all-to-all-start.2 = ((f32[16,32,384]{2,1,0:T(8,128)}), f32[16,32,384]{2,1,0:T(8,128)S(1)}, u32[]{:S(2)}, u32[]{:S(2)}) async-start(f32[16,32,384]{2,1,0:T(8,128)} %bitcast.5), calls=%async_computation.2 | async-start | bytes 1572864 | tf_op jit(solution)/shard_map/all_to_all | solution.py:290
  73.1 7.9 %collective-permute-start.2 = (f32[128,384]{1,0:T(8,128)S(1)}, f32[128,384]{1,0:T(8,128)S(1)}, u32[]{:S(2)}, u32[]{:S(2)}) collective-permute-start(f32[128,384]{1,0:T(8,128)S(1)} %slice.4.own), channel_id=1, source_target_pairs={{0,1},{1,0},{2,3},{3,2},{4,5},{5,4},{6,7},{7,6},{8,9},{9,8},{10,11... | collective-permute-start | bytes 589832 | tf_op jit(solution)/shard_map/ppermute | solution.py:278
  82.2 5.6 %collective-permute-start.3 = (f32[512,384]{1,0:T(8,128)S(1)}, f32[512,384]{1,0:T(8,128)S(1)}, u32[]{:S(2)}, u32[]{:S(2)}) collective-permute-start(f32[512,384]{1,0:T(8,128)S(1)} %shard_map.74.own), channel_id=1, source_target_pairs={{0,16},{16,0},{1,17},{17,1},{2,18},{18,2},{3,19},{19,3},{4,20},{20... | collective-permute-start | bytes 2359304 | tf_op jit(solution)/shard_map/ppermute | solution.py:282
  88.3 25.3 %copy-start.2 = (f32[16,32]{1,0:T(8,128)S(1)}, f32[16,32]{1,0:T(8,128)}, u32[]{:S(2)}) copy-start(f32[16,32]{1,0:T(8,128)} %pivot.1) | copy-start | bytes 6148

commit v9 on v7

--- a/solution.py
+++ b/solution.py
@@ -150,19 +150,22 @@
         copy.wait()
 
 
-def diagonal_kernel(blocks, normal, arrived, tile_out, out):
+def diagonal_kernel(blocks, normal, arrived, tile_out, out, held, sem):
     tile = arrived[0]
     for c in range(1, arrived.shape[0]):
         tile = tile + arrived[c]
-    tile_out[...] = -tile
+    held[...] = -tile
+    copy = pltpu.make_async_copy(held, tile_out, sem.at[0])
+    copy.start()
     listed = []
     for s in range(SLOTS):
         place = blocks[s]
         lane = pl.multiple_of(jnp.maximum(place, 0) * BLK, BLK)
-        listed.append(jnp.where(place >= 0, tile_out[:, pl.ds(lane, BLK)], 0.0).T)
+        listed.append(jnp.where(place >= 0, held[:, pl.ds(lane, BLK)], 0.0).T)
     total = dot(normal[...], right_parts(jnp.concatenate(listed, axis=0)))
     rows = out.shape[0]
     out[...] = jnp.concatenate([total[p * rows : (p + 1) * rows] for p in range(SHARE_PARTS)], axis=1)
+    copy.wait()
 
 
 def final_kernel(arrived, pivot, out):
@@ -180,7 +183,7 @@
         kernel,
         out_shape=shapes,
         in_specs=specs,
-        out_specs=jax.tree.map(lambda _: outs, shapes),
+        out_specs=outs if isinstance(outs, tuple) else jax.tree.map(lambda _: outs, shapes),
         scratch_shapes=scratch,
         compiler_params=pltpu.CompilerParams(vmem_limit_bytes=limit),
         input_output_aliases=aliases or {},
@@ -292,6 +295,11 @@
         [SMEM, VMEM, VMEM],
         flops=2 * 3 * width * span * (width // cols),
         moved=3 * 1024 * 1024,
+        outs=(ANY, VMEM),
+        scratch=[
+            pltpu.VMEM((width // cols, rows_here), jnp.float32),
+            pltpu.SemaphoreType.DMA((1,)),
+        ],
     )(own_blocks, row_normal, arrived)
     share = share.reshape(row_count, -1, BLK)
     shares = lax.all_to_all(share, ROW, 0, 0, tiled=True)

time: 113 us -> 113 us (level)
  no operation moved by 1% of the time
where the time goes in v9:
time: 113 us; the launch traced here: 112 us
  blocking collectives  53.9 us (48%)
  starting transfers between devices  26.7 us (24%)
  waiting for transfers between devices  19.1 us (17%)
  Pallas kernels  9.56 us (8%)
  local copies, waits for them, and re-layouts  1.3 us (1%)
    all_to_all x1, blocking collectives, on_device(): gathered = lax.all_to_all(payload, CHIPS, 0, 0, tiled=True)  35.8 us
    all_to_all x1, blocking collectives, on_device(): shares = lax.all_to_all(share, ROW, 0, 0, tiled=True)  18.1 us
    all_to_all x1, starting transfers between devices, on_device(): stored = lax.all_to_all(stored, COL, 0, 0, tiled=True)  8.69 us
    ppermute x1, starting transfers between devices, on_device(): col_other = lax.ppermute(col_own, 'core', swap)  6.57 us
    all_to_all x1, waiting for transfers between devices, on_device(): arrived = lax.all_to_all(partial_tile, COL, 0, 0, tiled=True)  5.7 us
    ppermute x1, waiting for transfers between devices, on_device(): half_other = lax.ppermute(half_own, 'x_lo', swap)  4.95 us
    all_to_all x1, starting transfers between devices, on_device(): arrived = lax.all_to_all(partial_tile, COL, 0, 0, tiled=True)  3.62 us
    ppermute x1, starting transfers between devices, on_device(): row_other = lax.ppermute(row_own, 'core', swap)  3.39 us
  transfers between devices with their start and end apart: 6, of which 6 were waited for; matrix products, arithmetic and copies ran while one was open for 1% of the time, Pallas kernels for 3%

profile of v9, /device:TPU:1, one launch (start us, length us, event | category | flops | bytes accessed | tf_op | source)
XLA Modules:
  0.0 112.4 jit_solution(15799450789709581832)
XLA Ops:
  0.6 1.6 %shard_map.68 = f32[16,16,256]{2,1,0:T(8,128)} custom-call(f32[16,256]{1,0:T(8,128)} %bitcast.11), custom_call_target="tpu_custom_call" | custom-call | tf_op jit(solution)/shard_map/pallas_call | solution.py:230
  2.2 8.7 %all-to-all-start = ((f32[16,16,256]{2,1,0:T(8,128)}), f32[16,16,256]{2,1,0:T(8,128)S(1)}, u32[]{:S(2)}, u32[]{:S(2)}) async-start(f32[16,16,256]{2,1,0:T(8,128)} %shard_map.68), calls=%async_computation | async-start | bytes 524288 | tf_op jit(solution)/shard_map/all_to_all | solution.py:241
  10.9 0.0 copy-start.1
  10.9 1.3 %collective-permute-start = (f32[16,512]{1,0:T(8,128)}, f32[16,512]{1,0:T(8,128)S(1)}, u32[]{:S(2)}, u32[]{:S(2)}) collective-permute-start(f32[16,512]{1,0:T(8,128)} %unit.1), channel_id=1, source_target_pairs={{256,0},{257,1},{258,2},{259,3},{260,4},{261,5},{262,6},{263,7},{2... | collective-permute-start | bytes 98312 | tf_op jit(solution)/shard_map/ppermute | solution.py:242
  12.2 0.7 broadcast_add_fusion.2
  12.9 0.2 convert_reduce_fusion
  13.1 0.1 select_reduce_fusion
  13.2 0.1 dynamic-slice_subtract_fusion
  13.3 0.1 pad_add_fusion.place
  13.4 1.3 %copy-done = f32[384,768]{1,0:T(8,128)S(1)} copy-done((f32[384,768]{1,0:T(8,128)S(1)}, f32[384,768]{1,0:T(8,128)}, u32[]{:S(2)}) %copy-start) | copy-done | bytes 1179672
  14.6 0.8 shard_map.69.inverse
  15.4 2.2 %collective-permute-done.far = f32[16,512]{1,0:T(8,128)S(1)} collective-permute-done((f32[16,512]{1,0:T(8,128)}, f32[16,512]{1,0:T(8,128)S(1)}, u32[]{:S(2)}, u32[]{:S(2)}) %collective-permute-start) | collective-permute-done | bytes 32800 | tf_op jit(solution)/shard_map/ppermute | solution.py:242
  17.6 0.6 shard_map.70.before
  18.2 2.4 %all-to-all-done.stored = f32[16,16,256]{2,1,0:T(8,128)S(1)} async-done(((f32[16,16,256]{2,1,0:T(8,128)}), f32[16,16,256]{2,1,0:T(8,128)S(1)}, u32[]{:S(2)}, u32[]{:S(2)}) %all-to-all-start) | async-done | bytes 262176 | tf_op jit(solution)/shard_map/all_to_all | solution.py:241
  20.6 0.8 shard_map.71
  21.4 35.8 %all_to_all.20 = f32[16,8,1920]{2,1,0:T(8,128)S(1)} all-to-all(f32[16,8,1920]{2,1,0:T(8,128)S(1)} %shard_map.71), channel_id=1, replica_groups=mesh['x_hi'=2,'z'=8,'core'=2,'y'=8,'x_lo'=2] {'x_hi','z'}, dimensions={0} | all-to-all | bytes 1966080 | tf_op jit(solution)/shard_map/all_to_all | solution.py:258
  57.2 0.6 shard_map.72.own
  57.8 6.6 %collective-permute-start.1 = (f32[512,384]{1,0:T(8,128)S(1)}, f32[512,384]{1,0:T(8,128)S(1)}, u32[]{:S(2)}, u32[]{:S(2)}) collective-permute-start(f32[512,384]{1,0:T(8,128)S(1)} %shard_map.72.own), channel_id=1, source_target_pairs={{0,16},{16,0},{1,17},{17,1},{2,18},{18,2},{3,19},{19,3},{4,20},{20... | collective-permute-start | bytes 2359304 | tf_op jit(solution)/shard_map/ppermute | solution.py:262
  64.4 1.9 %collective-permute-done.1.other = f32[512,384]{1,0:T(8,128)S(1)} collective-permute-done((f32[512,384]{1,0:T(8,128)S(1)}, f32[512,384]{1,0:T(8,128)S(1)}, u32[]{:S(2)}, u32[]{:S(2)}) %collective-permute-start.1) | collective-permute-done | bytes 786464 | tf_op jit(solution)/shard_map/ppermute | solution.py:262
  66.3 1.6 %shard_map.73 = f32[512,384]{1,0:T(8,128)} custom-call(bf16[1152,384]{1,0:T(8,128)(2,1)S(1)} %shard_map.69.inverse, f32[512,384]{1,0:T(8,128)S(1)} %shard_map.72.own, f32[512,384]{1,0:T(8,128)S(1)} %collective-permute-done.1.other), custom_call_target="tpu_custom_call" | custom-call | flops 452984832 | bytes 3145728 | tf_op jit(solution)/shard_map/pallas_call | solution.py:264
  67.9 3.6 %all-to-all-start.2 = ((f32[16,32,384]{2,1,0:T(8,128)}), f32[16,32,384]{2,1,0:T(8,128)S(1)}, u32[]{:S(2)}, u32[]{:S(2)}) async-start(f32[16,32,384]{2,1,0:T(8,128)} %bitcast.5), calls=%async_computation.2 | async-start | bytes 1572864 | tf_op jit(solution)/shard_map/all_to_all | solution.py:290
  71.5 3.1 %collective-permute-start.2 = (f32[128,384]{1,0:T(8,128)S(1)}, f32[128,384]{1,0:T(8,128)S(1)}, u32[]{:S(2)}, u32[]{:S(2)}) collective-permute-start(f32[128,384]{1,0:T(8,128)S(1)} %slice.4.own), channel_id=1, source_target_pairs={{0,1},{1,0},{2,3},{3,2},{4,5},{5,4},{6,7},{7,6},{8,9},{9,8},{10,11... | collective-permute-start | bytes 589832 | tf_op jit(solution)/shard_map/ppermute | solution.py:278
  74.7 4.9 %collective-permute-done.2.other = f32[128,384]{1,0:T(8,128)S(1)} collective-permute-done((f32[128,384]{1,0:T(8,128)S(1)}, f32[128,384]{1,0:T(8,128)S(1)}, u32[]{:S(2)}, u32[]{:S(2)}) %collective-permute-start.2) | collective-permute-done | bytes 196640 | tf_op jit(solution)/shard_map/ppermute | solution.py:278
  79.6 1.2 %shard_map.74.own = f32[512,384]{1,0:T(8,128)S(1)} custom-call(s32[3]{0:T(128)S(1)} %pad_add_fusion.place, f32[128,1920]{1,0:T(8,128)S(1)} %bitcast.9, f32[128,384]{1,0:T(8,128)S(1)} %slice.4.own, f32[128,384]{1,0:T(8,128)S(1)} %collective-permute-done.2.other), custom_call_target="tpu_custom_call" | custom-call | flops 301989888 | bytes 2097152 | tf_op jit(solution)/shard_map/pallas_call | solution.py:279
  80.8 3.4 %collective-permute-start.3 = (f32[512,384]{1,0:T(8,128)S(1)}, f32[512,384]{1,0:T(8,128)S(1)}, u32[]{:S(2)}, u32[]{:S(2)}) collective-permute-start(f32[512,384]{1,0:T(8,128)S(1)} %shard_map.74.own), channel_id=1, source_target_pairs={{0,16},{16,0},{1,17},{17,1},{2,18},{18,2},{3,19},{19,3},{4,20},{20... | collective-permute-start | bytes 2359304 | tf_op jit(solution)/shard_map/ppermute | solution.py:282
  84.2 1.9 %collective-permute-done.3.other = f32[512,384]{1,0:T(8,128)S(1)} collective-permute-done((f32[512,384]{1,0:T(8,128)S(1)}, f32[512,384]{1,0:T(8,128)S(1)}, u32[]{:S(2)}, u32[]{:S(2)}) %collective-permute-start.3) | collective-permute-done | bytes 786464 | tf_op jit(solution)/shard_map/ppermute | solution.py:282
  86.1 0.5 shard_map.75.normal
  86.6 0.0 copy-start.2
  86.6 5.7 %all-to-all-done.2.arrived = f32[16,32,384]{2,1,0:T(8,128)S(1)} async-done(((f32[16,32,384]{2,1,0:T(8,128)}), f32[16,32,384]{2,1,0:T(8,128)S(1)}, u32[]{:S(2)}, u32[]{:S(2)}) %all-to-all-start.2) | async-done | bytes 786464 | tf_op jit(solution)/shard_map/all_to_all | solution.py:290
  92.3 1.2 %shard_map.76 = (f32[32,384]{1,0:T(8,128)}, f32[128,128]{1,0:T(8,128)S(1)}) custom-call(s32[3]{0:T(128)S(1)} %get-tuple-element.17.blocks, bf16[512,1152]{1,0:T(8,128)(2,1)S(1)} %shard_map.75.normal, f32[16,32,384]{2,1,0:T(8,128)S(1)} %all-to-all-done.2.arrived), custom_call_target="tpu_custom_call" | custom-call | flops 37748736 | bytes 3145728 | tf_op jit(solution)/shard_map/pallas_call | solution.py:292
  93.6 18.1 %all_to_all.21.arrived = f32[32,4,128]{2,1,0:T(4,128)S(1)} all-to-all(f32[32,4,128]{2,1,0:T(4,128)S(1)} %bitcast.10), channel_id=1, replica_groups=mesh['x_hi'=2,'z'=8,'core'=2,'y'=8,'x_lo'=2] {'x_hi','z','core'}, dimensions={0} | all-to-all | bytes 131072 | tf_op jit(solution)/shard_map/all_to_all | solution.py:305
  111.7 0.7 shard_map.77
  (7 shorter events, 0.0 us)
Async XLA Ops:
  2.2 18.4 %all-to-all-start = ((f32[16,16,256]{2,1,0:T(8,128)}), f32[16,16,256]{2,1,0:T(8,128)S(1)}, u32[]{:S(2)}, u32[]{:S(2)}) async-start(f32[16,16,256]{2,1,0:T(8,128)} %shard_map.68), calls=%async_computation | async-start | bytes 524288 | tf_op jit(solution)/shard_map/all_to_all | solution.py:241
  10.9 6.7 %copy-start.1 = (f32[16,512]{1,0:T(8,128)S(1)}, f32[16,512]{1,0:T(8,128)}, u32[]{:S(2)}) copy-start(f32[16,512]{1,0:T(8,128)} %unit.1) | copy-start | bytes 98308
  10.9 6.7 %collective-permute-start = (f32[16,512]{1,0:T(8,128)}, f32[16,512]{1,0:T(8,128)S(1)}, u32[]{:S(2)}, u32[]{:S(2)}) collective-permute-start(f32[16,512]{1,0:T(8,128)} %unit.1), channel_id=1, source_target_pairs={{256,0},{257,1},{258,2},{259,3},{260,4},{261,5},{262,6},{263,7},{2... | collective-permute-start | bytes 98312 | tf_op jit(solution)/shard_map/ppermute | solution.py:242
  13.4 1.3 %copy-start = (f32[384,768]{1,0:T(8,128)S(1)}, f32[384,768]{1,0:T(8,128)}, u32[]{:S(2)}) copy-start(f32[384,768]{1,0:T(8,128)} %inverse.1) | copy-start | bytes 3538948
  57.8 8.5 %collective-permute-start.1 = (f32[512,384]{1,0:T(8,128)S(1)}, f32[512,384]{1,0:T(8,128)S(1)}, u32[]{:S(2)}, u32[]{:S(2)}) collective-permute-start(f32[512,384]{1,0:T(8,128)S(1)} %shard_map.72.own), channel_id=1, source_target_pairs={{0,16},{16,0},{1,17},{17,1},{2,18},{18,2},{3,19},{19,3},{4,20},{20... | collective-permute-start | bytes 2359304 | tf_op jit(solution)/shard_map/ppermute | solution.py:262
  67.9 24.4 %all-to-all-start.2 = ((f32[16,32,384]{2,1,0:T(8,128)}), f32[16,32,384]{2,1,0:T(8,128)S(1)}, u32[]{:S(2)}, u32[]{:S(2)}) async-start(f32[16,32,384]{2,1,0:T(8,128)} %bitcast.5), calls=%async_computation.2 | async-start | bytes 1572864 | tf_op jit(solution)/shard_map/all_to_all | solution.py:290
  71.5 8.1 %collective-permute-start.2 = (f32[128,384]{1,0:T(8,128)S(1)}, f32[128,384]{1,0:T(8,128)S(1)}, u32[]{:S(2)}, u32[]{:S(2)}) collective-permute-start(f32[128,384]{1,0:T(8,128)S(1)} %slice.4.own), channel_id=1, source_target_pairs={{0,1},{1,0},{2,3},{3,2},{4,5},{5,4},{6,7},{7,6},{8,9},{9,8},{10,11... | collective-permute-start | bytes 589832 | tf_op jit(solution)/shard_map/ppermute | solution.py:278
  80.8 5.3 %collective-permute-start.3 = (f32[512,384]{1,0:T(8,128)S(1)}, f32[512,384]{1,0:T(8,128)S(1)}, u32[]{:S(2)}, u32[]{:S(2)}) collective-permute-start(f32[512,384]{1,0:T(8,128)S(1)} %shard_map.74.own), channel_id=1, source_target_pairs={{0,16},{16,0},{1,17},{17,1},{2,18},{18,2},{3,19},{19,3},{4,20},{20... | collective-permute-start | bytes 2359304 | tf_op jit(solution)/shard_map/ppermute | solution.py:282
  86.6 25.1 %copy-start.2 = (f32[16,32]{1,0:T(8,128)S(1)}, f32[16,32]{1,0:T(8,128)}, u32[]{:S(2)}) copy-start(f32[16,32]{1,0:T(8,128)} %pivot.1) | copy-start | bytes 6148

commit v10 on v9

--- a/solution.py
+++ b/solution.py
@@ -16,7 +16,7 @@
 VMEM = pl.BlockSpec(memory_space=pltpu.VMEM)
 SMEM = pl.BlockSpec(memory_space=pltpu.SMEM)
 ANY = pl.BlockSpec(memory_space=pl.ANY)
-STEPS = 4
+STEPS = 8
 SHARE_ROWS = 16
 SHARE_PARTS = 4
 

time: 113 us -> 113 us (level)
  no operation moved by 1% of the time
where the time goes in v10:
time: 113 us
  blocking collectives  53.9 us (48%)
  starting transfers between devices  26.7 us (24%)
  waiting for transfers between devices  19 us (17%)
  Pallas kernels  9.9 us (9%)
  local copies, waits for them, and re-layouts  1.3 us (1%)
    all_to_all x1, blocking collectives, on_device(): gathered = lax.all_to_all(payload, CHIPS, 0, 0, tiled=True)  35.8 us
    all_to_all x1, blocking collectives, on_device(): shares = lax.all_to_all(share, ROW, 0, 0, tiled=True)  18.1 us
    all_to_all x1, starting transfers between devices, on_device(): stored = lax.all_to_all(stored, COL, 0, 0, tiled=True)  8.69 us
    ppermute x1, starting transfers between devices, on_device(): col_other = lax.ppermute(col_own, 'core', swap)  6.57 us
    all_to_all x1, waiting for transfers between devices, on_device(): arrived = lax.all_to_all(partial_tile, COL, 0, 0, tiled=True)  5.69 us
    ppermute x1, waiting for transfers between devices, on_device(): half_other = lax.ppermute(half_own, 'x_lo', swap)  4.95 us
    all_to_all x1, starting transfers between devices, on_device(): arrived = lax.all_to_all(partial_tile, COL, 0, 0, tiled=True)  3.62 us
    ppermute x1, starting transfers between devices, on_device(): row_other = lax.ppermute(row_own, 'core', swap)  3.39 us
  transfers between devices with their start and end apart: 6, of which 6 were waited for; matrix products, arithmetic and copies ran while one was open for 1% of the time, Pallas kernels for 3%

profile of v10, /device:TPU:1, one launch (start us, length us, event | category | flops | bytes accessed | tf_op | source)
XLA Modules:
  0.0 112.8 jit_solution(11095392482331003232)
XLA Ops:
  0.6 1.6 %shard_map.68 = f32[16,16,256]{2,1,0:T(8,128)} custom-call(f32[16,256]{1,0:T(8,128)} %bitcast.11), custom_call_target="tpu_custom_call" | custom-call | tf_op jit(solution)/shard_map/pallas_call | solution.py:230
  2.2 8.7 %all-to-all-start = ((f32[16,16,256]{2,1,0:T(8,128)}), f32[16,16,256]{2,1,0:T(8,128)S(1)}, u32[]{:S(2)}, u32[]{:S(2)}) async-start(f32[16,16,256]{2,1,0:T(8,128)} %shard_map.68), calls=%async_computation | async-start | bytes 524288 | tf_op jit(solution)/shard_map/all_to_all | solution.py:241
  10.9 0.0 copy-start.1
  10.9 1.3 %collective-permute-start = (f32[16,512]{1,0:T(8,128)}, f32[16,512]{1,0:T(8,128)S(1)}, u32[]{:S(2)}, u32[]{:S(2)}) collective-permute-start(f32[16,512]{1,0:T(8,128)} %unit.1), channel_id=1, source_target_pairs={{256,0},{257,1},{258,2},{259,3},{260,4},{261,5},{262,6},{263,7},{2... | collective-permute-start | bytes 98312 | tf_op jit(solution)/shard_map/ppermute | solution.py:242
  12.2 0.7 broadcast_add_fusion.2
  12.9 0.2 convert_reduce_fusion
  13.1 0.1 select_reduce_fusion
  13.2 0.1 dynamic-slice_subtract_fusion
  13.3 0.1 pad_add_fusion.place
  13.4 1.3 %copy-done = f32[384,768]{1,0:T(8,128)S(1)} copy-done((f32[384,768]{1,0:T(8,128)S(1)}, f32[384,768]{1,0:T(8,128)}, u32[]{:S(2)}) %copy-start) | copy-done | bytes 1179672
  14.6 0.8 shard_map.69.inverse
  15.4 2.2 %collective-permute-done.far = f32[16,512]{1,0:T(8,128)S(1)} collective-permute-done((f32[16,512]{1,0:T(8,128)}, f32[16,512]{1,0:T(8,128)S(1)}, u32[]{:S(2)}, u32[]{:S(2)}) %collective-permute-start) | collective-permute-done | bytes 32800 | tf_op jit(solution)/shard_map/ppermute | solution.py:242
  17.6 0.6 shard_map.70.before
  18.2 2.4 %all-to-all-done.stored = f32[16,16,256]{2,1,0:T(8,128)S(1)} async-done(((f32[16,16,256]{2,1,0:T(8,128)}), f32[16,16,256]{2,1,0:T(8,128)S(1)}, u32[]{:S(2)}, u32[]{:S(2)}) %all-to-all-start) | async-done | bytes 262176 | tf_op jit(solution)/shard_map/all_to_all | solution.py:241
  20.6 0.8 shard_map.71
  21.4 35.8 %all_to_all.20 = f32[16,8,1920]{2,1,0:T(8,128)S(1)} all-to-all(f32[16,8,1920]{2,1,0:T(8,128)S(1)} %shard_map.71), channel_id=1, replica_groups=mesh['x_hi'=2,'z'=8,'core'=2,'y'=8,'x_lo'=2] {'x_hi','z'}, dimensions={0} | all-to-all | bytes 1966080 | tf_op jit(solution)/shard_map/all_to_all | solution.py:258
  57.2 0.6 shard_map.72.own
  57.8 6.6 %collective-permute-start.1 = (f32[512,384]{1,0:T(8,128)S(1)}, f32[512,384]{1,0:T(8,128)S(1)}, u32[]{:S(2)}, u32[]{:S(2)}) collective-permute-start(f32[512,384]{1,0:T(8,128)S(1)} %shard_map.72.own), channel_id=1, source_target_pairs={{0,16},{16,0},{1,17},{17,1},{2,18},{18,2},{3,19},{19,3},{4,20},{20... | collective-permute-start | bytes 2359304 | tf_op jit(solution)/shard_map/ppermute | solution.py:262
  64.4 1.9 %collective-permute-done.1.other = f32[512,384]{1,0:T(8,128)S(1)} collective-permute-done((f32[512,384]{1,0:T(8,128)S(1)}, f32[512,384]{1,0:T(8,128)S(1)}, u32[]{:S(2)}, u32[]{:S(2)}) %collective-permute-start.1) | collective-permute-done | bytes 786464 | tf_op jit(solution)/shard_map/ppermute | solution.py:262
  66.3 1.9 %shard_map.73 = f32[512,384]{1,0:T(8,128)} custom-call(bf16[1152,384]{1,0:T(8,128)(2,1)S(1)} %shard_map.69.inverse, f32[512,384]{1,0:T(8,128)S(1)} %shard_map.72.own, f32[512,384]{1,0:T(8,128)S(1)} %collective-permute-done.1.other), custom_call_target="tpu_custom_call" | custom-call | flops 452984832 | bytes 3145728 | tf_op jit(solution)/shard_map/pallas_call | solution.py:264
  68.2 3.6 %all-to-all-start.2 = ((f32[16,32,384]{2,1,0:T(8,128)}), f32[16,32,384]{2,1,0:T(8,128)S(1)}, u32[]{:S(2)}, u32[]{:S(2)}) async-start(f32[16,32,384]{2,1,0:T(8,128)} %bitcast.5), calls=%async_computation.2 | async-start | bytes 1572864 | tf_op jit(solution)/shard_map/all_to_all | solution.py:290
  71.9 3.1 %collective-permute-start.2 = (f32[128,384]{1,0:T(8,128)S(1)}, f32[128,384]{1,0:T(8,128)S(1)}, u32[]{:S(2)}, u32[]{:S(2)}) collective-permute-start(f32[128,384]{1,0:T(8,128)S(1)} %slice.4.own), channel_id=1, source_target_pairs={{0,1},{1,0},{2,3},{3,2},{4,5},{5,4},{6,7},{7,6},{8,9},{9,8},{10,11... | collective-permute-start | bytes 589832 | tf_op jit(solution)/shard_map/ppermute | solution.py:278
  75.0 4.9 %collective-permute-done.2.other = f32[128,384]{1,0:T(8,128)S(1)} collective-permute-done((f32[128,384]{1,0:T(8,128)S(1)}, f32[128,384]{1,0:T(8,128)S(1)}, u32[]{:S(2)}, u32[]{:S(2)}) %collective-permute-start.2) | collective-permute-done | bytes 196640 | tf_op jit(solution)/shard_map/ppermute | solution.py:278
  80.0 1.2 %shard_map.74.own = f32[512,384]{1,0:T(8,128)S(1)} custom-call(s32[3]{0:T(128)S(1)} %pad_add_fusion.place, f32[128,1920]{1,0:T(8,128)S(1)} %bitcast.9, f32[128,384]{1,0:T(8,128)S(1)} %slice.4.own, f32[128,384]{1,0:T(8,128)S(1)} %collective-permute-done.2.other), custom_call_target="tpu_custom_call" | custom-call | flops 301989888 | bytes 2097152 | tf_op jit(solution)/shard_map/pallas_call | solution.py:279
  81.1 3.4 %collective-permute-start.3 = (f32[512,384]{1,0:T(8,128)S(1)}, f32[512,384]{1,0:T(8,128)S(1)}, u32[]{:S(2)}, u32[]{:S(2)}) collective-permute-start(f32[512,384]{1,0:T(8,128)S(1)} %shard_map.74.own), channel_id=1, source_target_pairs={{0,16},{16,0},{1,17},{17,1},{2,18},{18,2},{3,19},{19,3},{4,20},{20... | collective-permute-start | bytes 2359304 | tf_op jit(solution)/shard_map/ppermute | solution.py:282
  84.5 1.9 %collective-permute-done.3.other = f32[512,384]{1,0:T(8,128)S(1)} collective-permute-done((f32[512,384]{1,0:T(8,128)S(1)}, f32[512,384]{1,0:T(8,128)S(1)}, u32[]{:S(2)}, u32[]{:S(2)}) %collective-permute-start.3) | collective-permute-done | bytes 786464 | tf_op jit(solution)/shard_map/ppermute | solution.py:282
  86.4 0.5 shard_map.75.normal
  87.0 0.0 copy-start.2
  87.0 5.7 %all-to-all-done.2.arrived = f32[16,32,384]{2,1,0:T(8,128)S(1)} async-done(((f32[16,32,384]{2,1,0:T(8,128)}), f32[16,32,384]{2,1,0:T(8,128)S(1)}, u32[]{:S(2)}, u32[]{:S(2)}) %all-to-all-start.2) | async-done | bytes 786464 | tf_op jit(solution)/shard_map/all_to_all | solution.py:290
  92.7 1.2 %shard_map.76 = (f32[32,384]{1,0:T(8,128)}, f32[128,128]{1,0:T(8,128)S(1)}) custom-call(s32[3]{0:T(128)S(1)} %get-tuple-element.17.blocks, bf16[512,1152]{1,0:T(8,128)(2,1)S(1)} %shard_map.75.normal, f32[16,32,384]{2,1,0:T(8,128)S(1)} %all-to-all-done.2.arrived), custom_call_target="tpu_custom_call" | custom-call | flops 37748736 | bytes 3145728 | tf_op jit(solution)/shard_map/pallas_call | solution.py:292
  93.9 18.1 %all_to_all.21.arrived = f32[32,4,128]{2,1,0:T(4,128)S(1)} all-to-all(f32[32,4,128]{2,1,0:T(4,128)S(1)} %bitcast.10), channel_id=1, replica_groups=mesh['x_hi'=2,'z'=8,'core'=2,'y'=8,'x_lo'=2] {'x_hi','z','core'}, dimensions={0} | all-to-all | bytes 131072 | tf_op jit(solution)/shard_map/all_to_all | solution.py:305
  112.1 0.7 shard_map.77
  (7 shorter events, 0.0 us)
Async XLA Ops:
  2.2 18.4 %all-to-all-start = ((f32[16,16,256]{2,1,0:T(8,128)}), f32[16,16,256]{2,1,0:T(8,128)S(1)}, u32[]{:S(2)}, u32[]{:S(2)}) async-start(f32[16,16,256]{2,1,0:T(8,128)} %shard_map.68), calls=%async_computation | async-start | bytes 524288 | tf_op jit(solution)/shard_map/all_to_all | solution.py:241
  10.9 6.7 %copy-start.1 = (f32[16,512]{1,0:T(8,128)S(1)}, f32[16,512]{1,0:T(8,128)}, u32[]{:S(2)}) copy-start(f32[16,512]{1,0:T(8,128)} %unit.1) | copy-start | bytes 98308
  10.9 6.7 %collective-permute-start = (f32[16,512]{1,0:T(8,128)}, f32[16,512]{1,0:T(8,128)S(1)}, u32[]{:S(2)}, u32[]{:S(2)}) collective-permute-start(f32[16,512]{1,0:T(8,128)} %unit.1), channel_id=1, source_target_pairs={{256,0},{257,1},{258,2},{259,3},{260,4},{261,5},{262,6},{263,7},{2... | collective-permute-start | bytes 98312 | tf_op jit(solution)/shard_map/ppermute | solution.py:242
  13.4 1.3 %copy-start = (f32[384,768]{1,0:T(8,128)S(1)}, f32[384,768]{1,0:T(8,128)}, u32[]{:S(2)}) copy-start(f32[384,768]{1,0:T(8,128)} %inverse.1) | copy-start | bytes 3538948
  57.8 8.5 %collective-permute-start.1 = (f32[512,384]{1,0:T(8,128)S(1)}, f32[512,384]{1,0:T(8,128)S(1)}, u32[]{:S(2)}, u32[]{:S(2)}) collective-permute-start(f32[512,384]{1,0:T(8,128)S(1)} %shard_map.72.own), channel_id=1, source_target_pairs={{0,16},{16,0},{1,17},{17,1},{2,18},{18,2},{3,19},{19,3},{4,20},{20... | collective-permute-start | bytes 2359304 | tf_op jit(solution)/shard_map/ppermute | solution.py:262
  68.2 24.4 %all-to-all-start.2 = ((f32[16,32,384]{2,1,0:T(8,128)}), f32[16,32,384]{2,1,0:T(8,128)S(1)}, u32[]{:S(2)}, u32[]{:S(2)}) async-start(f32[16,32,384]{2,1,0:T(8,128)} %bitcast.5), calls=%async_computation.2 | async-start | bytes 1572864 | tf_op jit(solution)/shard_map/all_to_all | solution.py:290
  71.9 8.1 %collective-permute-start.2 = (f32[128,384]{1,0:T(8,128)S(1)}, f32[128,384]{1,0:T(8,128)S(1)}, u32[]{:S(2)}, u32[]{:S(2)}) collective-permute-start(f32[128,384]{1,0:T(8,128)S(1)} %slice.4.own), channel_id=1, source_target_pairs={{0,1},{1,0},{2,3},{3,2},{4,5},{5,4},{6,7},{7,6},{8,9},{9,8},{10,11... | collective-permute-start | bytes 589832 | tf_op jit(solution)/shard_map/ppermute | solution.py:278
  81.1 5.3 %collective-permute-start.3 = (f32[512,384]{1,0:T(8,128)S(1)}, f32[512,384]{1,0:T(8,128)S(1)}, u32[]{:S(2)}, u32[]{:S(2)}) collective-permute-start(f32[512,384]{1,0:T(8,128)S(1)} %shard_map.74.own), channel_id=1, source_target_pairs={{0,16},{16,0},{1,17},{17,1},{2,18},{18,2},{3,19},{19,3},{4,20},{20... | collective-permute-start | bytes 2359304 | tf_op jit(solution)/shard_map/ppermute | solution.py:282
  87.0 25.1 %copy-start.2 = (f32[16,32]{1,0:T(8,128)S(1)}, f32[16,32]{1,0:T(8,128)}, u32[]{:S(2)}) copy-start(f32[16,32]{1,0:T(8,128)} %pivot.1) | copy-start | bytes 6148
